TPU v7x, 512 devices: a whole 4x4x16 slice. The times are simulated.
512 devices in a mesh: leaf: 64 (over z, x), rows: 8 (over y, core).
Axes of the slice: x: 4, y: 4, z: 16, core: 2. Of those that a mesh axis runs over, the one named last changes fastest.
Arguments:
- right_side: bfloat16 [131072, 32], P(('leaf', 'rows')), may hold values from -6 to 6
- point_order: int32 [64, 2048], P('leaf'), may hold values from 0 to 2047, each once within a row
- leaf_inverse: bfloat16 [131072, 2048], P(('leaf', 'rows')), as said below
- bases: bfloat16 [131072, 6, 128], P(('leaf', 'rows'))
Outputs:
- solution: float32 [131072, 32], P(('leaf', 'rows'))
Inputs may be any that keep to these rules, and one draw needn't show every extreme that they name: Each row of point_order names every index 0 .. 2047 once. Each leaf block of leaf_inverse is symmetric.
All inputs are finite; a program needn't handle non-finite values.
Results may differ from a plain program's by a relative error of at most 0.00045.
Values may be sent and summed in bfloat16 or wider, within the bound.
No kernel may reach another device: no remote copies, remote signals or barrier semaphores. Data moves between devices by JAX's collectives and lax.ppermute only.
A program may use at most 64 MiB of HBM per device.

v0:
```python
import jax
import jax.numpy as jnp
from jax import lax
from jax.sharding import PartitionSpec as P

HIGHEST = lax.Precision.HIGHEST


def partner(value, axis, stride):
    mask = 2**stride
    pairs = [(source, source ^ mask) for source in range(lax.axis_size(axis))]
    return lax.ppermute(value, axis, pairs)


def couple(own_a, own_p, far_a, far_p):
    extent = own_a.shape[0]
    system = jnp.eye(extent, dtype=jnp.float32) - jnp.dot(far_a, own_a, precision=HIGHEST)
    target = far_p - jnp.dot(far_a, own_p, precision=HIGHEST)
    gram = jnp.dot(system.T, system, precision=HIGHEST)
    factor = jnp.linalg.cholesky(gram)
    lifted = jnp.dot(system.T, target, precision=HIGHEST)
    middle = lax.linalg.triangular_solve(factor, lifted, left_side=True, lower=True)
    return lax.linalg.triangular_solve(factor, middle, left_side=True, lower=True, transpose_a=True)


def project(basis_rows, values):
    return jnp.einsum("nk,nc->kc", basis_rows, values, precision=HIGHEST)


def local(right_side, point_order, leaf_inverse, bases):
    tiers = bases.shape[1]
    basis_width = bases.shape[2]
    rhs_width = right_side.shape[1]
    tree_order = point_order[0]
    pieces = (
        lax.all_gather(right_side, "rows", axis=0, tiled=True),
        lax.all_gather(bases, "rows", axis=0, tiled=True),
    )
    amount = pieces[0].shape[0]
    inside = (tree_order >= 0) & (tree_order < amount)
    picked = jnp.take(pieces[0], jnp.clip(tree_order, 0, amount - 1), axis=0)
    ordered = jnp.where(inside[:, None], picked.astype(jnp.float32), 0.0)
    flat_piece = pieces[1].reshape(amount, tiers * basis_width)
    ordered, images = (
        ordered,
        jnp.dot(leaf_inverse, flat_piece, preferred_element_type=jnp.float32),
    )
    solved = jnp.dot(leaf_inverse, ordered.astype(jnp.bfloat16), preferred_element_type=jnp.float32)
    basis_f = bases.astype(jnp.float32)
    widths = [images[:, k * basis_width : (k + 1) * basis_width] for k in range(tiers)]
    for height in range(tiers):
        live = jnp.concatenate([solved] + widths[height:], axis=1)
        summed = lax.psum(project(basis_f[:, height, :], live), "rows")
        for bit_pos in range(height):
            summed = summed + partner(summed, "leaf", bit_pos)
        other = partner(summed, "leaf", height)
        own_a = summed[:, rhs_width : rhs_width + basis_width]
        own_p = jnp.concatenate(
            [summed[:, :rhs_width], summed[:, rhs_width + basis_width :]], axis=1
        )
        far_a = other[:, rhs_width : rhs_width + basis_width]
        far_p = jnp.concatenate([other[:, :rhs_width], other[:, rhs_width + basis_width :]], axis=1)
        coeffs = couple(own_a, own_p, far_a, far_p)
        remain = jnp.concatenate([solved] + widths[height + 1 :], axis=1)
        remain = remain - jnp.dot(widths[height], coeffs, precision=HIGHEST)
        solved = remain[:, :rhs_width]
        later = [
            remain[:, rhs_width + k * basis_width : rhs_width + (k + 1) * basis_width]
            for k in range(tiers - height - 1)
        ]
        widths = widths[: height + 1] + later
    return solved


def solution(mesh):
    in_specs = (
        P(("leaf", "rows"), None),
        P("leaf", None),
        P(("leaf", "rows"), None),
        P(("leaf", "rows"), None, None),
    )
    out_specs = P(("leaf", "rows"), None)
    return jax.shard_map(local, mesh=mesh, in_specs=in_specs, out_specs=out_specs, check_vma=False)
```

profile of v0, /device:TPU:24, one launch (start us, length us, event | category | flops | bytes accessed | tf_op | source)
XLA Modules:
  0.0 894.2 jit_solution(2689182222563878276)
XLA Ops:
  9.5 15.6 %all_gather.6 = bf16[2048,32]{1,0:T(8,128)(2,1)S(1)} all-gather(bf16[256,32]{1,0:T(8,128)(2,1)S(1)} %copy.38), channel_id=1, replica_groups=mesh['leaf'=64,'rows'=8] {'rows'}, dimensions={0}, use_global_device_ids=true | all-gather | bytes 147456 | tf_op jit(solution)/shard_map/all_gather | solution.py:36
  33.3 19.0 %all-gather.2.cloned.1.call-done = bf16[2048,6,128]{0,2,1:T(8,128)(2,1)} async-done(((bf16[256,6,128]{0,2,1:T(8,128)(2,1)}), bf16[2048,6,128]{0,2,1:T(8,128)(2,1)}) %all-gather.2.cloned.1.call-update) | async-done | bytes 3145744 | tf_op jit(solution)/shard_map/all_gather | solution.py:37
  58.1 74.8 %all-reduce.7.cloned.1.call-done = f32[128,800]{0,1:T(8,128)} async-done(((f32[128,800]{0,1:T(8,128)}), f32[128,800]{0,1:T(8,128)}) %all-reduce.7.cloned.1.call-update) | async-done | bytes 409616 | tf_op jit(solution)/shard_map/psum | solution.py:53
  138.5 7.9 collective-permute-done
  147.9 11.7 %cholesky.104 = f32[128,128]{1,0:T(8,128)S(1)} custom-call(f32[128,128]{1,0:T(8,128)S(1)} %fusion.95), custom_call_target="Cholesky" | custom-call | tf_op jit(solution)/shard_map/jit(cholesky)/cholesky | solution.py:20
  161.0 9.8 %custom-call.32 = f32[1,128,128]{1,2,0:T(8,128)S(1)} custom-call(f32[1,128,128]{2,1,0:T(8,128)S(1)} %fusion.49), custom_call_target="InvertDiagBlocksLowerTriangular" | custom-call | tf_op jit(solution)/shard_map/triangular_solve | solution.py:23
  177.9 74.3 %all-reduce.9.cloned.1.call-done = f32[128,672]{0,1:T(8,128)} async-done(((f32[128,672]{0,1:T(8,128)}), f32[128,672]{0,1:T(8,128)}) %all-reduce.9.cloned.1.call-update) | async-done | bytes 344080 | tf_op jit(solution)/shard_map/psum | solution.py:53
  255.0 8.4 collective-permute-done.1
  270.2 8.1 collective-permute-done.2
  279.8 11.7 %cholesky.115 = f32[128,128]{1,0:T(8,128)S(1)} custom-call(f32[128,128]{1,0:T(8,128)S(1)} %fusion.89), custom_call_target="Cholesky" | custom-call | tf_op jit(solution)/shard_map/jit(cholesky)/cholesky | solution.py:20
  292.9 9.8 %custom-call.33 = f32[1,128,128]{1,2,0:T(8,128)S(1)} custom-call(f32[1,128,128]{2,1,0:T(8,128)S(1)} %fusion.50), custom_call_target="InvertDiagBlocksLowerTriangular" | custom-call | tf_op jit(solution)/shard_map/triangular_solve | solution.py:23
  308.7 73.4 %all-reduce.11.cloned.1.call-done = f32[128,544]{0,1:T(8,128)} async-done(((f32[128,544]{0,1:T(8,128)}), f32[128,544]{0,1:T(8,128)}) %all-reduce.11.cloned.1.call-update) | async-done | bytes 278544 | tf_op jit(solution)/shard_map/psum | solution.py:53
  384.9 7.1 collective-permute-done.3
  397.8 7.6 collective-permute-done.4
  409.8 6.5 collective-permute-done.5
  416.9 11.7 %cholesky.126 = f32[128,128]{1,0:T(8,128)S(1)} custom-call(f32[128,128]{1,0:T(8,128)S(1)} %fusion.83), custom_call_target="Cholesky" | custom-call | tf_op jit(solution)/shard_map/jit(cholesky)/cholesky | solution.py:20
  430.0 9.8 %custom-call.34 = f32[1,128,128]{1,2,0:T(8,128)S(1)} custom-call(f32[1,128,128]{2,1,0:T(8,128)S(1)} %fusion.51), custom_call_target="InvertDiagBlocksLowerTriangular" | custom-call | tf_op jit(solution)/shard_map/triangular_solve | solution.py:23
  442.8 73.0 %all-reduce.13.cloned.1.call-done = f32[128,416]{0,1:T(8,128)} async-done(((f32[128,416]{0,1:T(8,128)}), f32[128,416]{0,1:T(8,128)}) %all-reduce.13.cloned.1.call-update) | async-done | bytes 213008 | tf_op jit(solution)/shard_map/psum | solution.py:53
  518.6 7.1 collective-permute-done.6
  549.5 8.9 collective-permute-done.9
  559.1 11.7 %cholesky.137 = f32[128,128]{1,0:T(8,128)S(1)} custom-call(f32[128,128]{1,0:T(8,128)S(1)} %fusion.77), custom_call_target="Cholesky" | custom-call | tf_op jit(solution)/shard_map/jit(cholesky)/cholesky | solution.py:20
  572.1 9.8 %custom-call.35 = f32[1,128,128]{1,2,0:T(8,128)S(1)} custom-call(f32[1,128,128]{2,1,0:T(8,128)S(1)} %fusion.52), custom_call_target="InvertDiagBlocksLowerTriangular" | custom-call | tf_op jit(solution)/shard_map/triangular_solve | solution.py:23
  584.5 71.6 %all-reduce.15.cloned.1.call-done = f32[128,288]{0,1:T(8,128)} async-done(((f32[128,288]{0,1:T(8,128)}), f32[128,288]{0,1:T(8,128)}) %all-reduce.15.cloned.1.call-update) | async-done | bytes 147472 | tf_op jit(solution)/shard_map/psum | solution.py:53
  690.1 7.9 collective-permute-start.14
  698.0 8.8 collective-permute-done.14
  707.5 11.7 %cholesky.148 = f32[128,128]{1,0:T(8,128)S(1)} custom-call(f32[128,128]{1,0:T(8,128)S(1)} %fusion.71), custom_call_target="Cholesky" | custom-call | tf_op jit(solution)/shard_map/jit(cholesky)/cholesky | solution.py:20
  720.5 9.8 %custom-call.36 = f32[1,128,128]{1,2,0:T(8,128)S(1)} custom-call(f32[1,128,128]{2,1,0:T(8,128)S(1)} %fusion.53), custom_call_target="InvertDiagBlocksLowerTriangular" | custom-call | tf_op jit(solution)/shard_map/triangular_solve | solution.py:23
  732.5 70.3 %all-reduce.17.cloned.1.call-done = f32[128,160]{0,1:T(8,128)} async-done(((f32[128,160]{0,1:T(8,128)}), f32[128,160]{0,1:T(8,128)}) %all-reduce.17.cloned.1.call-update) | async-done | bytes 81936 | tf_op jit(solution)/shard_map/psum | solution.py:53
  839.2 6.5 collective-permute-done.19
  845.8 12.1 %collective-permute-start.20 = (f32[128,160]{0,1:T(8,128)S(1)}, f32[128,160]{0,1:T(8,128)S(1)}, u32[]{:S(2)}, u32[]{:S(2)}) collective-permute-start(f32[128,160]{0,1:T(8,128)S(1)} %add.121), channel_id=1, source_target_pairs={{0,256},{8,264},{16,272},{24,280},{32,288},{40,296},{48,304},{56,3... | collective-permute-start | bytes 245768 | tf_op jit(solution)/shard_map/ppermute | solution.py:12
  862.7 11.7 %cholesky.159 = f32[128,128]{1,0:T(8,128)S(1)} custom-call(f32[128,128]{1,0:T(8,128)S(1)} %fusion.65), custom_call_target="Cholesky" | custom-call | tf_op jit(solution)/shard_map/jit(cholesky)/cholesky | solution.py:20
  875.8 9.8 %custom-call.37 = f32[1,128,128]{1,2,0:T(8,128)S(1)} custom-call(f32[1,128,128]{2,1,0:T(8,128)S(1)} %fusion.54), custom_call_target="InvertDiagBlocksLowerTriangular" | custom-call | tf_op jit(solution)/shard_map/triangular_solve | solution.py:23
  (184 shorter events, 181.7 us)
Async XLA Ops:
  6.5 25.6 %copy-start = (bf16[256,2048]{1,0:T(8,128)(2,1)S(1)}, bf16[256,2048]{1,0:T(8,128)(2,1)}, u32[]{:S(2)}) copy-start(bf16[256,2048]{1,0:T(8,128)(2,1)} %param.7) | copy-start | bytes 3145732
  6.5 25.5 %copy-start.2 = (s32[1,2048]{1,0:T(1,128)S(1)}, s32[1,2048]{1,0:T(1,128)}, u32[]{:S(2)}) copy-start(s32[1,2048]{1,0:T(1,128)} %param.6) | copy-start | bytes 24580
  6.5 45.8 %all-gather.2.cloned.1.call-start = ((), (), s32[]{:S(2)}) async-start(), calls=%async_computation | async-start | bytes 3538944 | tf_op jit(solution)/shard_map/all_gather | solution.py:37
  8.6 124.4 %all-reduce.7.cloned.1.call-start = ((), (), s32[]{:S(2)}) async-start(), calls=%async_computation.1 | async-start | bytes 819200 | tf_op jit(solution)/shard_map/psum | solution.py:53
  58.0 194.1 %all-reduce.9.cloned.1.call-start = ((), (), s32[]{:S(2)}) async-start(), calls=%async_computation.2 | async-start | bytes 688128 | tf_op jit(solution)/shard_map/psum | solution.py:53
  132.9 13.4 %collective-permute-start = (f32[128,800]{0,1:T(8,128)}, f32[128,800]{0,1:T(8,128)}, u32[]{:S(2)}, u32[]{:S(2)}) collective-permute-start(f32[128,800]{0,1:T(8,128)} %all-reduce.7.cloned.1.call-done), channel_id=1, source_target_pairs={{0,8},{8,0},{16,24},{24,16},{32,40},{40,32},{48,56},{56,48},{64,72... | collective-permute-start | bytes 1228808 | tf_op jit(solution)/shard_map/ppermute | solution.py:12
  177.9 204.2 %all-reduce.11.cloned.1.call-start = ((), (), s32[]{:S(2)}) async-start(), calls=%async_computation.3 | async-start | bytes 557056 | tf_op jit(solution)/shard_map/psum | solution.py:53
  252.2 11.2 %collective-permute-start.1 = (f32[128,672]{0,1:T(8,128)}, f32[128,672]{0,1:T(8,128)S(1)}, u32[]{:S(2)}, u32[]{:S(2)}) collective-permute-start(f32[128,672]{0,1:T(8,128)} %all-reduce.9.cloned.1.call-done), channel_id=1, source_target_pairs={{0,8},{8,0},{16,24},{24,16},{32,40},{40,32},{48,56},{56,48},{64,72... | collective-permute-start | bytes 1032200 | tf_op jit(solution)/shard_map/ppermute | solution.py:12
  264.4 13.8 %collective-permute-start.2 = (f32[128,672]{0,1:T(8,128)S(1)}, f32[128,672]{0,1:T(8,128)}, u32[]{:S(2)}, u32[]{:S(2)}) collective-permute-start(f32[128,672]{0,1:T(8,128)S(1)} %add.107), channel_id=1, source_target_pairs={{0,16},{8,24},{16,0},{24,8},{32,48},{40,56},{48,32},{56,40},{64,80... | collective-permute-start | bytes 1032200 | tf_op jit(solution)/shard_map/ppermute | solution.py:12
  269.5 38.0 %copy-start.1 = (bf16[256,6,128]{2,0,1:T(8,128)(2,1)S(1)}, bf16[256,6,128]{2,0,1:T(8,128)(2,1)}, u32[]{:S(2)}) copy-start(bf16[256,6,128]{2,0,1:T(8,128)(2,1)} %param.8) | copy-start | bytes 1179652
  308.6 207.1 %all-reduce.13.cloned.1.call-start = ((), (), s32[]{:S(2)}) async-start(), calls=%async_computation.4 | async-start | bytes 425984 | tf_op jit(solution)/shard_map/psum | solution.py:53
  382.0 9.9 %collective-permute-start.3 = (f32[128,544]{0,1:T(8,128)}, f32[128,544]{0,1:T(8,128)S(1)}, u32[]{:S(2)}, u32[]{:S(2)}) collective-permute-start(f32[128,544]{0,1:T(8,128)} %all-reduce.11.cloned.1.call-done), channel_id=1, source_target_pairs={{0,8},{8,0},{16,24},{24,16},{32,40},{40,32},{48,56},{56,48},{64,72... | collective-permute-start | bytes 835592 | tf_op jit(solution)/shard_map/ppermute | solution.py:12
  393.0 12.4 %collective-permute-start.4 = (f32[128,544]{0,1:T(8,128)S(1)}, f32[128,544]{0,1:T(8,128)S(1)}, u32[]{:S(2)}, u32[]{:S(2)}) collective-permute-start(f32[128,544]{0,1:T(8,128)S(1)} %add.108), channel_id=1, source_target_pairs={{0,16},{8,24},{16,0},{24,8},{32,48},{40,56},{48,32},{56,40},{64,80... | collective-permute-start | bytes 835592 | tf_op jit(solution)/shard_map/ppermute | solution.py:12
  405.5 10.8 %collective-permute-start.5 = (f32[128,544]{0,1:T(8,128)S(1)}, f32[128,544]{0,1:T(8,128)S(1)}, u32[]{:S(2)}, u32[]{:S(2)}) collective-permute-start(f32[128,544]{0,1:T(8,128)S(1)} %add.109), channel_id=1, source_target_pairs={{0,32},{8,40},{16,48},{24,56},{32,0},{40,8},{48,16},{56,24},{64,96... | collective-permute-start | bytes 835592 | tf_op jit(solution)/shard_map/ppermute | solution.py:12
  442.7 213.4 %all-reduce.15.cloned.1.call-start = ((), (), s32[]{:S(2)}) async-start(), calls=%async_computation.5 | async-start | bytes 294912 | tf_op jit(solution)/shard_map/psum | solution.py:53
  515.8 10.0 %collective-permute-start.6 = (f32[128,416]{0,1:T(8,128)}, f32[128,416]{0,1:T(8,128)S(1)}, u32[]{:S(2)}, u32[]{:S(2)}) collective-permute-start(f32[128,416]{0,1:T(8,128)} %all-reduce.13.cloned.1.call-done), channel_id=1, source_target_pairs={{0,8},{8,0},{16,24},{24,16},{32,40},{40,32},{48,56},{56,48},{64,72... | collective-permute-start | bytes 638984 | tf_op jit(solution)/shard_map/ppermute | solution.py:12
  526.7 10.7 %collective-permute-start.7 = (f32[128,416]{0,1:T(8,128)S(1)}, f32[128,416]{0,1:T(8,128)S(1)}, u32[]{:S(2)}, u32[]{:S(2)}) collective-permute-start(f32[128,416]{0,1:T(8,128)S(1)} %add.110), channel_id=1, source_target_pairs={{0,16},{8,24},{16,0},{24,8},{32,48},{40,56},{48,32},{56,40},{64,80... | collective-permute-start | bytes 638984 | tf_op jit(solution)/shard_map/ppermute | solution.py:12
  537.4 8.3 collective-permute-start.8
  545.8 12.6 %collective-permute-start.9 = (f32[128,416]{0,1:T(8,128)S(1)}, f32[128,416]{0,1:T(8,128)S(1)}, u32[]{:S(2)}, u32[]{:S(2)}) collective-permute-start(f32[128,416]{0,1:T(8,128)S(1)} %add.112), channel_id=1, source_target_pairs={{0,64},{8,72},{16,80},{24,88},{32,96},{40,104},{48,112},{56,120},{... | collective-permute-start | bytes 638984 | tf_op jit(solution)/shard_map/ppermute | solution.py:12
  584.5 218.3 %all-reduce.17.cloned.1.call-start = ((), (), s32[]{:S(2)}) async-start(), calls=%async_computation.6 | async-start | bytes 163840 | tf_op jit(solution)/shard_map/psum | solution.py:53
  656.1 7.8 collective-permute-start.10
  664.9 8.5 collective-permute-start.11
  673.5 7.0 collective-permute-start.12
  680.5 9.5 %collective-permute-start.13 = (f32[128,288]{0,1:T(8,128)S(1)}, f32[128,288]{0,1:T(8,128)S(1)}, u32[]{:S(2)}, u32[]{:S(2)}) collective-permute-start(f32[128,288]{0,1:T(8,128)S(1)} %add.115), channel_id=1, source_target_pairs={{0,64},{8,72},{16,80},{24,88},{32,96},{40,104},{48,112},{56,120},{... | collective-permute-start | bytes 442376 | tf_op jit(solution)/shard_map/ppermute | solution.py:12
  690.1 16.7 %collective-permute-start.14 = (f32[128,288]{0,1:T(8,128)S(1)}, f32[128,288]{0,1:T(8,128)S(1)}, u32[]{:S(2)}, u32[]{:S(2)}) collective-permute-start(f32[128,288]{0,1:T(8,128)S(1)} %add.116), channel_id=1, source_target_pairs={{0,128},{8,136},{16,144},{24,152},{32,160},{40,168},{48,176},{56,1... | collective-permute-start | bytes 442376 | tf_op jit(solution)/shard_map/ppermute | solution.py:12
  802.8 6.7 collective-permute-start.15
  810.4 8.3 collective-permute-start.16
  818.7 6.3 collective-permute-start.17
  825.1 8.1 collective-permute-start.18
  833.2 12.6 %collective-permute-start.19 = (f32[128,160]{0,1:T(8,128)S(1)}, f32[128,160]{0,1:T(8,128)S(1)}, u32[]{:S(2)}, u32[]{:S(2)}) collective-permute-start(f32[128,160]{0,1:T(8,128)S(1)} %add.120), channel_id=1, source_target_pairs={{0,128},{8,136},{16,144},{24,152},{32,160},{40,168},{48,176},{56,1... | collective-permute-start | bytes 245768 | tf_op jit(solution)/shard_map/ppermute | solution.py:12
  845.8 16.2 %collective-permute-start.20 = (f32[128,160]{0,1:T(8,128)S(1)}, f32[128,160]{0,1:T(8,128)S(1)}, u32[]{:S(2)}, u32[]{:S(2)}) collective-permute-start(f32[128,160]{0,1:T(8,128)S(1)} %add.121), channel_id=1, source_target_pairs={{0,256},{8,264},{16,272},{24,280},{32,288},{40,296},{48,304},{56,3... | collective-permute-start | bytes 245768 | tf_op jit(solution)/shard_map/ppermute | solution.py:12
Sparse Core Ops, SparseCore 0:
  9.5 42.8 all-gather.1
  58.2 74.7 all-reduce.6
  178.0 74.1 all-reduce.8
  308.8 73.2 all-reduce.10
  442.8 72.8 all-reduce.12
  584.6 71.5 all-reduce.14
  732.6 70.1 all-reduce.16
where the time goes:
time: 899 us; the launch traced here: 894 us
  waiting for transfers between devices  584 us (65%)
  other arithmetic  143 us (16%)
  starting transfers between devices  90.6 us (10%)
  matrix products  30.2 us (3%)
  local copies, waits for them, and re-layouts  16 us (2%)
  blocking collectives  15.6 us (2%)
  between operations  14.7 us (2%)
    psum x6, waiting for transfers between devices, local(): summed = lax.psum(project(basis_f[:, height, :], live), 'rows')  437 us
    ppermute x21, waiting for transfers between devices, partner(): return lax.ppermute(value, axis, pairs)  128 us
    ppermute x21, starting transfers between devices, partner(): return lax.ppermute(value, axis, pairs)  90.4 us
    another operation x18, other arithmetic, couple(): factor = jnp.linalg.cholesky(gram)  74.3 us
    another operation x12, other arithmetic, couple(): lax.linalg.triangular_solve(factor, middle, left_side=True, lower=True, t...  62.8 us
    all_gather x1, waiting for transfers between devices, local(): lax.all_gather(bases, 'rows', axis=0, tiled=True)  19 us
  transfers between devices with their start and end apart: 28, of which 28 were waited for; matrix products, arithmetic and copies ran while one was open for 1% of the time, Pallas kernels for 0%

commit v1 on v0

v1 whole, which is shorter than its diff:
```python
import functools

import jax
import jax.numpy as jnp
from jax import lax
from jax.experimental import pallas as pl
from jax.experimental.pallas import tpu as pltpu
from jax.sharding import PartitionSpec as P

F32 = jnp.float32
BF16 = jnp.bfloat16
FULL = lax.Precision.HIGHEST
CORES = 2
VMEM_BYTES = 40 * 1024 * 1024


def mm(a, b, precision=FULL):
    return lax.dot_general(a, b, (((1,), (0,)), ((), ())), precision=precision, preferred_element_type=F32)


def mm_nt(a, b, precision=FULL):
    return lax.dot_general(a, b, (((1,), (1,)), ((), ())), precision=precision, preferred_element_type=F32)


def section_rows(height, tiers, rank, width):
    return width + rank * (tiers - height)


def section_offset(height, tiers, rank, width):
    return sum(section_rows(h, tiers, rank, width) for h in range(height))


def inverse_one_minus(left, right):
    rank = left.shape[0]
    eye = (
        lax.broadcasted_iota(jnp.int32, (rank, rank), 0) == lax.broadcasted_iota(jnp.int32, (rank, rank), 1)
    ).astype(F32)
    power = mm(left, right)
    system = eye - power
    guess = eye + power
    for _ in range(5):
        power = mm(power, power)
        guess = guess + mm(guess, power)

    def residual(x):
        gap = eye - mm(system, x)
        return gap, jnp.sum(gap * gap)

    gap, size = residual(guess)

    def restart():
        size_a = jnp.abs(system)
        bound = jnp.max(jnp.sum(size_a, axis=0)) * jnp.max(jnp.sum(size_a, axis=1))
        start = system.T / bound
        return (start,) + residual(start)

    def keep():
        return guess, gap, size

    def step(carry):
        count, x, gap, _ = carry
        x = x + mm(x, gap)
        return (count + 1, x) + residual(x)

    def more(carry):
        count, _, _, size = carry
        return jnp.logical_and(count < 80, jnp.logical_not(size < 1e-9))

    x, gap, size = lax.cond(size < 0.25, keep, restart)
    return lax.while_loop(more, step, (0, x, gap, size))[1]


def level_kernel(height, tiers, rank, width, own_ref, far_ref, *out_refs):
    rest = tiers - height - 1
    own = own_ref[0 : width + rank * (rest + 1), :]
    far = far_ref[0 : width + rank * (rest + 1), :]
    own_a, far_a = own[width : width + rank], far[width : width + rank]
    own_r, far_r = own[:width], far[:width]
    if rest > 0:
        own_r = jnp.concatenate([own_r, own[width + rank :]], axis=0)
        far_r = jnp.concatenate([far_r, far[width + rank :]], axis=0)
    target = far_r - mm(own_r, far_a)
    coeff = mm(target, inverse_one_minus(own_a, far_a))
    out_refs[0][...] = coeff
    if rest == 0:
        return
    other = own_r - mm(coeff, own_a)
    both = jnp.concatenate([coeff, other], axis=1)
    images = jnp.concatenate([own_r[width:], far_r[width:]], axis=1)
    base = width + rank * (rest + 1)
    top = mm_nt(both[:width], images)
    place = 0
    for g in range(rest):
        rows = width + rank * (rest - g)
        low = mm_nt(both[width + rank * g :], images[rank * g : rank * (g + 1)])
        part = jnp.concatenate([top[:, rank * g : rank * (g + 1)], low], axis=0)
        span = slice(base + place, base + place + rows)
        out_refs[1][place : place + rows, :] = own_ref[span, :] + far_ref[span, :] - part
        place += rows


def run_level(height, tiers, rank, width, own, far):
    rest = tiers - height - 1
    shapes = [jax.ShapeDtypeStruct((width + rank * rest, rank), F32)]
    left = own.shape[0] - section_rows(height, tiers, rank, width)
    if rest > 0:
        shapes.append(jax.ShapeDtypeStruct((left, rank), F32))
    return pl.pallas_call(
        functools.partial(level_kernel, height, tiers, rank, width),
        out_shape=shapes,
        in_specs=[pl.BlockSpec(memory_space=pltpu.VMEM)] * 2,
        out_specs=[pl.BlockSpec(memory_space=pltpu.VMEM)] * len(shapes),
        compiler_params=pltpu.CompilerParams(vmem_limit_bytes=VMEM_BYTES),
        name=f"level{height}",
    )(own, far)


def finish_kernel(tiers, rank, width, solved_ref, images_ref, *refs):
    coeff_refs, out_ref = refs[:tiers], refs[tiers]
    found = [None] * tiers
    for h in reversed(range(tiers)):
        value = coeff_refs[h][0:width, :]
        if h + 1 < tiers:
            above = jnp.concatenate(found[h + 1 :], axis=1)
            value = value - mm(above, coeff_refs[h][width:, :])
        found[h] = value
    out_ref[...] = solved_ref[...] - mm_nt(images_ref[...], jnp.concatenate(found, axis=1))


def finish(tiers, rank, width, solved, images, coeffs):
    return pl.pallas_call(
        functools.partial(finish_kernel, tiers, rank, width),
        out_shape=jax.ShapeDtypeStruct(solved.shape, F32),
        in_specs=[pl.BlockSpec(memory_space=pltpu.VMEM)] * (2 + tiers),
        out_specs=pl.BlockSpec(memory_space=pltpu.VMEM),
        compiler_params=pltpu.CompilerParams(vmem_limit_bytes=VMEM_BYTES),
        name="finish",
    )(solved, images, *coeffs)


def leaf_kernel(tiers, rank, width, inverse_ref, bases_ref, ordered_ref, own_ref, solved_ref, images_ref, gram_ref):
    inverse = inverse_ref[...]
    solved = mm(inverse, ordered_ref[...], None)
    images = mm(inverse, bases_ref[...], None)
    solved_ref[...] = solved
    images_ref[...] = images
    live = jnp.concatenate([images, solved], axis=1)
    high = live.astype(BF16)
    left = live - high.astype(F32)
    middle = left.astype(BF16)
    low = (left - middle.astype(F32)).astype(BF16)
    own = own_ref[...]

    def project(first, last, basis):
        total = None
        for piece in (high, middle, low):
            term = lax.dot_general(
                piece[:, first:last], basis, (((0,), (0,)), ((), ())), preferred_element_type=F32
            )
            total = term if total is None else total + term
        return total

    place = 0
    for h in range(tiers):
        basis = own[:, rank * h : rank * (h + 1)]
        gram_ref[place : place + width, :] = project(rank * tiers, rank * tiers + width, basis)
        rows = rank * (tiers - h)
        gram_ref[place + width : place + width + rows, :] = project(rank * h, rank * tiers, basis)
        place += width + rows


def leaf_step(tiers, rank, width, inverse, bases, ordered, own):
    rows = inverse.shape[0]
    total = section_offset(tiers, tiers, rank, width)
    return pl.pallas_call(
        functools.partial(leaf_kernel, tiers, rank, width),
        out_shape=[
            jax.ShapeDtypeStruct((rows, width), F32),
            jax.ShapeDtypeStruct((rows, tiers * rank), F32),
            jax.ShapeDtypeStruct((total, rank), F32),
        ],
        in_specs=[pl.BlockSpec(memory_space=pltpu.VMEM)] * 4,
        out_specs=[pl.BlockSpec(memory_space=pltpu.VMEM)] * 3,
        compiler_params=pltpu.CompilerParams(vmem_limit_bytes=VMEM_BYTES),
        name="leaf",
    )(inverse, bases, ordered, own)


def partner(value, axis, mask):
    return lax.ppermute(value, axis, [(i, i ^ mask) for i in range(lax.axis_size(axis))])


def local(right_side, point_order, leaf_inverse, bases):
    tiers, rank, width = bases.shape[1], bases.shape[2], right_side.shape[1]
    rows = bases.shape[0]
    flat = bases.reshape(rows, tiers * rank)
    given = lax.all_gather(right_side, "rows", axis=0, tiled=True)
    whole = lax.all_gather(flat, "rows", axis=0, tiled=True)
    ordered = jnp.take(given, point_order[0], axis=0, mode="clip")
    solved, images, gram = leaf_step(tiers, rank, width, leaf_inverse, whole, ordered, flat)

    members = lax.axis_size("rows")
    chips = members // CORES
    core = lax.axis_index("rows") % CORES
    groups = [[chip * CORES + c for chip in range(chips)] for c in range(CORES)]
    total = gram.shape[0]
    half = total // CORES
    keep = lax.dynamic_slice_in_dim(gram, core * half, half)
    give = lax.dynamic_slice_in_dim(gram, (1 - core) * half, half)
    keep = keep + partner(give, "rows", 1)
    parts = lax.all_to_all(keep.reshape(chips, half // chips, rank), "rows", 0, 0, axis_index_groups=groups)
    share = parts.sum(axis=0)
    spread = lax.all_to_all(
        jnp.broadcast_to(share[None], (chips, half // chips, rank)), "rows", 0, 0, axis_index_groups=groups
    )
    mine = spread.reshape(half, rank)

    def join(mine, theirs):
        first = jnp.where(core == 0, mine, theirs)
        second = jnp.where(core == 0, theirs, mine)
        return jnp.concatenate([first, second], axis=0)

    own = join(mine, partner(mine, "rows", 1))
    coeffs = []
    for height in range(tiers):
        if height < 2:
            half = own.shape[0] // CORES
            mine = lax.dynamic_slice_in_dim(own, core * half, half)
            got = partner(mine, "leaf", 2**height)
            far = join(got, partner(got, "rows", 1))
        else:
            far = partner(own, "leaf", 2**height)
        result = run_level(height, tiers, rank, width, own, far)
        coeffs.append(result[0])
        if height + 1 < tiers:
            own = result[1]
    return finish(tiers, rank, width, solved, images, coeffs)


def solution(mesh):
    in_specs = (
        P(("leaf", "rows"), None),
        P("leaf", None),
        P(("leaf", "rows"), None),
        P(("leaf", "rows"), None, None),
    )
    out_specs = P(("leaf", "rows"), None)
    return jax.shard_map(local, mesh=mesh, in_specs=in_specs, out_specs=out_specs, check_vma=False)
```

time: 899 us -> 263 us (0.29)
  waiting for transfers between devices: 584 us -> 116 us
  other arithmetic: 143 us -> 1.09 us
  starting transfers between devices: 90.6 us -> 43.6 us
  matrix products: 30.2 us -> 0 us
  blocking collectives: 15.6 us -> 43.7 us
  Pallas kernels: 0 us -> 28 us
    psum x6 -> x0, waiting for transfers between devices: 437 us -> none  [local(): summed = lax.psum(project(basis_f[:, height, :], live), 'rows')]
    another operation x30 -> x0, other arithmetic: 137 us -> none  [the longest x18 74.3 us: couple(): factor = jnp.linalg.cholesky(gram)]
    ppermute x21 -> x10, starting transfers between devices: 90.4 us -> 43.6 us  [partner(): lax.ppermute(value, axis, [(i, i ^ mask) for i in range(lax.axis_size(axi...]
    ppermute x21 -> x10, waiting for transfers between devices: 128 us -> 99.1 us  [partner(): lax.ppermute(value, axis, [(i, i ^ mask) for i in range(lax.axis_size(axi...]
    all_to_all x0 -> x2, blocking collectives: none -> 28 us  [the longest x1 14.6 us: local(): lax.all_to_all(keep.reshape(chips, half // chips, rank), 'rows', 0, 0, ax...]
    pallas_call x0 -> x8, Pallas kernels: none -> 28 us  [the longest x6 23.1 us: run_level(): pl.pallas_call(functools.partial(level_kernel, height, tiers, rank, width...]
    dot_general x38 -> x0, matrix products: 26.5 us -> none  [the longest x6 8.67 us: project(): return jnp.einsum('nk,nc->kc', basis_rows, values, precision=HIGHEST)]
  transfers between devices with their start and end apart: 28 -> 11, of which waited for: 28 -> 11; matrix products, arithmetic and copies ran while one was open for 1% -> 2% of each run, Pallas kernels for 0% -> 0%
where the time goes in v1:
time: 263 us; the launch traced here: 259 us
  waiting for transfers between devices  116 us (44%)
  blocking collectives  43.7 us (17%)
  starting transfers between devices  43.6 us (17%)
  Pallas kernels  28 us (11%)
  between operations  13.7 us (5%)
  local copies, waits for them, and re-layouts  12.7 us (5%)
    ppermute x10, waiting for transfers between devices, partner(): lax.ppermute(value, axis, [(i, i ^ mask) for i in range(lax.axis_size(axi...  99.1 us
    ppermute x10, starting transfers between devices, partner(): lax.ppermute(value, axis, [(i, i ^ mask) for i in range(lax.axis_size(axi...  43.6 us
    pallas_call x6, Pallas kernels, run_level(): pl.pallas_call(functools.partial(level_kernel, height, tiers, rank, width...  23.1 us
    all_gather x1, waiting for transfers between devices, local(): whole = lax.all_gather(flat, 'rows', axis=0, tiled=True)  17.3 us
    all_gather x1, blocking collectives, local(): given = lax.all_gather(right_side, 'rows', axis=0, tiled=True)  15.6 us
    all_to_all x1, blocking collectives, local(): lax.all_to_all(keep.reshape(chips, half // chips, rank), 'rows', 0, 0, ax...  14.6 us
    all_to_all x1, blocking collectives, local(): lax.all_to_all(jnp.broadcast_to(share[None], (chips, half // chips, rank)...  13.4 us
    gather x1, local copies, waits for them, and re-layouts, local(): ordered = jnp.take(given, point_order[0], axis=0, mode='clip')  6.18 us
  transfers between devices with their start and end apart: 11, of which 11 were waited for; matrix products, arithmetic and copies ran while one was open for 2% of the time, Pallas kernels for 0%

profile of v1, /device:TPU:24, one launch (start us, length us, event | category | flops | bytes accessed | tf_op | source)
XLA Modules:
  0.0 259.2 jit_solution(12648145642223672071)
XLA Ops:
  8.8 15.6 %all_gather.7 = bf16[2048,32]{1,0:T(8,128)(2,1)S(1)} all-gather(bf16[256,32]{1,0:T(8,128)(2,1)S(1)} %copy.10), channel_id=1, replica_groups=mesh['leaf'=64,'rows'=8] {'rows'}, dimensions={0}, use_global_device_ids=true | all-gather | bytes 147456 | tf_op jit(solution)/shard_map/all_gather | solution.py:197
  24.5 6.2 %gather_fusion = bf16[2048,32]{1,0:T(8,128)(2,1)S(1)} fusion(bf16[2048,32]{1,0:T(8,128)(2,1)S(1)} %all_gather.7, s32[2048]{0:T(1024)S(1)} %broadcast_clamp_fusion), kind=kCustom, calls=%fused_computation | custom fusion | bytes 270336 | tf_op jit(solution)/shard_map/jit(_take)/gather | solution.py:199
  30.7 17.3 %all-gather.2.cloned.1.call-done.bases_ref = bf16[2048,768]{1,0:T(8,128)(2,1)} async-done(((bf16[256,768]{1,0:T(8,128)(2,1)}), bf16[2048,768]{1,0:T(8,128)(2,1)}) %all-gather.2.cloned.1.call-update) | async-done | bytes 3145744 | tf_op jit(solution)/shard_map/all_gather | solution.py:198
  49.9 3.0 %leaf.1 = (f32[256,32]{1,0:T(8,128)S(1)}, f32[256,768]{1,0:T(8,128)S(1)}, f32[2880,128]{1,0:T(8,128)S(1)}) custom-call(bf16[256,2048]{1,0:T(8,128)(2,1)S(1)} %copy-done.2, bf16[2048,768]{1,0:T(8,128)(2,1)S(1)} %copy-done.1, bf16[2048,32]{1,0:T(8,128)(2,1)S(1)} %gather_fusion, bf16[256,768]{1,0:T(8,128)(2,1)S(1)} %copy-done), custom_call_target="tpu_custom_call" | custom-call | tf_op jit(solution)/shard_map/leaf/pallas_call | solution.py:175
  54.5 2.1 collective-permute-start
  56.7 1.9 collective-permute-done
  58.7 14.6 %all_to_all.10 = f32[4,360,128]{2,1,0:T(8,128)S(1)} all-to-all(f32[4,360,128]{2,1,0:T(8,128)S(1)} %bitcast.6), channel_id=1, replica_groups={{0,2,4,6},{1,3,5,7},{8,10,12,14},{9,11,13,15},{16,18,20,22},{17,19,21,2..., dimensions={0} | all-to-all | bytes 1474560 | tf_op jit(solution)/shard_map/all_to_all | solution.py:211
  73.4 13.4 %all_to_all.11 = f32[4,360,128]{2,1,0:T(8,128)S(1)} all-to-all(f32[4,360,128]{2,1,0:T(8,128)S(1)} %broadcast_in_dim.11), channel_id=1, replica_groups={{0,2,4,6},{1,3,5,7},{8,10,12,14},{9,11,13,15},{16,18,20,22},{17,19,21,2..., dimensions={0} | all-to-all | bytes 1474560 | tf_op jit(solution)/shard_map/all_to_all | solution.py:213
  86.8 1.9 collective-permute-start.1
  88.7 2.2 collective-permute-done.1
  91.5 3.4 %collective-permute-start.2 = (f32[1440,128]{1,0:T(8,128)S(1)}, f32[1440,128]{1,0:T(8,128)S(1)}, u32[]{:S(2)}, u32[]{:S(2)}) collective-permute-start(f32[1440,128]{1,0:T(8,128)S(1)} %fusion), channel_id=1, source_target_pairs={{0,8},{8,0},{16,24},{24,16},{32,40},{40,32},{48,56},{56,48},{64,72... | collective-permute-start | bytes 2211848 | tf_op jit(solution)/shard_map/ppermute | solution.py:190
  94.8 17.0 %collective-permute-done.2 = f32[1440,128]{1,0:T(8,128)S(1)} collective-permute-done((f32[1440,128]{1,0:T(8,128)S(1)}, f32[1440,128]{1,0:T(8,128)S(1)}, u32[]{:S(2)}, u32[]{:S(2)}) %collective-permute-start.2) | collective-permute-done | bytes 737312 | tf_op jit(solution)/shard_map/ppermute | solution.py:190
  111.9 1.9 collective-permute-start.3
  113.9 2.1 collective-permute-done.3
  116.2 6.0 %level0.1 = (f32[672,128]{1,0:T(8,128)S(1)}, f32[2080,128]{1,0:T(8,128)S(1)}) custom-call(f32[2880,128]{1,0:T(8,128)S(1)} %pad_maximum_fusion.own_ref, f32[2880,128]{1,0:T(8,128)S(1)} %pad_maximum_fusion.1.far_ref), custom_call_target="tpu_custom_call" | custom-call | tf_op jit(solution)/shard_map/level0/pallas_call | solution.py:108
  122.2 4.9 %collective-permute-start.4 = (f32[1040,128]{1,0:T(8,128)S(1)}, f32[1040,128]{1,0:T(8,128)S(1)}, u32[]{:S(2)}, u32[]{:S(2)}) collective-permute-start(f32[1040,128]{1,0:T(8,128)S(1)} %constant_dynamic-slice_fusion), channel_id=1, source_target_pairs={{0,16},{8,24},{16,0},{24,8},{32,48},{40,56},{48,32},{56,40},{64,80... | collective-permute-start | bytes 1597448 | tf_op jit(solution)/shard_map/ppermute | solution.py:190
  127.1 12.6 %collective-permute-done.4 = f32[1040,128]{1,0:T(8,128)S(1)} collective-permute-done((f32[1040,128]{1,0:T(8,128)S(1)}, f32[1040,128]{1,0:T(8,128)S(1)}, u32[]{:S(2)}, u32[]{:S(2)}) %collective-permute-start.4) | collective-permute-done | bytes 532512 | tf_op jit(solution)/shard_map/ppermute | solution.py:190
  139.7 2.1 collective-permute-start.5
  143.7 4.7 %level1.1 = (f32[544,128]{1,0:T(8,128)S(1)}, f32[1408,128]{1,0:T(8,128)S(1)}) custom-call(f32[2080,128]{1,0:T(8,128)S(1)} %get-tuple-element.22.own_ref, f32[2080,128]{1,0:T(8,128)S(1)} %pad_maximum_fusion.2.far_ref), custom_call_target="tpu_custom_call" | custom-call | tf_op jit(solution)/shard_map/level1/pallas_call | solution.py:108
  148.4 3.6 %collective-permute-start.6 = (f32[1408,128]{1,0:T(8,128)S(1)}, f32[1408,128]{1,0:T(8,128)S(1)}, u32[]{:S(2)}, u32[]{:S(2)}) collective-permute-start(f32[1408,128]{1,0:T(8,128)S(1)} %get-tuple-element.24.own_ref), channel_id=1, source_target_pairs={{0,32},{8,40},{16,48},{24,56},{32,0},{40,8},{48,16},{56,24},{64,96... | collective-permute-start | bytes 2162696 | tf_op jit(solution)/shard_map/ppermute | solution.py:190
  152.0 16.6 %collective-permute-done.6.far_ref = f32[1408,128]{1,0:T(8,128)S(1)} collective-permute-done((f32[1408,128]{1,0:T(8,128)S(1)}, f32[1408,128]{1,0:T(8,128)S(1)}, u32[]{:S(2)}, u32[]{:S(2)}) %collective-permute-start.6) | collective-permute-done | bytes 720928 | tf_op jit(solution)/shard_map/ppermute | solution.py:190
  168.6 4.2 %level2.1 = (f32[416,128]{1,0:T(8,128)S(1)}, f32[864,128]{1,0:T(8,128)S(1)}) custom-call(f32[1408,128]{1,0:T(8,128)S(1)} %get-tuple-element.24.own_ref, f32[1408,128]{1,0:T(8,128)S(1)} %collective-permute-done.6.far_ref), custom_call_target="tpu_custom_call" | custom-call | tf_op jit(solution)/shard_map/level2/pallas_call | solution.py:108
  172.8 4.5 %collective-permute-start.7 = (f32[864,128]{1,0:T(8,128)S(1)}, f32[864,128]{1,0:T(8,128)S(1)}, u32[]{:S(2)}, u32[]{:S(2)}) collective-permute-start(f32[864,128]{1,0:T(8,128)S(1)} %get-tuple-element.26.own_ref), channel_id=1, source_target_pairs={{0,64},{8,72},{16,80},{24,88},{32,96},{40,104},{48,112},{56,120},{... | collective-permute-start | bytes 1327112 | tf_op jit(solution)/shard_map/ppermute | solution.py:190
  177.2 19.2 %collective-permute-done.7.far_ref = f32[864,128]{1,0:T(8,128)S(1)} collective-permute-done((f32[864,128]{1,0:T(8,128)S(1)}, f32[864,128]{1,0:T(8,128)S(1)}, u32[]{:S(2)}, u32[]{:S(2)}) %collective-permute-start.7) | collective-permute-done | bytes 442400 | tf_op jit(solution)/shard_map/ppermute | solution.py:190
  196.4 3.2 %level3.1 = (f32[288,128]{1,0:T(8,128)S(1)}, f32[448,128]{1,0:T(8,128)S(1)}) custom-call(f32[864,128]{1,0:T(8,128)S(1)} %get-tuple-element.26.own_ref, f32[864,128]{1,0:T(8,128)S(1)} %collective-permute-done.7.far_ref), custom_call_target="tpu_custom_call" | custom-call | tf_op jit(solution)/shard_map/level3/pallas_call | solution.py:108
  199.7 7.6 %collective-permute-start.8 = (f32[448,128]{1,0:T(8,128)S(1)}, f32[448,128]{1,0:T(8,128)S(1)}, u32[]{:S(2)}, u32[]{:S(2)}) collective-permute-start(f32[448,128]{1,0:T(8,128)S(1)} %get-tuple-element.28.own_ref), channel_id=1, source_target_pairs={{0,128},{8,136},{16,144},{24,152},{32,160},{40,168},{48,176},{56,1... | collective-permute-start | bytes 688136 | tf_op jit(solution)/shard_map/ppermute | solution.py:190
  207.3 18.4 %collective-permute-done.8.far_ref = f32[448,128]{1,0:T(8,128)S(1)} collective-permute-done((f32[448,128]{1,0:T(8,128)S(1)}, f32[448,128]{1,0:T(8,128)S(1)}, u32[]{:S(2)}, u32[]{:S(2)}) %collective-permute-start.8) | collective-permute-done | bytes 229408 | tf_op jit(solution)/shard_map/ppermute | solution.py:190
  225.7 2.8 %level4.1 = (f32[160,128]{1,0:T(8,128)S(1)}, f32[160,128]{1,0:T(8,128)S(1)}) custom-call(f32[448,128]{1,0:T(8,128)S(1)} %get-tuple-element.28.own_ref, f32[448,128]{1,0:T(8,128)S(1)} %collective-permute-done.8.far_ref), custom_call_target="tpu_custom_call" | custom-call | tf_op jit(solution)/shard_map/level4/pallas_call | solution.py:108
  228.6 11.6 %collective-permute-start.9 = (f32[160,128]{1,0:T(8,128)S(1)}, f32[160,128]{1,0:T(8,128)S(1)}, u32[]{:S(2)}, u32[]{:S(2)}) collective-permute-start(f32[160,128]{1,0:T(8,128)S(1)} %get-tuple-element.30.own_ref), channel_id=1, source_target_pairs={{0,256},{8,264},{16,272},{24,280},{32,288},{40,296},{48,304},{56,3... | collective-permute-start | bytes 245768 | tf_op jit(solution)/shard_map/ppermute | solution.py:190
  240.2 7.3 %collective-permute-done.9.far_ref = f32[160,128]{1,0:T(8,128)S(1)} collective-permute-done((f32[160,128]{1,0:T(8,128)S(1)}, f32[160,128]{1,0:T(8,128)S(1)}, u32[]{:S(2)}, u32[]{:S(2)}) %collective-permute-start.9) | collective-permute-done | bytes 81952 | tf_op jit(solution)/shard_map/ppermute | solution.py:190
  247.5 2.2 level5.1.refs_5_
  249.8 1.9 finish.1
  (38 shorter events, 9.3 us)
Async XLA Ops:
  6.5 2.1 copy-start.7
  6.5 17.9 %copy-start.8 = (s32[1,2048]{1,0:T(1,128)S(1)}, s32[1,2048]{1,0:T(1,128)}, u32[]{:S(2)}) copy-start(s32[1,2048]{1,0:T(1,128)} %param.5) | copy-start | bytes 24580
  6.5 41.5 %all-gather.2.cloned.1.call-start = ((), (), s32[]{:S(2)}) async-start(), calls=%async_computation.2 | async-start | bytes 3538944 | tf_op jit(solution)/shard_map/all_gather | solution.py:198
  24.5 23.6 %copy-start = (bf16[256,768]{1,0:T(8,128)(2,1)S(1)}, bf16[256,768]{1,0:T(8,128)(2,1)}, u32[]{:S(2)}) copy-start(bf16[256,768]{1,0:T(8,128)(2,1)} %copy.9.own_ref) | copy-start | bytes 1179652
  24.5 23.6 %copy-start.2 = (bf16[256,2048]{1,0:T(8,128)(2,1)S(1)}, bf16[256,2048]{1,0:T(8,128)(2,1)}, u32[]{:S(2)}) copy-start(bf16[256,2048]{1,0:T(8,128)(2,1)} %inverse_ref.1) | copy-start | bytes 3145732
  48.0 1.9 copy-start.1
  52.9 0.9 copy-start.3
  53.8 0.6 copy-start.5
  54.5 4.1 %collective-permute-start = (f32[1440,128]{1,0:T(8,128)S(1)}, f32[1440,128]{1,0:T(8,128)S(1)}, u32[]{:S(2)}, u32[]{:S(2)}) collective-permute-start(f32[1440,128]{1,0:T(8,128)S(1)} %constant_dynamic-slice_fusion.1), channel_id=1, source_target_pairs={{0,1},{1,0},{2,3},{3,2},{4,5},{5,4},{6,7},{7,6},{8,9},{9,8},{10,11... | collective-permute-start | bytes 2211848 | tf_op jit(solution)/shard_map/ppermute | solution.py:190
  86.8 4.1 %collective-permute-start.1 = (f32[1440,128]{1,0:T(8,128)S(1)}, f32[1440,128]{1,0:T(8,128)S(1)}, u32[]{:S(2)}, u32[]{:S(2)}) collective-permute-start(f32[1440,128]{1,0:T(8,128)S(1)} %bitcast.7), channel_id=1, source_target_pairs={{0,1},{1,0},{2,3},{3,2},{4,5},{5,4},{6,7},{7,6},{8,9},{9,8},{10,11... | collective-permute-start | bytes 2211848 | tf_op jit(solution)/shard_map/ppermute | solution.py:190
  91.5 20.4 %collective-permute-start.2 = (f32[1440,128]{1,0:T(8,128)S(1)}, f32[1440,128]{1,0:T(8,128)S(1)}, u32[]{:S(2)}, u32[]{:S(2)}) collective-permute-start(f32[1440,128]{1,0:T(8,128)S(1)} %fusion), channel_id=1, source_target_pairs={{0,8},{8,0},{16,24},{24,16},{32,40},{40,32},{48,56},{56,48},{64,72... | collective-permute-start | bytes 2211848 | tf_op jit(solution)/shard_map/ppermute | solution.py:190
  111.9 4.1 %collective-permute-start.3 = (f32[1440,128]{1,0:T(8,128)S(1)}, f32[1440,128]{1,0:T(8,128)S(1)}, u32[]{:S(2)}, u32[]{:S(2)}) collective-permute-start(f32[1440,128]{1,0:T(8,128)S(1)} %collective-permute-done.2), channel_id=1, source_target_pairs={{0,1},{1,0},{2,3},{3,2},{4,5},{5,4},{6,7},{7,6},{8,9},{9,8},{10,11... | collective-permute-start | bytes 2211848 | tf_op jit(solution)/shard_map/ppermute | solution.py:190
  122.2 17.5 %collective-permute-start.4 = (f32[1040,128]{1,0:T(8,128)S(1)}, f32[1040,128]{1,0:T(8,128)S(1)}, u32[]{:S(2)}, u32[]{:S(2)}) collective-permute-start(f32[1040,128]{1,0:T(8,128)S(1)} %constant_dynamic-slice_fusion), channel_id=1, source_target_pairs={{0,16},{8,24},{16,0},{24,8},{32,48},{40,56},{48,32},{56,40},{64,80... | collective-permute-start | bytes 1597448 | tf_op jit(solution)/shard_map/ppermute | solution.py:190
  139.7 3.8 %collective-permute-start.5 = (f32[1040,128]{1,0:T(8,128)S(1)}, f32[1040,128]{1,0:T(8,128)S(1)}, u32[]{:S(2)}, u32[]{:S(2)}) collective-permute-start(f32[1040,128]{1,0:T(8,128)S(1)} %collective-permute-done.4), channel_id=1, source_target_pairs={{0,1},{1,0},{2,3},{3,2},{4,5},{5,4},{6,7},{7,6},{8,9},{9,8},{10,11... | collective-permute-start | bytes 1597448 | tf_op jit(solution)/shard_map/ppermute | solution.py:190
  148.4 101.4 %copy-start.4 = (f32[256,768]{1,0:T(8,128)S(1)}, f32[256,768]{1,0:T(8,128)}, u32[]{:S(2)}) copy-start(f32[256,768]{1,0:T(8,128)} %copy-done.3) | copy-start | bytes 2359300
  148.4 101.4 %copy-start.6 = (f32[256,32]{1,0:T(8,128)S(1)}, f32[256,32]{1,0:T(8,128)}, u32[]{:S(2)}) copy-start(f32[256,32]{1,0:T(8,128)} %copy-done.5) | copy-start | bytes 98308
  148.4 20.2 %collective-permute-start.6 = (f32[1408,128]{1,0:T(8,128)S(1)}, f32[1408,128]{1,0:T(8,128)S(1)}, u32[]{:S(2)}, u32[]{:S(2)}) collective-permute-start(f32[1408,128]{1,0:T(8,128)S(1)} %get-tuple-element.24.own_ref), channel_id=1, source_target_pairs={{0,32},{8,40},{16,48},{24,56},{32,0},{40,8},{48,16},{56,24},{64,96... | collective-permute-start | bytes 2162696 | tf_op jit(solution)/shard_map/ppermute | solution.py:190
  172.8 23.7 %collective-permute-start.7 = (f32[864,128]{1,0:T(8,128)S(1)}, f32[864,128]{1,0:T(8,128)S(1)}, u32[]{:S(2)}, u32[]{:S(2)}) collective-permute-start(f32[864,128]{1,0:T(8,128)S(1)} %get-tuple-element.26.own_ref), channel_id=1, source_target_pairs={{0,64},{8,72},{16,80},{24,88},{32,96},{40,104},{48,112},{56,120},{... | collective-permute-start | bytes 1327112 | tf_op jit(solution)/shard_map/ppermute | solution.py:190
  199.7 26.1 %collective-permute-start.8 = (f32[448,128]{1,0:T(8,128)S(1)}, f32[448,128]{1,0:T(8,128)S(1)}, u32[]{:S(2)}, u32[]{:S(2)}) collective-permute-start(f32[448,128]{1,0:T(8,128)S(1)} %get-tuple-element.28.own_ref), channel_id=1, source_target_pairs={{0,128},{8,136},{16,144},{24,152},{32,160},{40,168},{48,176},{56,1... | collective-permute-start | bytes 688136 | tf_op jit(solution)/shard_map/ppermute | solution.py:190
  228.6 19.0 %collective-permute-start.9 = (f32[160,128]{1,0:T(8,128)S(1)}, f32[160,128]{1,0:T(8,128)S(1)}, u32[]{:S(2)}, u32[]{:S(2)}) collective-permute-start(f32[160,128]{1,0:T(8,128)S(1)} %get-tuple-element.30.own_ref), channel_id=1, source_target_pairs={{0,256},{8,264},{16,272},{24,280},{32,288},{40,296},{48,304},{56,3... | collective-permute-start | bytes 245768 | tf_op jit(solution)/shard_map/ppermute | solution.py:190
Sparse Core Ops, SparseCore 0:
  9.5 38.5 all-gather.1

commit v2 on v0

v2 whole, which is shorter than its diff:
```python
import functools

import jax
import jax.numpy as jnp
from jax import lax
from jax.experimental import pallas as pl
from jax.experimental.pallas import tpu as pltpu
from jax.sharding import PartitionSpec as P

F32 = jnp.float32
BF16 = jnp.bfloat16
FULL = lax.Precision.HIGHEST
TRIPLE = lax.Precision.HIGH
DOUBLINGS = 3
MEMBERS = 8
CORES = 2
CHIPS = MEMBERS // CORES
PAD = 64
VMEM_BYTES = 16 * 1024 * 1024
BOTH = ("leaf", "rows")
NEAR = (1, 3, 4, 8, 16, 48)


def mm(a, b, precision=TRIPLE):
    return lax.dot_general(a, b, (((1,), (0,)), ((), ())), precision=precision, preferred_element_type=F32)


def mm_nt(a, b, precision=TRIPLE):
    return lax.dot_general(a, b, (((1,), (1,)), ((), ())), precision=precision, preferred_element_type=F32)


def share_rows(height, tiers, rank):
    return PAD // MEMBERS + (rank // MEMBERS) * (tiers - height)


def inverses(pairs):
    rank = pairs[0][0].shape[0]
    eye = (
        lax.broadcasted_iota(jnp.int32, (rank, rank), 0) == lax.broadcasted_iota(jnp.int32, (rank, rank), 1)
    ).astype(F32)
    powers = [mm(left, right) for left, right in pairs]
    systems = [eye - power for power in powers]
    guesses = [eye + power for power in powers]
    for _ in range(DOUBLINGS):
        powers = [mm(power, power) for power in powers]
        guesses = [guess + mm(guess, power) for guess, power in zip(guesses, powers)]
    gaps = [eye - mm(system, guess) for system, guess in zip(systems, guesses)]
    size = functools.reduce(jnp.maximum, [jnp.sum(gap * gap) for gap in gaps])

    def close():
        return [guess + mm(guess, gap) for guess, gap in zip(guesses, gaps)]

    def refine(left, right, guess):
        system = eye - mm(left, right, FULL)
        entries = jnp.abs(system)
        bound = jnp.max(jnp.sum(entries, axis=0)) * jnp.max(jnp.sum(entries, axis=1))

        def measured(x):
            gap = eye - mm(system, x, FULL)
            return x, gap, jnp.sum(gap * gap)

        def step(carry):
            count, _, x, gap, size = carry
            return (count + 1, size) + measured(x + mm(x, gap, FULL))

        def more(carry):
            count, before, _, _, size = carry
            falls = jnp.logical_and(size > 1e-10, size < 0.5 * before)
            return jnp.logical_and(count < 80, jnp.logical_or(size >= 0.25, falls))

        first = measured(guess)
        first = lax.cond(first[2] < 0.25, lambda: first, lambda: measured(system.T / bound))
        return lax.while_loop(more, step, (0, jnp.float32(jnp.inf)) + first)[2]

    def far_off():
        return [refine(left, right, guess) for (left, right), guess in zip(pairs, guesses)]

    return lax.cond(size < 1e-6, close, far_off)


def position(height):
    leaf, row = lax.axis_index("leaf"), lax.axis_index("rows")
    core = row % CORES
    return core, core * CHIPS + row // CORES, (leaf // 2**height) % 2


def without(section, width, rank):
    if section.shape[0] == width + rank:
        return section[:width]
    return jnp.concatenate([section[:width], section[width + rank :]], axis=0)


def couple(children, width, rank):
    blocks = [(s[width : width + rank], t[width : width + rank]) for s, t in children]
    found = []
    for (s, t), (s_a, t_a), inverse in zip(children, blocks, inverses(blocks)):
        s_r, t_r = without(s, width, rank), without(t, width, rank)
        s_c = mm(t_r - mm(s_r, t_a), inverse)
        found.append((s_c, s_r - mm(s_c, s_a)))
    return found


def images_of(s, t, width, rank):
    return jnp.concatenate([s[width + rank :], t[width + rank :]], axis=1)


def gathered(first, second, place, rank):
    low, each = PAD // MEMBERS, rank // MEMBERS

    def joined(start, rows):
        halves = [half[:, start : start + rows] for half in (first, second)]
        return jnp.concatenate([half.reshape(half.shape[0] * rows, rank) for half in halves], axis=0)

    def section(width, blocks):
        parts = [joined(place, low)[:width]]
        parts += [joined(place + low + each * k, each) for k in range(blocks)]
        return jnp.concatenate(parts, axis=0)

    return section


def share_level_kernel(height, tiers, rank, width, mine_ref, theirs_ref, coeff_ref, change_ref, wide_ref):
    rest = tiers - height - 1
    core, member, bit = position(height)
    mine, theirs = mine_ref[...], theirs_ref[...]
    first = jnp.where(core == 0, mine, theirs)
    second = jnp.where(core == 0, theirs, mine)
    s, t = [
        gathered(first[CHIPS * k : CHIPS * (k + 1)], second[CHIPS * k : CHIPS * (k + 1)], 0, rank)(width, rest + 1)
        for k in range(2)
    ]
    ((s_c, t_c),) = couple([(s, t)], width, rank)
    coeff_ref[...] = jnp.where(bit == 0, s_c, t_c)
    both = jnp.concatenate([s_c, t_c], axis=1)
    wide_ref[0:width, :] = both[:width]
    wide_ref[width:PAD, :] = jnp.zeros((PAD - width, 2 * rank), F32)
    wide_ref[PAD : PAD + rank * rest, :] = both[width:]
    low, each = PAD // MEMBERS, rank // MEMBERS
    slices = [wide_ref[pl.ds(pl.multiple_of(member * low, low), low), :]]
    for k in range(rest):
        slices.append(wide_ref[pl.ds(pl.multiple_of(PAD + rank * k + member * each, each), each), :])
    change = mm_nt(jnp.concatenate(slices, axis=0), images_of(s, t, width, rank))
    place = 0
    for g in range(rest):
        columns = slice(rank * g, rank * (g + 1))
        part = jnp.concatenate([change[:low, columns], change[low + each * g :, columns]], axis=0)
        rows = low + each * (rest - g)
        change_ref[place : place + rows, :] = part
        place += rows


def vmem(count):
    return [pl.BlockSpec(memory_space=pltpu.VMEM)] * count


def params():
    return pltpu.CompilerParams(vmem_limit_bytes=VMEM_BYTES)


def share_level(height, tiers, rank, width, mine, theirs):
    rest = tiers - height - 1
    rows = sum(share_rows(h, tiers, rank) for h in range(height + 1, tiers))
    return pl.pallas_call(
        functools.partial(share_level_kernel, height, tiers, rank, width),
        out_shape=[
            jax.ShapeDtypeStruct((width + rank * rest, rank), F32),
            jax.ShapeDtypeStruct((rows, rank), F32),
        ],
        in_specs=vmem(2),
        out_specs=vmem(2),
        scratch_shapes=[pltpu.VMEM((PAD + rank * rest, 2 * rank), F32)],
        compiler_params=params(),
        name=f"level{height}",
    )(mine, theirs)


def merged(coeffs, s, t, width, rank):
    both = jnp.concatenate(coeffs, axis=1)
    images = images_of(s[0], t[0], width, rank)
    top = mm_nt(both[:width], images)
    out = []
    for g in range(len(s) - 1):
        columns = slice(rank * g, rank * (g + 1))
        low = mm_nt(both[width + rank * g :], images[columns])
        out.append(s[g + 1] + t[g + 1] - jnp.concatenate([top[:, columns], low], axis=0))
    return out


def first_pair_kernel(height, tiers, rank, width, mine_ref, theirs_ref, coeff_ref, next_ref):
    core, _, bit = position(height)
    mine, theirs = mine_ref[...], theirs_ref[...]
    first = jnp.where(core == 0, mine, theirs)
    second = jnp.where(core == 0, theirs, mine)
    nodes = []
    for k in range(2):
        span = slice(CHIPS * k, CHIPS * (k + 1))
        place, sections = 0, []
        for h in range(height, tiers):
            sections.append(gathered(first[span], second[span], place, rank)(width, tiers - h))
            place += share_rows(h, tiers, rank)
        nodes.append(sections)
    join_pair(bit, nodes[0], nodes[1], width, rank, coeff_ref, next_ref)


def join_pair(bit, s, t, width, rank, coeff_ref, next_ref):
    (pair,) = couple([(s[0], t[0])], width, rank)
    coeff_ref[...] = jnp.where(bit == 0, pair[0], pair[1])
    place = 0
    for section in merged(pair, s, t, width, rank):
        next_ref[place : place + section.shape[0], :] = section
        place += section.shape[0]


def pair_kernel(height, tiers, rank, width, own_ref, got_ref, passed_ref, coeff_ref, next_ref):
    core, _, bit = position(height)
    own, got, passed = own_ref[...], got_ref[...], passed_ref[...]
    far = jnp.concatenate([jnp.where(core == 0, got, passed), jnp.where(core == 0, passed, got)], axis=0)
    lower = jnp.where(bit == 0, own, far)
    upper = jnp.where(bit == 0, far, own)

    def cut(value):
        place, out = 0, []
        for h in range(height, tiers):
            rows = width + rank * (tiers - h)
            out.append(value[place : place + rows])
            place += rows
        return out

    join_pair(bit, cut(lower), cut(upper), width, rank, coeff_ref, next_ref)


def pair_level(kernel, height, tiers, rank, width, *sections):
    rows = sum(width + rank * (tiers - h) for h in range(height + 1, tiers))
    return pl.pallas_call(
        functools.partial(kernel, height, tiers, rank, width),
        out_shape=[
            jax.ShapeDtypeStruct((width + rank * (tiers - height - 1), rank), F32),
            jax.ShapeDtypeStruct((rows, rank), F32),
        ],
        in_specs=vmem(len(sections)),
        out_specs=vmem(2),
        compiler_params=params(),
        name=f"level{height}",
    )(*sections)


def finish_kernel(tiers, rank, width, own_ref, far_ref, solved_ref, images_ref, *refs):
    coeff_refs, out_ref = refs[: tiers - 1], refs[tiers - 1]
    ((value, _),) = couple([(own_ref[...], far_ref[...])], width, rank)
    found = [None] * tiers
    found[tiers - 1] = value
    for h in reversed(range(tiers - 1)):
        above = jnp.concatenate(found[h + 1 :], axis=1)
        found[h] = coeff_refs[h][0:width, :] - mm(above, coeff_refs[h][width:, :])
    out_ref[...] = solved_ref[...] - mm_nt(images_ref[...], jnp.concatenate(found, axis=1))


def finish(tiers, rank, width, own, far, solved, images, coeffs):
    return pl.pallas_call(
        functools.partial(finish_kernel, tiers, rank, width),
        out_shape=jax.ShapeDtypeStruct(solved.shape, F32),
        in_specs=vmem(4 + len(coeffs)),
        out_specs=pl.BlockSpec(memory_space=pltpu.VMEM),
        compiler_params=params(),
        name="finish",
    )(own, far, solved, images, *coeffs)


def reorder_kernel(order_ref, inverse_ref, out_ref):
    columns = inverse_ref.shape[1]
    step = columns // MEMBERS
    inverse = inverse_ref[...]
    order = order_ref[...]
    for k in range(MEMBERS):
        given = lax.broadcasted_iota(jnp.int32, (step, columns), 0) + step * k
        chosen = jnp.where(given == order, 1.0, 0.0).astype(BF16)
        moved = lax.dot_general(inverse, chosen, (((1,), (1,)), ((), ())), preferred_element_type=F32)
        out_ref[:, step * k : step * (k + 1)] = moved.astype(BF16)


def reorder(order, inverse):
    return pl.pallas_call(
        reorder_kernel,
        out_shape=jax.ShapeDtypeStruct(inverse.shape, BF16),
        in_specs=vmem(2),
        out_specs=pl.BlockSpec(memory_space=pltpu.VMEM),
        compiler_params=params(),
        cost_estimate=pl.CostEstimate(
            flops=2 * inverse.size * inverse.shape[1], bytes_accessed=4 * inverse.size, transcendentals=0
        ),
        name="reorder",
    )(order, inverse)


def leaf_kernel(
    tiers, rank, width, inverse_ref, moved_ref, mine_ref, theirs_ref, own_ref, solved_ref, images_ref, gram_ref, images_vmem, sem
):
    rows = own_ref.shape[1]
    core = lax.axis_index("rows") % CORES
    images, solved = None, None
    for chip in range(CHIPS):
        for ref, side in ((mine_ref, core), (theirs_ref, 1 - core)):
            columns = pl.ds(pl.multiple_of((CORES * chip + side) * rows, rows), rows)
            wide = jnp.concatenate([ref[chip, h] for h in range(tiers)], axis=1)
            term = mm(inverse_ref[:, columns], wide, None)
            images = term if images is None else images + term
            term = mm(moved_ref[:, columns], ref[chip, tiers][:, :width], None)
            solved = term if solved is None else solved + term
    solved_ref[...] = solved
    images_vmem[...] = images
    copy = pltpu.make_async_copy(images_vmem, images_ref, sem)
    copy.start()
    live = jnp.concatenate([images, solved], axis=1)
    high = live.astype(BF16)
    left = live - high.astype(F32)
    middle = left.astype(BF16)
    low = (left - middle.astype(F32)).astype(BF16)

    def project(first, last, basis):
        total = None
        for piece in (high, middle, low):
            term = lax.dot_general(
                piece[:, first:last], basis, (((0,), (0,)), ((), ())), preferred_element_type=F32
            )
            total = term if total is None else total + term
        return total

    few, each = PAD // MEMBERS, rank // MEMBERS
    place = 0
    for h in range(tiers):
        basis = own_ref[h]
        top = project(rank * tiers, rank * tiers + width, basis)
        top = jnp.concatenate([top, jnp.zeros((PAD - width, rank), F32)], axis=0)
        gram_ref[:, place : place + few, :] = top.reshape(MEMBERS, few, rank)
        place += few
        body = project(rank * h, rank * tiers, basis)
        for k in range(tiers - h):
            block = body[rank * k : rank * (k + 1)]
            gram_ref[:, place : place + each, :] = block.reshape(MEMBERS, each, rank)
            place += each
    copy.wait()


def leaf_step(tiers, rank, width, inverse, moved, mine, theirs, own):
    rows = inverse.shape[0]
    share = sum(share_rows(h, tiers, rank) for h in range(tiers))
    return pl.pallas_call(
        functools.partial(leaf_kernel, tiers, rank, width),
        out_shape=[
            jax.ShapeDtypeStruct((rows, width), F32),
            jax.ShapeDtypeStruct((rows, tiers * rank), F32),
            jax.ShapeDtypeStruct((MEMBERS, share, rank), F32),
        ],
        in_specs=vmem(5),
        out_specs=vmem(1) + [pl.BlockSpec(memory_space=pl.ANY)] + vmem(1),
        scratch_shapes=[pltpu.VMEM((rows, tiers * rank), F32), pltpu.SemaphoreType.DMA],
        compiler_params=params(),
        name="leaf",
    )(inverse, moved, mine, theirs, own)


def swap_cores(value):
    return lax.ppermute(value, "rows", [(i, i ^ 1) for i in range(MEMBERS)])


def swap_leaves(value, mask):
    return lax.ppermute(value, "leaf", [(i, i ^ mask) for i in range(lax.axis_size("leaf"))])


def groups_of(sets):
    return [
        [leaf * MEMBERS + chip * CORES + core for leaf in leaves for chip in range(CHIPS)]
        for leaves in sets
        for core in range(CORES)
    ]


def spread(value, sets):
    groups = groups_of(sets)
    count = len(groups[0])
    return lax.all_to_all(
        jnp.broadcast_to(value[None], (count,) + value.shape), BOTH, 0, 0, axis_index_groups=groups
    )


def local(right_side, point_order, leaf_inverse, bases):
    tiers, rank, width = bases.shape[1], bases.shape[2], right_side.shape[1]
    leaves = range(lax.axis_size("leaf"))
    own = jnp.concatenate(
        [jnp.swapaxes(bases, 0, 1), jnp.pad(right_side, ((0, 0), (0, rank - width)))[None]], axis=0
    )
    groups = [[c + CORES * y for y in range(CHIPS)] for c in range(CORES)]
    mine = lax.all_to_all(jnp.broadcast_to(own[None], (CHIPS,) + own.shape), "rows", 0, 0, axis_index_groups=groups)
    theirs = swap_cores(mine)
    order, inverse, _ = lax.optimization_barrier((point_order, leaf_inverse, mine))
    moved = reorder(order, inverse)
    solved, images, gram = leaf_step(tiers, rank, width, leaf_inverse, moved, mine, theirs, own)

    core = lax.axis_index("rows") % CORES

    keep = lax.dynamic_slice_in_dim(gram, core * CHIPS, CHIPS)
    give = lax.dynamic_slice_in_dim(gram, (1 - core) * CHIPS, CHIPS)
    parts = keep + swap_cores(give)
    share = lax.all_to_all(parts, "rows", 0, 0, axis_index_groups=groups).sum(axis=0)

    coeffs = []
    for height in range(2):
        cut = share_rows(height, tiers, rank)
        section, own = share[:cut], share[cut:]
        far = swap_leaves(own, NEAR[height])
        sets = [(i, i ^ NEAR[height]) for i in leaves if not (i >> height) & 1]
        mine = spread(section, sets)
        theirs = swap_cores(mine)
        coeff, change = share_level(height, tiers, rank, width, mine, theirs)
        share = own + far - change
        coeffs.append(coeff)

    mine = spread(share, [(i, i ^ NEAR[2]) for i in leaves if not (i >> 2) & 1])
    theirs = swap_cores(mine)
    coeff, own = pair_level(first_pair_kernel, 2, tiers, rank, width, mine, theirs)
    coeffs.append(coeff)
    for height in range(3, tiers - 1):
        half = own.shape[0] // CORES
        got = swap_leaves(lax.dynamic_slice_in_dim(own, core * half, half), NEAR[height])
        passed = swap_cores(got)
        coeff, own = pair_level(pair_kernel, height, tiers, rank, width, own, got, passed)
        coeffs.append(coeff)
    far = swap_leaves(own, NEAR[5])
    return finish(tiers, rank, width, own, far, solved, images, coeffs)


def solution(mesh):
    in_specs = (
        P(("leaf", "rows"), None),
        P("leaf", None),
        P(("leaf", "rows"), None),
        P(("leaf", "rows"), None, None),
    )
    out_specs = P(("leaf", "rows"), None)
    return jax.shard_map(local, mesh=mesh, in_specs=in_specs, out_specs=out_specs, check_vma=False)
```

time: 899 us -> 194 us (0.22)
  waiting for transfers between devices: 584 us -> 37.8 us
  other arithmetic: 143 us -> 2.36 us
  blocking collectives: 15.6 us -> 82.3 us
  starting transfers between devices: 90.6 us -> 40.1 us
  matrix products: 30.2 us -> 0 us
  Pallas kernels: 0 us -> 22.7 us
  between operations: 14.7 us -> 0.37 us
  local copies, waits for them, and re-layouts: 16 us -> 4.5 us
    psum x6 -> x0, waiting for transfers between devices: 437 us -> none  [local(): summed = lax.psum(project(basis_f[:, height, :], live), 'rows')]
    another operation x30 -> x0, other arithmetic: 137 us -> none  [the longest x18 74.3 us: couple(): factor = jnp.linalg.cholesky(gram)]
    ppermute x21 -> x12, waiting for transfers between devices: 128 us -> 37.8 us  [the longest x5 29.2 us: swap_leaves(): lax.ppermute(value, 'leaf', [(i, i ^ mask) for i in range(lax.axis_size('...]
    all_to_all x0 -> x5, blocking collectives: none -> 82.3 us  [the longest x3 41 us: spread(): lax.all_to_all(jnp.broadcast_to(value[None], (count,) + value.shape), BOT...]
    ppermute x21 -> x12, starting transfers between devices: 90.4 us -> 40.1 us  [the longest x5 26.5 us: swap_leaves(): lax.ppermute(value, 'leaf', [(i, i ^ mask) for i in range(lax.axis_size('...]
    dot_general x38 -> x0, matrix products: 26.5 us -> none  [the longest x6 8.67 us: project(): return jnp.einsum('nk,nc->kc', basis_rows, values, precision=HIGHEST)]
    pallas_call x0 -> x8, Pallas kernels: none -> 22.7 us  [the longest x3 7.47 us: pair_level(): pl.pallas_call(functools.partial(kernel, height, tiers, rank, width), out...]
    all_gather x1 -> x0, waiting for transfers between devices: 19 us -> none  [local(): lax.all_gather(bases, 'rows', axis=0, tiled=True)]
  transfers between devices with their start and end apart: 28 -> 12, of which waited for: 28 -> 10; matrix products, arithmetic and copies ran while one was open for 1% -> 0% of each run, Pallas kernels for 0% -> 4%
where the time goes in v2:
time: 194 us; the launch traced here: 190 us
  blocking collectives  82.3 us (42%)
  starting transfers between devices  40.1 us (21%)
  waiting for transfers between devices  37.8 us (19%)
  Pallas kernels  22.7 us (12%)
  local copies, waits for them, and re-layouts  4.5 us (2%)
  other arithmetic  2.36 us (1%)
    all_to_all x3, blocking collectives, spread(): lax.all_to_all(jnp.broadcast_to(value[None], (count,) + value.shape), BOT...  41 us
    ppermute x5, waiting for transfers between devices, swap_leaves(): lax.ppermute(value, 'leaf', [(i, i ^ mask) for i in range(lax.axis_size('...  29.2 us
    ppermute x5, starting transfers between devices, swap_leaves(): lax.ppermute(value, 'leaf', [(i, i ^ mask) for i in range(lax.axis_size('...  26.5 us
    all_to_all x1, blocking collectives, local(): lax.all_to_all(jnp.broadcast_to(own[None], (CHIPS,) + own.shape), 'rows',...  26.1 us
    all_to_all x1, blocking collectives, local(): lax.all_to_all(parts, 'rows', 0, 0, axis_index_groups=groups).sum(axis=0)  15.3 us
    ppermute x7, starting transfers between devices, swap_cores(): return lax.ppermute(value, 'rows', [(i, i ^ 1) for i in range(MEMBERS)])  13.7 us
    ppermute x7, waiting for transfers between devices, swap_cores(): return lax.ppermute(value, 'rows', [(i, i ^ 1) for i in range(MEMBERS)])  8.53 us
    pallas_call x3, Pallas kernels, pair_level(): pl.pallas_call(functools.partial(kernel, height, tiers, rank, width), out...  7.47 us
  transfers between devices with their start and end apart: 12, of which 10 were waited for; matrix products, arithmetic and copies ran while one was open for 0% of the time, Pallas kernels for 4%

profile of v2, /device:TPU:24, one launch (start us, length us, event | category | flops | bytes accessed | tf_op | source)
XLA Modules:
  0.0 190.1 jit_solution(8347560640573629569)
XLA Ops:
  2.3 26.1 %all_to_all.25.mine_ref = bf16[4,7,256,128]{3,2,1,0:T(8,128)(2,1)S(1)} all-to-all(bf16[4,7,256,128]{3,2,1,0:T(8,128)(2,1)S(1)} %broadcast_in_dim.11), channel_id=1, replica_groups={{0,2,4,6},{1,3,5,7},{8,10,12,14},{9,11,13,15},{16,18,20,22},{17,19,21,2..., dimensions={0} | all-to-all | bytes 3670016 | tf_op jit(solution)/shard_map/all_to_all | solution.py:393
  28.4 1.9 %collective-permute-start = (bf16[4,7,256,128]{3,2,1,0:T(8,128)(2,1)S(1)}, bf16[4,7,256,128]{3,2,1,0:T(8,128)(2,1)}, u32[]{:S(2)}, u32[]{:S(2)}) collective-permute-start(bf16[4,7,256,128]{3,2,1,0:T(8,128)(2,1)S(1)} %all_to_all.25.mine_ref), channel_id=1, source_target_pairs={{0,1},{1,0},{2,3},{3,2},{4,5},{5,4},{6,7},{7,6},{8,9},{9,8},{10,11... | collective-permute-start | bytes 5505032 | tf_op jit(solution)/shard_map/ppermute | solution.py:363
  30.4 2.4 %reorder.1.moved_ref = bf16[256,2048]{1,0:T(8,128)(2,1)S(1)} custom-call(s32[1,2048]{1,0:T(1,128)S(1)} %copy-done.6, bf16[256,2048]{1,0:T(8,128)(2,1)S(1)} %copy-done.1), custom_call_target="tpu_custom_call" | custom-call | flops 2147483648 | bytes 2097152 | tf_op jit(solution)/shard_map/reorder/pallas_call | solution.py:282
  34.2 4.3 %leaf.1 = (f32[256,32]{1,0:T(8,128)S(1)}, f32[256,768]{1,0:T(8,128)S(1)}, f32[8,384,128]{2,1,0:T(8,128)S(1)}) custom-call(bf16[256,2048]{1,0:T(8,128)(2,1)S(1)} %copy-done.1, bf16[256,2048]{1,0:T(8,128)(2,1)S(1)} %reorder.1.moved_ref, bf16[4,7,256,128]{3,2,1,0:T(8,128)(2,1)S(1)} %all_to_all.25.mine_ref, ...), custom_call_target="tpu_custom_call" | custom-call | tf_op jit(solution)/shard_map/leaf/pallas_call | solution.py:347
  40.0 2.0 %collective-permute-start.1 = (f32[4,384,128]{2,1,0:T(8,128)S(1)}, f32[4,384,128]{2,1,0:T(8,128)S(1)}, u32[]{:S(2)}, u32[]{:S(2)}) collective-permute-start(f32[4,384,128]{2,1,0:T(8,128)S(1)} %constant_dynamic-slice_fusion.2), channel_id=1, source_target_pairs={{0,1},{1,0},{2,3},{3,2},{4,5},{5,4},{6,7},{7,6},{8,9},{9,8},{10,11... | collective-permute-start | bytes 2359304 | tf_op jit(solution)/shard_map/ppermute | solution.py:363
  42.0 2.1 %collective-permute-done.1 = f32[4,384,128]{2,1,0:T(8,128)S(1)} collective-permute-done((f32[4,384,128]{2,1,0:T(8,128)S(1)}, f32[4,384,128]{2,1,0:T(8,128)S(1)}, u32[]{:S(2)}, u32[]{:S(2)}) %collective-permute-start.1) | collective-permute-done | bytes 786464 | tf_op jit(solution)/shard_map/ppermute | solution.py:363
  45.4 15.3 %all_to_all.26 = f32[4,384,128]{2,1,0:T(8,128)S(1)} all-to-all(f32[4,384,128]{2,1,0:T(8,128)S(1)} %dynamic-slice_add_fusion), channel_id=1, replica_groups={{0,2,4,6},{1,3,5,7},{8,10,12,14},{9,11,13,15},{16,18,20,22},{17,19,21,2..., dimensions={0} | all-to-all | bytes 1572864 | tf_op jit(solution)/shard_map/all_to_all | solution.py:404
  60.7 11.5 %all_to_all.27.mine_ref = f32[8,104,128]{2,1,0:T(8,128)S(1)} all-to-all(f32[8,104,128]{2,1,0:T(8,128)S(1)} %broadcast_in_dim.12), channel_id=1, replica_groups={{0,2,4,6,8,10,12,14},{1,3,5,7,9,11,13,15},{16,18,20,22,24,26,28,30},{17..., dimensions={0} | all-to-all | bytes 851968 | tf_op jit(solution)/shard_map/all_to_all | solution.py:381
  72.2 1.9 %collective-permute-start.3 = (f32[8,104,128]{2,1,0:T(8,128)S(1)}, f32[8,104,128]{2,1,0:T(8,128)S(1)}, u32[]{:S(2)}, u32[]{:S(2)}) collective-permute-start(f32[8,104,128]{2,1,0:T(8,128)S(1)} %all_to_all.27.mine_ref), channel_id=1, source_target_pairs={{0,1},{1,0},{2,3},{3,2},{4,5},{5,4},{6,7},{7,6},{8,9},{9,8},{10,11... | collective-permute-start | bytes 1277960 | tf_op jit(solution)/shard_map/ppermute | solution.py:363
  74.2 2.9 %collective-permute-start.2 = (f32[280,128]{1,0:T(8,128)S(1)}, f32[280,128]{1,0:T(8,128)S(1)}, u32[]{:S(2)}, u32[]{:S(2)}) collective-permute-start(f32[280,128]{1,0:T(8,128)S(1)} %slice.16), channel_id=1, source_target_pairs={{0,8},{8,0},{16,24},{24,16},{32,40},{40,32},{48,56},{56,48},{64,72... | collective-permute-start | bytes 430088 | tf_op jit(solution)/shard_map/ppermute | solution.py:367
  77.1 2.9 %level0.1 = (f32[672,128]{1,0:T(8,128)S(1)}, f32[280,128]{1,0:T(8,128)S(1)}) custom-call(f32[8,104,128]{2,1,0:T(8,128)S(1)} %all_to_all.27.mine_ref, f32[8,104,128]{2,1,0:T(8,128)S(1)} %collective-permute-done.3.theirs_ref), custom_call_target="tpu_custom_call" | custom-call | tf_op jit(solution)/shard_map/level0/pallas_call | solution.py:163
  80.0 2.2 %collective-permute-done.2 = f32[280,128]{1,0:T(8,128)S(1)} collective-permute-done((f32[280,128]{1,0:T(8,128)S(1)}, f32[280,128]{1,0:T(8,128)S(1)}, u32[]{:S(2)}, u32[]{:S(2)}) %collective-permute-start.2) | collective-permute-done | bytes 143392 | tf_op jit(solution)/shard_map/ppermute | solution.py:367
  82.3 13.4 %all_to_all.28.mine_ref = f32[8,88,128]{2,1,0:T(8,128)S(1)} all-to-all(f32[8,88,128]{2,1,0:T(8,128)S(1)} %broadcast_in_dim.13), channel_id=1, replica_groups={{0,2,4,6,24,26,28,30},{1,3,5,7,25,27,29,31},{8,10,12,14,16,18,20,22},{9..., dimensions={0} | all-to-all | bytes 720896 | tf_op jit(solution)/shard_map/all_to_all | solution.py:381
  95.7 1.9 %collective-permute-start.5 = (f32[8,88,128]{2,1,0:T(8,128)S(1)}, f32[8,88,128]{2,1,0:T(8,128)S(1)}, u32[]{:S(2)}, u32[]{:S(2)}) collective-permute-start(f32[8,88,128]{2,1,0:T(8,128)S(1)} %all_to_all.28.mine_ref), channel_id=1, source_target_pairs={{0,1},{1,0},{2,3},{3,2},{4,5},{5,4},{6,7},{7,6},{8,9},{9,8},{10,11... | collective-permute-start | bytes 1081352 | tf_op jit(solution)/shard_map/ppermute | solution.py:363
  97.7 2.7 %collective-permute-start.4 = (f32[192,128]{1,0:T(8,128)S(1)}, f32[192,128]{1,0:T(8,128)S(1)}, u32[]{:S(2)}, u32[]{:S(2)}) collective-permute-start(f32[192,128]{1,0:T(8,128)S(1)} %slice.18), channel_id=1, source_target_pairs={{0,24},{8,16},{16,8},{24,0},{32,56},{40,48},{48,40},{56,32},{64,88... | collective-permute-start | bytes 294920 | tf_op jit(solution)/shard_map/ppermute | solution.py:367
  100.4 2.7 %level1.1 = (f32[544,128]{1,0:T(8,128)S(1)}, f32[192,128]{1,0:T(8,128)S(1)}) custom-call(f32[8,88,128]{2,1,0:T(8,128)S(1)} %all_to_all.28.mine_ref, f32[8,88,128]{2,1,0:T(8,128)S(1)} %collective-permute-done.5.theirs_ref), custom_call_target="tpu_custom_call" | custom-call | tf_op jit(solution)/shard_map/level1/pallas_call | solution.py:163
  103.1 2.8 %collective-permute-done.4 = f32[192,128]{1,0:T(8,128)S(1)} collective-permute-done((f32[192,128]{1,0:T(8,128)S(1)}, f32[192,128]{1,0:T(8,128)S(1)}, u32[]{:S(2)}, u32[]{:S(2)}) %collective-permute-start.4) | collective-permute-done | bytes 98336 | tf_op jit(solution)/shard_map/ppermute | solution.py:367
  106.0 16.0 %all_to_all.29.mine_ref = f32[8,192,128]{2,1,0:T(8,128)S(1)} all-to-all(f32[8,192,128]{2,1,0:T(8,128)S(1)} %broadcast_in_dim.14), channel_id=1, replica_groups={{0,2,4,6,32,34,36,38},{1,3,5,7,33,35,37,39},{8,10,12,14,40,42,44,46},{9..., dimensions={0} | all-to-all | bytes 1572864 | tf_op jit(solution)/shard_map/all_to_all | solution.py:381
  122.1 2.0 %collective-permute-start.6 = (f32[8,192,128]{2,1,0:T(8,128)S(1)}, f32[8,192,128]{2,1,0:T(8,128)S(1)}, u32[]{:S(2)}, u32[]{:S(2)}) collective-permute-start(f32[8,192,128]{2,1,0:T(8,128)S(1)} %all_to_all.29.mine_ref), channel_id=1, source_target_pairs={{0,1},{1,0},{2,3},{3,2},{4,5},{5,4},{6,7},{7,6},{8,9},{9,8},{10,11... | collective-permute-start | bytes 2359304 | tf_op jit(solution)/shard_map/ppermute | solution.py:363
  124.1 2.2 %collective-permute-done.6.theirs_ref = f32[8,192,128]{2,1,0:T(8,128)S(1)} collective-permute-done((f32[8,192,128]{2,1,0:T(8,128)S(1)}, f32[8,192,128]{2,1,0:T(8,128)S(1)}, u32[]{:S(2)}, u32[]{:S(2)}) %collective-permute-start.6) | collective-permute-done | bytes 786464 | tf_op jit(solution)/shard_map/ppermute | solution.py:363
  126.4 2.9 %level2.1 = (f32[416,128]{1,0:T(8,128)S(1)}, f32[864,128]{1,0:T(8,128)S(1)}) custom-call(f32[8,192,128]{2,1,0:T(8,128)S(1)} %all_to_all.29.mine_ref, f32[8,192,128]{2,1,0:T(8,128)S(1)} %collective-permute-done.6.theirs_ref), custom_call_target="tpu_custom_call" | custom-call | tf_op jit(solution)/shard_map/level2/pallas_call | solution.py:234
  129.4 5.2 %collective-permute-start.7 = (f32[432,128]{1,0:T(8,128)S(1)}, f32[432,128]{1,0:T(8,128)S(1)}, u32[]{:S(2)}, u32[]{:S(2)}) collective-permute-start(f32[432,128]{1,0:T(8,128)S(1)} %constant_dynamic-slice_fusion.1), channel_id=1, source_target_pairs={{0,64},{8,72},{16,80},{24,88},{32,96},{40,104},{48,112},{56,120},{... | collective-permute-start | bytes 663560 | tf_op jit(solution)/shard_map/ppermute | solution.py:367
  134.6 10.4 %collective-permute-done.7.got_ref = f32[432,128]{1,0:T(8,128)S(1)} collective-permute-done((f32[432,128]{1,0:T(8,128)S(1)}, f32[432,128]{1,0:T(8,128)S(1)}, u32[]{:S(2)}, u32[]{:S(2)}) %collective-permute-start.7) | collective-permute-done | bytes 221216 | tf_op jit(solution)/shard_map/ppermute | solution.py:367
  145.0 1.9 %collective-permute-start.8 = (f32[432,128]{1,0:T(8,128)S(1)}, f32[432,128]{1,0:T(8,128)S(1)}, u32[]{:S(2)}, u32[]{:S(2)}) collective-permute-start(f32[432,128]{1,0:T(8,128)S(1)} %collective-permute-done.7.got_ref), channel_id=1, source_target_pairs={{0,1},{1,0},{2,3},{3,2},{4,5},{5,4},{6,7},{7,6},{8,9},{9,8},{10,11... | collective-permute-start | bytes 663560 | tf_op jit(solution)/shard_map/ppermute | solution.py:363
  148.4 2.4 %level3.1 = (f32[288,128]{1,0:T(8,128)S(1)}, f32[448,128]{1,0:T(8,128)S(1)}) custom-call(f32[864,128]{1,0:T(8,128)S(1)} %get-tuple-element.25.own_ref, f32[432,128]{1,0:T(8,128)S(1)} %collective-permute-done.7.got_ref, f32[432,128]{1,0:T(8,128)S(1)} %collective-permute-done.8.passed_ref), custom_call_target="tpu_custom_call" | custom-call | tf_op jit(solution)/shard_map/level3/pallas_call | solution.py:234
  150.8 9.1 %collective-permute-start.9 = (f32[224,128]{1,0:T(8,128)S(1)}, f32[224,128]{1,0:T(8,128)S(1)}, u32[]{:S(2)}, u32[]{:S(2)}) collective-permute-start(f32[224,128]{1,0:T(8,128)S(1)} %constant_dynamic-slice_fusion), channel_id=1, source_target_pairs={{0,128},{8,136},{16,144},{24,152},{32,160},{40,168},{48,176},{56,1... | collective-permute-start | bytes 344072 | tf_op jit(solution)/shard_map/ppermute | solution.py:367
  159.9 9.8 %collective-permute-done.9.got_ref = f32[224,128]{1,0:T(8,128)S(1)} collective-permute-done((f32[224,128]{1,0:T(8,128)S(1)}, f32[224,128]{1,0:T(8,128)S(1)}, u32[]{:S(2)}, u32[]{:S(2)}) %collective-permute-start.9) | collective-permute-done | bytes 114720 | tf_op jit(solution)/shard_map/ppermute | solution.py:367
  169.7 2.0 %collective-permute-start.10 = (f32[224,128]{1,0:T(8,128)S(1)}, f32[224,128]{1,0:T(8,128)S(1)}, u32[]{:S(2)}, u32[]{:S(2)}) collective-permute-start(f32[224,128]{1,0:T(8,128)S(1)} %collective-permute-done.9.got_ref), channel_id=1, source_target_pairs={{0,1},{1,0},{2,3},{3,2},{4,5},{5,4},{6,7},{7,6},{8,9},{9,8},{10,11... | collective-permute-start | bytes 344072 | tf_op jit(solution)/shard_map/ppermute | solution.py:363
  172.9 2.1 %level4.1 = (f32[160,128]{1,0:T(8,128)S(1)}, f32[160,128]{1,0:T(8,128)S(1)}) custom-call(f32[448,128]{1,0:T(8,128)S(1)} %get-tuple-element.26.own_ref, f32[224,128]{1,0:T(8,128)S(1)} %collective-permute-done.9.got_ref, f32[224,128]{1,0:T(8,128)S(1)} %collective-permute-done.10.passed_ref), custom_call_target="tpu_custom_call" | custom-call | tf_op jit(solution)/shard_map/level4/pallas_call | solution.py:234
  175.0 6.5 %collective-permute-start.11 = (f32[160,128]{1,0:T(8,128)S(1)}, f32[160,128]{1,0:T(8,128)S(1)}, u32[]{:S(2)}, u32[]{:S(2)}) collective-permute-start(f32[160,128]{1,0:T(8,128)S(1)} %get-tuple-element.27.own_ref), channel_id=1, source_target_pairs={{0,384},{8,392},{16,400},{24,408},{32,416},{40,424},{48,432},{56,4... | collective-permute-start | bytes 245768 | tf_op jit(solution)/shard_map/ppermute | solution.py:367
  181.6 4.0 %collective-permute-done.11.far_ref = f32[160,128]{1,0:T(8,128)S(1)} collective-permute-done((f32[160,128]{1,0:T(8,128)S(1)}, f32[160,128]{1,0:T(8,128)S(1)}, u32[]{:S(2)}, u32[]{:S(2)}) %collective-permute-start.11) | collective-permute-done | bytes 81952 | tf_op jit(solution)/shard_map/ppermute | solution.py:367
  186.5 2.9 %finish.1 = f32[256,32]{1,0:T(8,128)S(1)} custom-call(f32[160,128]{1,0:T(8,128)S(1)} %get-tuple-element.27.own_ref, f32[160,128]{1,0:T(8,128)S(1)} %collective-permute-done.11.far_ref, f32[256,32]{1,0:T(8,128)S(1)} %get-tuple-element.28.solved_ref, f32[256,768]{1,0:T(8,128)S(1)} %copy-done.3, f32[672,128]{1,0:T(8,128)S(1)} %get-tuple-element.30.refs_0_, ...), custom_call_target="tpu_custom_call" | custom-call | tf_op jit(solution)/shard_map/finish/pallas_call | solution.py:259
  (38 shorter events, 11.0 us)
Async XLA Ops:
  2.3 28.0 %copy-start.1 = (bf16[256,2048]{1,0:T(8,128)(2,1)S(1)}, bf16[256,2048]{1,0:T(8,128)(2,1)}, u32[]{:S(2)}) copy-start(bf16[256,2048]{1,0:T(8,128)(2,1)} %inverse_ref.2) | copy-start | bytes 3145732
  2.3 28.0 %copy-start.6 = (s32[1,2048]{1,0:T(1,128)S(1)}, s32[1,2048]{1,0:T(1,128)}, u32[]{:S(2)}) copy-start(s32[1,2048]{1,0:T(1,128)} %order_ref) | copy-start | bytes 24580
  28.4 5.8 %collective-permute-start = (bf16[4,7,256,128]{3,2,1,0:T(8,128)(2,1)S(1)}, bf16[4,7,256,128]{3,2,1,0:T(8,128)(2,1)}, u32[]{:S(2)}, u32[]{:S(2)}) collective-permute-start(bf16[4,7,256,128]{3,2,1,0:T(8,128)(2,1)S(1)} %all_to_all.25.mine_ref), channel_id=1, source_target_pairs={{0,1},{1,0},{2,3},{3,2},{4,5},{5,4},{6,7},{7,6},{8,9},{9,8},{10,11... | collective-permute-start | bytes 5505032 | tf_op jit(solution)/shard_map/ppermute | solution.py:363
  38.5 1.2 copy-start
  38.5 1.4 copy-start.2
  40.0 4.2 %collective-permute-start.1 = (f32[4,384,128]{2,1,0:T(8,128)S(1)}, f32[4,384,128]{2,1,0:T(8,128)S(1)}, u32[]{:S(2)}, u32[]{:S(2)}) collective-permute-start(f32[4,384,128]{2,1,0:T(8,128)S(1)} %constant_dynamic-slice_fusion.2), channel_id=1, source_target_pairs={{0,1},{1,0},{2,3},{3,2},{4,5},{5,4},{6,7},{7,6},{8,9},{9,8},{10,11... | collective-permute-start | bytes 2359304 | tf_op jit(solution)/shard_map/ppermute | solution.py:363
  72.2 4.9 %collective-permute-start.3 = (f32[8,104,128]{2,1,0:T(8,128)S(1)}, f32[8,104,128]{2,1,0:T(8,128)S(1)}, u32[]{:S(2)}, u32[]{:S(2)}) collective-permute-start(f32[8,104,128]{2,1,0:T(8,128)S(1)} %all_to_all.27.mine_ref), channel_id=1, source_target_pairs={{0,1},{1,0},{2,3},{3,2},{4,5},{5,4},{6,7},{7,6},{8,9},{9,8},{10,11... | collective-permute-start | bytes 1277960 | tf_op jit(solution)/shard_map/ppermute | solution.py:363
  74.2 8.1 %collective-permute-start.2 = (f32[280,128]{1,0:T(8,128)S(1)}, f32[280,128]{1,0:T(8,128)S(1)}, u32[]{:S(2)}, u32[]{:S(2)}) collective-permute-start(f32[280,128]{1,0:T(8,128)S(1)} %slice.16), channel_id=1, source_target_pairs={{0,8},{8,0},{16,24},{24,16},{32,40},{40,32},{48,56},{56,48},{64,72... | collective-permute-start | bytes 430088 | tf_op jit(solution)/shard_map/ppermute | solution.py:367
  95.7 4.7 %collective-permute-start.5 = (f32[8,88,128]{2,1,0:T(8,128)S(1)}, f32[8,88,128]{2,1,0:T(8,128)S(1)}, u32[]{:S(2)}, u32[]{:S(2)}) collective-permute-start(f32[8,88,128]{2,1,0:T(8,128)S(1)} %all_to_all.28.mine_ref), channel_id=1, source_target_pairs={{0,1},{1,0},{2,3},{3,2},{4,5},{5,4},{6,7},{7,6},{8,9},{9,8},{10,11... | collective-permute-start | bytes 1081352 | tf_op jit(solution)/shard_map/ppermute | solution.py:363
  97.7 8.3 %collective-permute-start.4 = (f32[192,128]{1,0:T(8,128)S(1)}, f32[192,128]{1,0:T(8,128)S(1)}, u32[]{:S(2)}, u32[]{:S(2)}) collective-permute-start(f32[192,128]{1,0:T(8,128)S(1)} %slice.18), channel_id=1, source_target_pairs={{0,24},{8,16},{16,8},{24,0},{32,56},{40,48},{48,40},{56,32},{64,88... | collective-permute-start | bytes 294920 | tf_op jit(solution)/shard_map/ppermute | solution.py:367
  122.1 63.5 %copy-start.3 = (f32[256,768]{1,0:T(8,128)S(1)}, f32[256,768]{1,0:T(8,128)}, u32[]{:S(2)}) copy-start(f32[256,768]{1,0:T(8,128)} %copy-done.2) | copy-start | bytes 2359300
  122.1 4.3 %collective-permute-start.6 = (f32[8,192,128]{2,1,0:T(8,128)S(1)}, f32[8,192,128]{2,1,0:T(8,128)S(1)}, u32[]{:S(2)}, u32[]{:S(2)}) collective-permute-start(f32[8,192,128]{2,1,0:T(8,128)S(1)} %all_to_all.29.mine_ref), channel_id=1, source_target_pairs={{0,1},{1,0},{2,3},{3,2},{4,5},{5,4},{6,7},{7,6},{8,9},{9,8},{10,11... | collective-permute-start | bytes 2359304 | tf_op jit(solution)/shard_map/ppermute | solution.py:363
  129.3 15.7 %copy-start.4 = (f32[416,128]{1,0:T(8,128)}, f32[416,128]{1,0:T(8,128)S(1)}, u32[]{:S(2)}) copy-start(f32[416,128]{1,0:T(8,128)S(1)} %get-tuple-element.32.refs_2_) | copy-start | bytes 638980
  129.4 15.6 %collective-permute-start.7 = (f32[432,128]{1,0:T(8,128)S(1)}, f32[432,128]{1,0:T(8,128)S(1)}, u32[]{:S(2)}, u32[]{:S(2)}) collective-permute-start(f32[432,128]{1,0:T(8,128)S(1)} %constant_dynamic-slice_fusion.1), channel_id=1, source_target_pairs={{0,64},{8,72},{16,80},{24,88},{32,96},{40,104},{48,112},{56,120},{... | collective-permute-start | bytes 663560 | tf_op jit(solution)/shard_map/ppermute | solution.py:367
  145.0 3.4 %collective-permute-start.8 = (f32[432,128]{1,0:T(8,128)S(1)}, f32[432,128]{1,0:T(8,128)S(1)}, u32[]{:S(2)}, u32[]{:S(2)}) collective-permute-start(f32[432,128]{1,0:T(8,128)S(1)} %collective-permute-done.7.got_ref), channel_id=1, source_target_pairs={{0,1},{1,0},{2,3},{3,2},{4,5},{5,4},{6,7},{7,6},{8,9},{9,8},{10,11... | collective-permute-start | bytes 663560 | tf_op jit(solution)/shard_map/ppermute | solution.py:363
  150.8 18.9 %collective-permute-start.9 = (f32[224,128]{1,0:T(8,128)S(1)}, f32[224,128]{1,0:T(8,128)S(1)}, u32[]{:S(2)}, u32[]{:S(2)}) collective-permute-start(f32[224,128]{1,0:T(8,128)S(1)} %constant_dynamic-slice_fusion), channel_id=1, source_target_pairs={{0,128},{8,136},{16,144},{24,152},{32,160},{40,168},{48,176},{56,1... | collective-permute-start | bytes 344072 | tf_op jit(solution)/shard_map/ppermute | solution.py:367
  169.7 3.2 %collective-permute-start.10 = (f32[224,128]{1,0:T(8,128)S(1)}, f32[224,128]{1,0:T(8,128)S(1)}, u32[]{:S(2)}, u32[]{:S(2)}) collective-permute-start(f32[224,128]{1,0:T(8,128)S(1)} %collective-permute-done.9.got_ref), channel_id=1, source_target_pairs={{0,1},{1,0},{2,3},{3,2},{4,5},{5,4},{6,7},{7,6},{8,9},{9,8},{10,11... | collective-permute-start | bytes 344072 | tf_op jit(solution)/shard_map/ppermute | solution.py:363
  175.0 10.5 %collective-permute-start.11 = (f32[160,128]{1,0:T(8,128)S(1)}, f32[160,128]{1,0:T(8,128)S(1)}, u32[]{:S(2)}, u32[]{:S(2)}) collective-permute-start(f32[160,128]{1,0:T(8,128)S(1)} %get-tuple-element.27.own_ref), channel_id=1, source_target_pairs={{0,384},{8,392},{16,400},{24,408},{32,416},{40,424},{48,432},{56,4... | collective-permute-start | bytes 245768 | tf_op jit(solution)/shard_map/ppermute | solution.py:367
  185.5 0.9 copy-start.5

commit v3 on v2

--- a/solution.py
+++ b/solution.py
@@ -18,7 +18,7 @@
 PAD = 64
 VMEM_BYTES = 16 * 1024 * 1024
 BOTH = ("leaf", "rows")
-NEAR = (1, 3, 4, 8, 16, 48)
+NEAR = {2: 4, 3: 8, 4: 16, 5: 48}
 
 
 def mm(a, b, precision=TRIPLE):
@@ -33,7 +33,7 @@
     return PAD // MEMBERS + (rank // MEMBERS) * (tiers - height)
 
 
-def inverses(pairs):
+def solve(pairs, targets):
     rank = pairs[0][0].shape[0]
     eye = (
         lax.broadcasted_iota(jnp.int32, (rank, rank), 0) == lax.broadcasted_iota(jnp.int32, (rank, rank), 1)
@@ -47,8 +47,10 @@
     gaps = [eye - mm(system, guess) for system, guess in zip(systems, guesses)]
     size = functools.reduce(jnp.maximum, [jnp.sum(gap * gap) for gap in gaps])
 
+    firsts = [mm(target, guess) for target, guess in zip(targets, guesses)]
+
     def close():
-        return [guess + mm(guess, gap) for guess, gap in zip(guesses, gaps)]
+        return [first + mm(first, gap) for first, gap in zip(firsts, gaps)]
 
     def refine(left, right, guess):
         system = eye - mm(left, right, FULL)
@@ -73,7 +75,8 @@
         return lax.while_loop(more, step, (0, jnp.float32(jnp.inf)) + first)[2]
 
     def far_off():
-        return [refine(left, right, guess) for (left, right), guess in zip(pairs, guesses)]
+        found = [refine(left, right, guess) for (left, right), guess in zip(pairs, guesses)]
+        return [mm(target, inverse, FULL) for target, inverse in zip(targets, found)]
 
     return lax.cond(size < 1e-6, close, far_off)
 
@@ -92,24 +95,22 @@
 
 def couple(children, width, rank):
     blocks = [(s[width : width + rank], t[width : width + rank]) for s, t in children]
-    found = []
-    for (s, t), (s_a, t_a), inverse in zip(children, blocks, inverses(blocks)):
-        s_r, t_r = without(s, width, rank), without(t, width, rank)
-        s_c = mm(t_r - mm(s_r, t_a), inverse)
-        found.append((s_c, s_r - mm(s_c, s_a)))
-    return found
+    rests = [(without(s, width, rank), without(t, width, rank)) for s, t in children]
+    targets = [t_r - mm(s_r, t_a) for (s_r, t_r), (_, t_a) in zip(rests, blocks)]
+    found = solve(blocks, targets)
+    return [(s_c, s_r - mm(s_c, s_a)) for s_c, (s_r, _), (s_a, _) in zip(found, rests, blocks)]
 
 
 def images_of(s, t, width, rank):
     return jnp.concatenate([s[width + rank :], t[width + rank :]], axis=1)
 
 
-def gathered(first, second, place, rank):
+def gathered(halves, node, place, rank):
     low, each = PAD // MEMBERS, rank // MEMBERS
+    chips = slice(CHIPS * node, CHIPS * (node + 1))
 
     def joined(start, rows):
-        halves = [half[:, start : start + rows] for half in (first, second)]
-        return jnp.concatenate([half.reshape(half.shape[0] * rows, rank) for half in halves], axis=0)
+        return jnp.concatenate([half[chips, start : start + rows, :].reshape(CHIPS * rows, rank) for half in halves], axis=0)
 
     def section(width, blocks):
         parts = [joined(place, low)[:width]]
@@ -119,58 +120,94 @@
     return section
 
 
-def share_level_kernel(height, tiers, rank, width, mine_ref, theirs_ref, coeff_ref, change_ref, wide_ref):
-    rest = tiers - height - 1
-    core, member, bit = position(height)
-    mine, theirs = mine_ref[...], theirs_ref[...]
-    first = jnp.where(core == 0, mine, theirs)
-    second = jnp.where(core == 0, theirs, mine)
-    s, t = [
-        gathered(first[CHIPS * k : CHIPS * (k + 1)], second[CHIPS * k : CHIPS * (k + 1)], 0, rank)(width, rest + 1)
-        for k in range(2)
-    ]
-    ((s_c, t_c),) = couple([(s, t)], width, rank)
-    coeff_ref[...] = jnp.where(bit == 0, s_c, t_c)
-    both = jnp.concatenate([s_c, t_c], axis=1)
+def by_core(core, mine_ref, theirs_ref, body):
+    @pl.when(core == 0)
+    def _():
+        body((mine_ref, theirs_ref))
+
+    @pl.when(core != 0)
+    def _():
+        body((theirs_ref, mine_ref))
+
+
+def vmem(count):
+    return [pl.BlockSpec(memory_space=pltpu.VMEM)] * count
+
+
+def params():
+    return pltpu.CompilerParams(vmem_limit_bytes=VMEM_BYTES)
+
+
+def own_rows(both, member, wide_ref, width, rank):
+    rest = (both.shape[0] - width) // rank
+    low, each = PAD // MEMBERS, rank // MEMBERS
     wide_ref[0:width, :] = both[:width]
     wide_ref[width:PAD, :] = jnp.zeros((PAD - width, 2 * rank), F32)
     wide_ref[PAD : PAD + rank * rest, :] = both[width:]
-    low, each = PAD // MEMBERS, rank // MEMBERS
     slices = [wide_ref[pl.ds(pl.multiple_of(member * low, low), low), :]]
     for k in range(rest):
         slices.append(wide_ref[pl.ds(pl.multiple_of(PAD + rank * k + member * each, each), each), :])
-    change = mm_nt(jnp.concatenate(slices, axis=0), images_of(s, t, width, rank))
-    place = 0
-    for g in range(rest):
-        columns = slice(rank * g, rank * (g + 1))
-        part = jnp.concatenate([change[:low, columns], change[low + each * g :, columns]], axis=0)
-        rows = low + each * (rest - g)
-        change_ref[place : place + rows, :] = part
-        place += rows
-
-
-def vmem(count):
-    return [pl.BlockSpec(memory_space=pltpu.VMEM)] * count
-
-
-def params():
-    return pltpu.CompilerParams(vmem_limit_bytes=VMEM_BYTES)
-
-
-def share_level(height, tiers, rank, width, mine, theirs):
-    rest = tiers - height - 1
-    rows = sum(share_rows(h, tiers, rank) for h in range(height + 1, tiers))
-    return pl.pallas_call(
-        functools.partial(share_level_kernel, height, tiers, rank, width),
+    return jnp.concatenate(slices, axis=0)
+
+
+def share_change(rows, images, skip, rank):
+    low, each = PAD // MEMBERS, rank // MEMBERS
+    parts = []
+    for g in range(skip, images.shape[0] // rank):
+        chosen = jnp.concatenate([rows[:low], rows[low + each * g :]], axis=0)
+        parts.append(mm_nt(chosen, images[rank * g : rank * (g + 1)]))
+    return jnp.concatenate(parts, axis=0)
+
+
+def four_leaves_kernel(tiers, rank, width, mine_ref, theirs_ref, low_ref, high_ref, change_ref, *wide_refs):
+    by_core(
+        position(0)[0],
+        mine_ref,
+        theirs_ref,
+        functools.partial(join_four, tiers, rank, width, low_ref, high_ref, change_ref, wide_refs),
+    )
+
+
+def join_four(tiers, rank, width, low_ref, high_ref, change_ref, wide_refs, halves):
+    _, member, odd = position(0)
+    upper = position(1)[2]
+    place = share_rows(0, tiers, rank)
+    nodes = [
+        (gathered(halves, k, 0, rank)(width, tiers), gathered(halves, k, place, rank)(width, tiers - 1))
+        for k in range(4)
+    ]
+    pairs = [(nodes[0], nodes[1]), (nodes[2], nodes[3])]
+    found = couple([(s[0], t[0]) for s, t in pairs], width, rank)
+    picked = [jnp.where(odd == 0, s_c, t_c) for s_c, t_c in found]
+    low_ref[...] = jnp.where(upper == 0, picked[0], picked[1])
+    change, joined = None, []
+    for (s_c, t_c), (s, t), wide_ref in zip(found, pairs, wide_refs):
+        both = jnp.concatenate([s_c, t_c], axis=1)
+        images = images_of(s[0], t[0], width, rank)
+        joined.append(s[1] + t[1] - mm_nt(both, images[:rank]))
+        term = share_change(own_rows(both, member, wide_ref, width, rank), images, 1, rank)
+        change = term if change is None else change + term
+    ((s_c, t_c),) = couple([tuple(joined)], width, rank)
+    high_ref[...] = jnp.where(upper == 0, s_c, t_c)
+    both = jnp.concatenate([s_c, t_c], axis=1)
+    rows = own_rows(both, member, wide_refs[2], width, rank)
+    change_ref[...] = change + share_change(rows, images_of(*joined, width, rank), 0, rank)
+
+
+def four_leaves(tiers, rank, width, mine, theirs):
+    rows = sum(share_rows(h, tiers, rank) for h in range(2, tiers))
+    return pl.pallas_call(
+        functools.partial(four_leaves_kernel, tiers, rank, width),
         out_shape=[
-            jax.ShapeDtypeStruct((width + rank * rest, rank), F32),
+            jax.ShapeDtypeStruct((width + rank * (tiers - 1), rank), F32),
+            jax.ShapeDtypeStruct((width + rank * (tiers - 2), rank), F32),
             jax.ShapeDtypeStruct((rows, rank), F32),
         ],
         in_specs=vmem(2),
-        out_specs=vmem(2),
-        scratch_shapes=[pltpu.VMEM((PAD + rank * rest, 2 * rank), F32)],
-        compiler_params=params(),
-        name=f"level{height}",
+        out_specs=vmem(3),
+        scratch_shapes=[pltpu.VMEM((PAD + rank * (tiers - k), 2 * rank), F32) for k in (1, 1, 2)],
+        compiler_params=params(),
+        name="level0",
     )(mine, theirs)
 
 
@@ -188,18 +225,18 @@
 
 def first_pair_kernel(height, tiers, rank, width, mine_ref, theirs_ref, coeff_ref, next_ref):
     core, _, bit = position(height)
-    mine, theirs = mine_ref[...], theirs_ref[...]
-    first = jnp.where(core == 0, mine, theirs)
-    second = jnp.where(core == 0, theirs, mine)
-    nodes = []
-    for k in range(2):
-        span = slice(CHIPS * k, CHIPS * (k + 1))
-        place, sections = 0, []
-        for h in range(height, tiers):
-            sections.append(gathered(first[span], second[span], place, rank)(width, tiers - h))
-            place += share_rows(h, tiers, rank)
-        nodes.append(sections)
-    join_pair(bit, nodes[0], nodes[1], width, rank, coeff_ref, next_ref)
+
+    def body(halves):
+        nodes = []
+        for k in range(2):
+            place, sections = 0, []
+            for h in range(height, tiers):
+                sections.append(gathered(halves, k, place, rank)(width, tiers - h))
+                place += share_rows(h, tiers, rank)
+            nodes.append(sections)
+        join_pair(bit, nodes[0], nodes[1], width, rank, coeff_ref, next_ref)
+
+    by_core(core, mine_ref, theirs_ref, body)
 
 
 def join_pair(bit, s, t, width, rank, coeff_ref, next_ref):
@@ -252,7 +289,7 @@
     for h in reversed(range(tiers - 1)):
         above = jnp.concatenate(found[h + 1 :], axis=1)
         found[h] = coeff_refs[h][0:width, :] - mm(above, coeff_refs[h][width:, :])
-    out_ref[...] = solved_ref[...] - mm_nt(images_ref[...], jnp.concatenate(found, axis=1))
+    out_ref[...] = solved_ref[...] - mm_nt(images_ref[...], jnp.concatenate(found, axis=1)).T
 
 
 def finish(tiers, rank, width, own, far, solved, images, coeffs):
@@ -264,6 +301,30 @@
         compiler_params=params(),
         name="finish",
     )(own, far, solved, images, *coeffs)
+
+
+def pack_kernel(bases_ref, given_ref, out_ref):
+    tiers, rows, rank = bases_ref.shape
+    width = given_ref.shape[0]
+    for copy in range(CHIPS):
+        for h in range(tiers):
+            out_ref[copy, rows * h : rows * (h + 1), :] = bases_ref[h]
+        for k in range(rows // rank):
+            place = rows * tiers + width * k
+            out_ref[copy, place : place + width, :] = given_ref[:, rank * k : rank * (k + 1)]
+
+
+def pack(bases, given):
+    tiers, rows, rank = bases.shape
+    total = tiers * rows + given.size // rank
+    return pl.pallas_call(
+        pack_kernel,
+        out_shape=jax.ShapeDtypeStruct((CHIPS, total, rank), bases.dtype),
+        in_specs=vmem(2),
+        out_specs=pl.BlockSpec(memory_space=pltpu.VMEM),
+        compiler_params=params(),
+        name="pack",
+    )(bases, given)
 
 
 def reorder_kernel(order_ref, inverse_ref, out_ref):
@@ -293,50 +354,50 @@
 
 
 def leaf_kernel(
-    tiers, rank, width, inverse_ref, moved_ref, mine_ref, theirs_ref, own_ref, solved_ref, images_ref, gram_ref, images_vmem, sem
+    tiers, rank, width, inverse_ref, moved_ref, mine_ref, theirs_ref, own_ref, solved_ref, images_ref, keep_ref, give_ref, images_vmem, sem
 ):
-    rows = own_ref.shape[1]
+    rows = inverse_ref.shape[0]
     core = lax.axis_index("rows") % CORES
     images, solved = None, None
     for chip in range(CHIPS):
         for ref, side in ((mine_ref, core), (theirs_ref, 1 - core)):
             columns = pl.ds(pl.multiple_of((CORES * chip + side) * rows, rows), rows)
-            wide = jnp.concatenate([ref[chip, h] for h in range(tiers)], axis=1)
+            wide = jnp.concatenate([ref[chip, rows * h : rows * (h + 1)] for h in range(tiers)], axis=1)
             term = mm(inverse_ref[:, columns], wide, None)
             images = term if images is None else images + term
-            term = mm(moved_ref[:, columns], ref[chip, tiers][:, :width], None)
+            given = ref[chip, rows * tiers :]
+            given = jnp.concatenate([given[width * k : width * (k + 1)] for k in range(rows // rank)], axis=1)
+            term = mm_nt(given, moved_ref[:, columns], None)
             solved = term if solved is None else solved + term
     solved_ref[...] = solved
     images_vmem[...] = images
     copy = pltpu.make_async_copy(images_vmem, images_ref, sem)
     copy.start()
-    live = jnp.concatenate([images, solved], axis=1)
-    high = live.astype(BF16)
-    left = live - high.astype(F32)
-    middle = left.astype(BF16)
-    low = (left - middle.astype(F32)).astype(BF16)
-
-    def project(first, last, basis):
-        total = None
-        for piece in (high, middle, low):
-            term = lax.dot_general(
-                piece[:, first:last], basis, (((0,), (0,)), ((), ())), preferred_element_type=F32
-            )
-            total = term if total is None else total + term
-        return total
-
+
+    def pieces(value):
+        high = value.astype(BF16)
+        return high, (value - high.astype(F32)).astype(BF16)
+
+    own = [own_ref[0, rows * h : rows * (h + 1)] for h in range(tiers)]
+    flipped = jnp.concatenate(own, axis=1).T
+    solved_high, solved_low = pieces(solved)
     few, each = PAD // MEMBERS, rank // MEMBERS
+
+    def put(block, place, size):
+        block = block.reshape(MEMBERS, size, rank)
+        first, second = block[:CHIPS], block[CHIPS:]
+        keep_ref[:, place : place + size, :] = jnp.where(core == 0, first, second)
+        give_ref[:, place : place + size, :] = jnp.where(core == 0, second, first)
+
     place = 0
     for h in range(tiers):
-        basis = own_ref[h]
-        top = project(rank * tiers, rank * tiers + width, basis)
-        top = jnp.concatenate([top, jnp.zeros((PAD - width, rank), F32)], axis=0)
-        gram_ref[:, place : place + few, :] = top.reshape(MEMBERS, few, rank)
+        top = mm(solved_high, own[h], None) + mm(solved_low, own[h], None)
+        put(jnp.concatenate([top, jnp.zeros((PAD - width, rank), F32)], axis=0), place, few)
         place += few
-        body = project(rank * h, rank * tiers, basis)
+        high, low = pieces(images[:, rank * h : rank * (h + 1)])
+        body = mm(flipped[rank * h :], high, None) + mm(flipped[rank * h :], low, None)
         for k in range(tiers - h):
-            block = body[rank * k : rank * (k + 1)]
-            gram_ref[:, place : place + each, :] = block.reshape(MEMBERS, each, rank)
+            put(body[rank * k : rank * (k + 1)], place, each)
             place += each
     copy.wait()
 
@@ -347,12 +408,13 @@
     return pl.pallas_call(
         functools.partial(leaf_kernel, tiers, rank, width),
         out_shape=[
-            jax.ShapeDtypeStruct((rows, width), F32),
+            jax.ShapeDtypeStruct((width, rows), F32),
             jax.ShapeDtypeStruct((rows, tiers * rank), F32),
-            jax.ShapeDtypeStruct((MEMBERS, share, rank), F32),
+            jax.ShapeDtypeStruct((CHIPS, share, rank), F32),
+            jax.ShapeDtypeStruct((CHIPS, share, rank), F32),
         ],
         in_specs=vmem(5),
-        out_specs=vmem(1) + [pl.BlockSpec(memory_space=pl.ANY)] + vmem(1),
+        out_specs=vmem(1) + [pl.BlockSpec(memory_space=pl.ANY)] + vmem(2),
         scratch_shapes=[pltpu.VMEM((rows, tiers * rank), F32), pltpu.SemaphoreType.DMA],
         compiler_params=params(),
         name="leaf",
@@ -386,39 +448,33 @@
 def local(right_side, point_order, leaf_inverse, bases):
     tiers, rank, width = bases.shape[1], bases.shape[2], right_side.shape[1]
     leaves = range(lax.axis_size("leaf"))
-    own = jnp.concatenate(
-        [jnp.swapaxes(bases, 0, 1), jnp.pad(right_side, ((0, 0), (0, rank - width)))[None]], axis=0
-    )
+    rows = bases.shape[0]
+    packed = pack(jnp.swapaxes(bases, 0, 1), right_side.T)
     groups = [[c + CORES * y for y in range(CHIPS)] for c in range(CORES)]
-    mine = lax.all_to_all(jnp.broadcast_to(own[None], (CHIPS,) + own.shape), "rows", 0, 0, axis_index_groups=groups)
+    mine = lax.all_to_all(packed, "rows", 0, 0, axis_index_groups=groups)
     theirs = swap_cores(mine)
     order, inverse, _ = lax.optimization_barrier((point_order, leaf_inverse, mine))
     moved = reorder(order, inverse)
-    solved, images, gram = leaf_step(tiers, rank, width, leaf_inverse, moved, mine, theirs, own)
-
-    core = lax.axis_index("rows") % CORES
-
-    keep = lax.dynamic_slice_in_dim(gram, core * CHIPS, CHIPS)
-    give = lax.dynamic_slice_in_dim(gram, (1 - core) * CHIPS, CHIPS)
+    solved, images, keep, give = leaf_step(tiers, rank, width, leaf_inverse, moved, mine, theirs, packed)
+
     parts = keep + swap_cores(give)
     share = lax.all_to_all(parts, "rows", 0, 0, axis_index_groups=groups).sum(axis=0)
 
-    coeffs = []
-    for height in range(2):
-        cut = share_rows(height, tiers, rank)
-        section, own = share[:cut], share[cut:]
-        far = swap_leaves(own, NEAR[height])
-        sets = [(i, i ^ NEAR[height]) for i in leaves if not (i >> height) & 1]
-        mine = spread(section, sets)
-        theirs = swap_cores(mine)
-        coeff, change = share_level(height, tiers, rank, width, mine, theirs)
-        share = own + far - change
-        coeffs.append(coeff)
+    cut = share_rows(0, tiers, rank) + share_rows(1, tiers, rank)
+    tail = share[cut:]
+    mine = spread(share[:cut], [tuple(range(i, i + 4)) for i in leaves if i % 4 == 0])
+    theirs = swap_cores(mine)
+    tail = tail + swap_leaves(tail, 1)
+    tail = tail + swap_leaves(tail, 3)
+    low, high, change = four_leaves(tiers, rank, width, mine, theirs)
+    share = tail - change
+    coeffs = [low, high]
 
     mine = spread(share, [(i, i ^ NEAR[2]) for i in leaves if not (i >> 2) & 1])
     theirs = swap_cores(mine)
     coeff, own = pair_level(first_pair_kernel, 2, tiers, rank, width, mine, theirs)
     coeffs.append(coeff)
+    core = lax.axis_index("rows") % CORES
     for height in range(3, tiers - 1):
         half = own.shape[0] // CORES
         got = swap_leaves(lax.dynamic_slice_in_dim(own, core * half, half), NEAR[height])
@@ -426,7 +482,7 @@
         coeff, own = pair_level(pair_kernel, height, tiers, rank, width, own, got, passed)
         coeffs.append(coeff)
     far = swap_leaves(own, NEAR[5])
-    return finish(tiers, rank, width, own, far, solved, images, coeffs)
+    return finish(tiers, rank, width, own, far, solved, images, coeffs).T
 
 
 def solution(mesh):

time: 194 us -> 183 us (0.943)
  local copies, waits for them, and re-layouts: 4.5 us -> 1.98 us
  other arithmetic: 2.36 us -> 0.15 us
  waiting for transfers between devices: 37.8 us -> 35.6 us
    all_to_all x1, blocking collectives: 26.1 us -> 24 us  [local(): mine = lax.all_to_all(packed, 'rows', 0, 0, axis_index_groups=groups)]
    ppermute x7 -> x6, starting transfers between devices: 13.7 us -> 11.6 us  [swap_cores(): return lax.ppermute(value, 'rows', [(i, i ^ 1) for i in range(MEMBERS)])]
    ppermute x5, waiting for transfers between devices: 29.2 us -> 27.2 us  [swap_leaves(): lax.ppermute(value, 'leaf', [(i, i ^ mask) for i in range(lax.axis_size('...]
    all_to_all x3 -> x2, blocking collectives: 41 us -> 42.1 us  [spread(): lax.all_to_all(jnp.broadcast_to(value[None], (count,) + value.shape), BOT...]
    ppermute x7 -> x6, waiting for transfers between devices: 8.53 us -> 8.39 us  [swap_cores(): return lax.ppermute(value, 'rows', [(i, i ^ 1) for i in range(MEMBERS)])]
  transfers between devices with their start and end apart: 12 -> 11, of which waited for: 10 -> 10; matrix products, arithmetic and copies ran while one was open for 0% -> 0% of each run, Pallas kernels for 4% -> 5%
where the time goes in v3:
time: 183 us; the launch traced here: 180 us
  blocking collectives  81.4 us (44%)
  starting transfers between devices  39 us (21%)
  waiting for transfers between devices  35.6 us (19%)
  Pallas kernels  21.6 us (12%)
  local copies, waits for them, and re-layouts  1.98 us (1%)
    all_to_all x2, blocking collectives, spread(): lax.all_to_all(jnp.broadcast_to(value[None], (count,) + value.shape), BOT...  42.1 us
    ppermute x5, starting transfers between devices, swap_leaves(): lax.ppermute(value, 'leaf', [(i, i ^ mask) for i in range(lax.axis_size('...  27.3 us
    ppermute x5, waiting for transfers between devices, swap_leaves(): lax.ppermute(value, 'leaf', [(i, i ^ mask) for i in range(lax.axis_size('...  27.2 us
    all_to_all x1, blocking collectives, local(): mine = lax.all_to_all(packed, 'rows', 0, 0, axis_index_groups=groups)  24 us
    all_to_all x1, blocking collectives, local(): lax.all_to_all(parts, 'rows', 0, 0, axis_index_groups=groups).sum(axis=0)  15.3 us
    ppermute x6, starting transfers between devices, swap_cores(): return lax.ppermute(value, 'rows', [(i, i ^ 1) for i in range(MEMBERS)])  11.6 us
    ppermute x6, waiting for transfers between devices, swap_cores(): return lax.ppermute(value, 'rows', [(i, i ^ 1) for i in range(MEMBERS)])  8.39 us
    pallas_call x1, Pallas kernels, four_leaves(): pl.pallas_call(functools.partial(four_leaves_kernel, tiers, rank, width),...  6.68 us
  transfers between devices with their start and end apart: 11, of which 10 were waited for; matrix products, arithmetic and copies ran while one was open for 0% of the time, Pallas kernels for 5%

profile of v3, /device:TPU:24, one launch (start us, length us, event | category | flops | bytes accessed | tf_op | source)
XLA Modules:
  0.0 180.0 jit_solution(81655773095049707)
XLA Ops:
  0.0 1.0 copy-done.1
  2.0 24.0 %all_to_all.20.mine_ref = bf16[4,1600,128]{2,1,0:T(8,128)(2,1)S(1)} all-to-all(bf16[4,1600,128]{2,1,0:T(8,128)(2,1)S(1)} %pack.1.own_ref), channel_id=1, replica_groups={{0,2,4,6},{1,3,5,7},{8,10,12,14},{9,11,13,15},{16,18,20,22},{17,19,21,2..., dimensions={0} | all-to-all | bytes 3276800 | tf_op jit(solution)/shard_map/all_to_all | solution.py:454
  25.9 1.9 %collective-permute-start = (bf16[4,1600,128]{2,1,0:T(8,128)(2,1)S(1)}, bf16[4,1600,128]{2,1,0:T(8,128)(2,1)S(1)}, u32[]{:S(2)}, u32[]{:S(2)}) collective-permute-start(bf16[4,1600,128]{2,1,0:T(8,128)(2,1)S(1)} %all_to_all.20.mine_ref), channel_id=1, source_target_pairs={{0,1},{1,0},{2,3},{3,2},{4,5},{5,4},{6,7},{7,6},{8,9},{9,8},{10,11... | collective-permute-start | bytes 4915208 | tf_op jit(solution)/shard_map/ppermute | solution.py:425
  27.9 2.4 %reorder.1.moved_ref = bf16[256,2048]{1,0:T(8,128)(2,1)S(1)} custom-call(s32[1,2048]{1,0:T(1,128)S(1)} %copy-done.5, bf16[256,2048]{1,0:T(8,128)(2,1)S(1)} %copy-done), custom_call_target="tpu_custom_call" | custom-call | flops 2147483648 | bytes 2097152 | tf_op jit(solution)/shard_map/reorder/pallas_call | solution.py:343
  30.2 1.1 collective-permute-done.theirs_ref
  31.3 2.5 %leaf.1 = (f32[32,256]{1,0:T(8,128)S(1)}, f32[256,768]{1,0:T(8,128)S(1)}, f32[4,384,128]{2,1,0:T(8,128)S(1)}, f32[4,384,128]{2,1,0:T(8,128)S(1)}) custom-call(bf16[256,2048]{1,0:T(8,128)(2,1)S(1)} %copy-done, bf16[256,2048]{1,0:T(8,128)(2,1)S(1)} %reorder.1.moved_ref, bf16[4,1600,128]{2,1,0:T(8,128)(2,1)S(1)} %all_to_all.20.mine_ref, ...), custom_call_target="tpu_custom_call" | custom-call | tf_op jit(solution)/shard_map/leaf/pallas_call | solution.py:408
  33.8 2.0 %collective-permute-start.1 = (f32[4,384,128]{2,1,0:T(8,128)S(1)}, f32[4,384,128]{2,1,0:T(8,128)S(1)}, u32[]{:S(2)}, u32[]{:S(2)}) collective-permute-start(f32[4,384,128]{2,1,0:T(8,128)S(1)} %get-tuple-element.23), channel_id=1, source_target_pairs={{0,1},{1,0},{2,3},{3,2},{4,5},{5,4},{6,7},{7,6},{8,9},{9,8},{10,11... | collective-permute-start | bytes 2359304 | tf_op jit(solution)/shard_map/ppermute | solution.py:425
  35.9 2.1 %collective-permute-done.1 = f32[4,384,128]{2,1,0:T(8,128)S(1)} collective-permute-done((f32[4,384,128]{2,1,0:T(8,128)S(1)}, f32[4,384,128]{2,1,0:T(8,128)S(1)}, u32[]{:S(2)}, u32[]{:S(2)}) %collective-permute-start.1) | collective-permute-done | bytes 786464 | tf_op jit(solution)/shard_map/ppermute | solution.py:425
  38.1 15.3 %all_to_all.21 = f32[4,384,128]{2,1,0:T(8,128)S(1)} all-to-all(f32[4,384,128]{2,1,0:T(8,128)S(1)} %add.19), channel_id=1, replica_groups={{0,2,4,6},{1,3,5,7},{8,10,12,14},{9,11,13,15},{16,18,20,22},{17,19,21,2..., dimensions={0} | all-to-all | bytes 1572864 | tf_op jit(solution)/shard_map/all_to_all | solution.py:461
  53.4 3.4 %collective-permute-start.2 = (f32[192,128]{1,0:T(8,128)S(1)}, f32[192,128]{1,0:T(8,128)S(1)}, u32[]{:S(2)}, u32[]{:S(2)}) collective-permute-start(f32[192,128]{1,0:T(8,128)S(1)} %slice.8), channel_id=1, source_target_pairs={{0,8},{8,0},{16,24},{24,16},{32,40},{40,32},{48,56},{56,48},{64,72... | collective-permute-start | bytes 294920 | tf_op jit(solution)/shard_map/ppermute | solution.py:429
  56.8 3.1 %collective-permute-done.2 = f32[192,128]{1,0:T(8,128)S(1)} collective-permute-done((f32[192,128]{1,0:T(8,128)S(1)}, f32[192,128]{1,0:T(8,128)S(1)}, u32[]{:S(2)}, u32[]{:S(2)}) %collective-permute-start.2) | collective-permute-done | bytes 98336 | tf_op jit(solution)/shard_map/ppermute | solution.py:429
  60.1 25.2 %all_to_all.22.mine_ref = f32[16,192,128]{2,1,0:T(8,128)S(1)} all-to-all(f32[16,192,128]{2,1,0:T(8,128)S(1)} %broadcast_in_dim.4), channel_id=1, replica_groups={{0,2,4,6,8,10,12,14,16,18,20,22,24,26,28,30},{1,3,5,7,9,11,13,15,17,19,..., dimensions={0} | all-to-all | bytes 3145728 | tf_op jit(solution)/shard_map/all_to_all | solution.py:443
  85.4 1.9 %collective-permute-start.4 = (f32[16,192,128]{2,1,0:T(8,128)S(1)}, f32[16,192,128]{2,1,0:T(8,128)S(1)}, u32[]{:S(2)}, u32[]{:S(2)}) collective-permute-start(f32[16,192,128]{2,1,0:T(8,128)S(1)} %all_to_all.22.mine_ref), channel_id=1, source_target_pairs={{0,1},{1,0},{2,3},{3,2},{4,5},{5,4},{6,7},{7,6},{8,9},{9,8},{10,11... | collective-permute-start | bytes 4718600 | tf_op jit(solution)/shard_map/ppermute | solution.py:425
  87.3 3.1 %collective-permute-start.3 = (f32[192,128]{1,0:T(8,128)S(1)}, f32[192,128]{1,0:T(8,128)S(1)}, u32[]{:S(2)}, u32[]{:S(2)}) collective-permute-start(f32[192,128]{1,0:T(8,128)S(1)} %get-tuple-element.35), channel_id=1, source_target_pairs={{0,24},{8,16},{16,8},{24,0},{32,56},{40,48},{48,40},{56,32},{64,88... | collective-permute-start | bytes 294920 | tf_op jit(solution)/shard_map/ppermute | solution.py:429
  90.7 6.7 %level0.1 = (f32[672,128]{1,0:T(8,128)S(1)}, f32[544,128]{1,0:T(8,128)S(1)}, f32[192,128]{1,0:T(8,128)S(1)}) custom-call(f32[16,192,128]{2,1,0:T(8,128)S(1)} %all_to_all.22.mine_ref, f32[16,192,128]{2,1,0:T(8,128)S(1)} %collective-permute-done.4.theirs_ref), custom_call_target="tpu_custom_call" | custom-call | tf_op jit(solution)/shard_map/level0/pallas_call | solution.py:199
  97.4 16.9 %all_to_all.23.mine_ref = f32[8,192,128]{2,1,0:T(8,128)S(1)} all-to-all(f32[8,192,128]{2,1,0:T(8,128)S(1)} %broadcast_in_dim.5), channel_id=1, replica_groups={{0,2,4,6,32,34,36,38},{1,3,5,7,33,35,37,39},{8,10,12,14,40,42,44,46},{9..., dimensions={0} | all-to-all | bytes 1572864 | tf_op jit(solution)/shard_map/all_to_all | solution.py:443
  114.3 1.9 %collective-permute-start.5 = (f32[8,192,128]{2,1,0:T(8,128)S(1)}, f32[8,192,128]{2,1,0:T(8,128)S(1)}, u32[]{:S(2)}, u32[]{:S(2)}) collective-permute-start(f32[8,192,128]{2,1,0:T(8,128)S(1)} %all_to_all.23.mine_ref), channel_id=1, source_target_pairs={{0,1},{1,0},{2,3},{3,2},{4,5},{5,4},{6,7},{7,6},{8,9},{9,8},{10,11... | collective-permute-start | bytes 2359304 | tf_op jit(solution)/shard_map/ppermute | solution.py:425
  116.3 2.2 %collective-permute-done.5.theirs_ref = f32[8,192,128]{2,1,0:T(8,128)S(1)} collective-permute-done((f32[8,192,128]{2,1,0:T(8,128)S(1)}, f32[8,192,128]{2,1,0:T(8,128)S(1)}, u32[]{:S(2)}, u32[]{:S(2)}) %collective-permute-start.5) | collective-permute-done | bytes 786464 | tf_op jit(solution)/shard_map/ppermute | solution.py:425
  118.5 2.6 %level2.1 = (f32[416,128]{1,0:T(8,128)S(1)}, f32[864,128]{1,0:T(8,128)S(1)}) custom-call(f32[8,192,128]{2,1,0:T(8,128)S(1)} %all_to_all.23.mine_ref, f32[8,192,128]{2,1,0:T(8,128)S(1)} %collective-permute-done.5.theirs_ref), custom_call_target="tpu_custom_call" | custom-call | tf_op jit(solution)/shard_map/level2/pallas_call | solution.py:271
  121.2 5.2 %collective-permute-start.6 = (f32[432,128]{1,0:T(8,128)S(1)}, f32[432,128]{1,0:T(8,128)S(1)}, u32[]{:S(2)}, u32[]{:S(2)}) collective-permute-start(f32[432,128]{1,0:T(8,128)S(1)} %constant_dynamic-slice_fusion.1), channel_id=1, source_target_pairs={{0,64},{8,72},{16,80},{24,88},{32,96},{40,104},{48,112},{56,120},{... | collective-permute-start | bytes 663560 | tf_op jit(solution)/shard_map/ppermute | solution.py:429
  126.4 10.4 %collective-permute-done.6.got_ref = f32[432,128]{1,0:T(8,128)S(1)} collective-permute-done((f32[432,128]{1,0:T(8,128)S(1)}, f32[432,128]{1,0:T(8,128)S(1)}, u32[]{:S(2)}, u32[]{:S(2)}) %collective-permute-start.6) | collective-permute-done | bytes 221216 | tf_op jit(solution)/shard_map/ppermute | solution.py:429
  136.8 1.9 %collective-permute-start.7 = (f32[432,128]{1,0:T(8,128)S(1)}, f32[432,128]{1,0:T(8,128)S(1)}, u32[]{:S(2)}, u32[]{:S(2)}) collective-permute-start(f32[432,128]{1,0:T(8,128)S(1)} %collective-permute-done.6.got_ref), channel_id=1, source_target_pairs={{0,1},{1,0},{2,3},{3,2},{4,5},{5,4},{6,7},{7,6},{8,9},{9,8},{10,11... | collective-permute-start | bytes 663560 | tf_op jit(solution)/shard_map/ppermute | solution.py:425
  138.8 1.4 collective-permute-done.7.passed_ref
  140.2 2.0 %level3.1 = (f32[288,128]{1,0:T(8,128)S(1)}, f32[448,128]{1,0:T(8,128)S(1)}) custom-call(f32[864,128]{1,0:T(8,128)S(1)} %get-tuple-element.25.own_ref, f32[432,128]{1,0:T(8,128)S(1)} %collective-permute-done.6.got_ref, f32[432,128]{1,0:T(8,128)S(1)} %collective-permute-done.7.passed_ref), custom_call_target="tpu_custom_call" | custom-call | tf_op jit(solution)/shard_map/level3/pallas_call | solution.py:271
  142.2 9.1 %collective-permute-start.8 = (f32[224,128]{1,0:T(8,128)S(1)}, f32[224,128]{1,0:T(8,128)S(1)}, u32[]{:S(2)}, u32[]{:S(2)}) collective-permute-start(f32[224,128]{1,0:T(8,128)S(1)} %constant_dynamic-slice_fusion), channel_id=1, source_target_pairs={{0,128},{8,136},{16,144},{24,152},{32,160},{40,168},{48,176},{56,1... | collective-permute-start | bytes 344072 | tf_op jit(solution)/shard_map/ppermute | solution.py:429
  151.3 9.8 %collective-permute-done.8.got_ref = f32[224,128]{1,0:T(8,128)S(1)} collective-permute-done((f32[224,128]{1,0:T(8,128)S(1)}, f32[224,128]{1,0:T(8,128)S(1)}, u32[]{:S(2)}, u32[]{:S(2)}) %collective-permute-start.8) | collective-permute-done | bytes 114720 | tf_op jit(solution)/shard_map/ppermute | solution.py:429
  161.1 2.0 %collective-permute-start.9 = (f32[224,128]{1,0:T(8,128)S(1)}, f32[224,128]{1,0:T(8,128)S(1)}, u32[]{:S(2)}, u32[]{:S(2)}) collective-permute-start(f32[224,128]{1,0:T(8,128)S(1)} %collective-permute-done.8.got_ref), channel_id=1, source_target_pairs={{0,1},{1,0},{2,3},{3,2},{4,5},{5,4},{6,7},{7,6},{8,9},{9,8},{10,11... | collective-permute-start | bytes 344072 | tf_op jit(solution)/shard_map/ppermute | solution.py:425
  163.1 1.2 collective-permute-done.9.passed_ref
  164.3 1.8 %level4.1 = (f32[160,128]{1,0:T(8,128)S(1)}, f32[160,128]{1,0:T(8,128)S(1)}) custom-call(f32[448,128]{1,0:T(8,128)S(1)} %get-tuple-element.26.own_ref, f32[224,128]{1,0:T(8,128)S(1)} %collective-permute-done.8.got_ref, f32[224,128]{1,0:T(8,128)S(1)} %collective-permute-done.9.passed_ref), custom_call_target="tpu_custom_call" | custom-call | tf_op jit(solution)/shard_map/level4/pallas_call | solution.py:271
  166.2 6.6 %collective-permute-start.10 = (f32[160,128]{1,0:T(8,128)S(1)}, f32[160,128]{1,0:T(8,128)S(1)}, u32[]{:S(2)}, u32[]{:S(2)}) collective-permute-start(f32[160,128]{1,0:T(8,128)S(1)} %get-tuple-element.27.own_ref), channel_id=1, source_target_pairs={{0,384},{8,392},{16,400},{24,408},{32,416},{40,424},{48,432},{56,4... | collective-permute-start | bytes 245768 | tf_op jit(solution)/shard_map/ppermute | solution.py:429
  172.8 3.9 %collective-permute-done.10.far_ref = f32[160,128]{1,0:T(8,128)S(1)} collective-permute-done((f32[160,128]{1,0:T(8,128)S(1)}, f32[160,128]{1,0:T(8,128)S(1)}, u32[]{:S(2)}, u32[]{:S(2)}) %collective-permute-start.10) | collective-permute-done | bytes 81952 | tf_op jit(solution)/shard_map/ppermute | solution.py:429
  176.7 3.3 %finish.1 = f32[32,256]{1,0:T(8,128)} custom-call(f32[160,128]{1,0:T(8,128)S(1)} %get-tuple-element.27.own_ref, f32[160,128]{1,0:T(8,128)S(1)} %collective-permute-done.10.far_ref, f32[32,256]{1,0:T(8,128)S(1)} %get-tuple-element.28.solved_ref, f32[256,768]{1,0:T(8,128)S(1)} %get-tuple-element.29.images_ref, f32[672,128]{1,0:T(8,128)S(1)} %get-tuple-element.30.refs_0_, ...), custom_call_target="tpu_custom_call" | custom-call | tf_op jit(solution)/shard_map/finish/pallas_call | solution.py:296
  (23 shorter events, 1.6 us)
Async XLA Ops:
  0.0 1.0 copy-start.1
  1.0 0.7 copy-start.4
  1.9 25.9 %copy-start = (bf16[256,2048]{1,0:T(8,128)(2,1)S(1)}, bf16[256,2048]{1,0:T(8,128)(2,1)}, u32[]{:S(2)}) copy-start(bf16[256,2048]{1,0:T(8,128)(2,1)} %inverse_ref.2) | copy-start | bytes 3145732
  1.9 25.9 %copy-start.5 = (s32[1,2048]{1,0:T(1,128)S(1)}, s32[1,2048]{1,0:T(1,128)}, u32[]{:S(2)}) copy-start(s32[1,2048]{1,0:T(1,128)} %order_ref) | copy-start | bytes 24580
  25.9 5.4 %collective-permute-start = (bf16[4,1600,128]{2,1,0:T(8,128)(2,1)S(1)}, bf16[4,1600,128]{2,1,0:T(8,128)(2,1)S(1)}, u32[]{:S(2)}, u32[]{:S(2)}) collective-permute-start(bf16[4,1600,128]{2,1,0:T(8,128)(2,1)S(1)} %all_to_all.20.mine_ref), channel_id=1, source_target_pairs={{0,1},{1,0},{2,3},{3,2},{4,5},{5,4},{6,7},{7,6},{8,9},{9,8},{10,11... | collective-permute-start | bytes 4915208 | tf_op jit(solution)/shard_map/ppermute | solution.py:425
  33.8 4.2 %collective-permute-start.1 = (f32[4,384,128]{2,1,0:T(8,128)S(1)}, f32[4,384,128]{2,1,0:T(8,128)S(1)}, u32[]{:S(2)}, u32[]{:S(2)}) collective-permute-start(f32[4,384,128]{2,1,0:T(8,128)S(1)} %get-tuple-element.23), channel_id=1, source_target_pairs={{0,1},{1,0},{2,3},{3,2},{4,5},{5,4},{6,7},{7,6},{8,9},{9,8},{10,11... | collective-permute-start | bytes 2359304 | tf_op jit(solution)/shard_map/ppermute | solution.py:425
  53.4 6.5 %collective-permute-start.2 = (f32[192,128]{1,0:T(8,128)S(1)}, f32[192,128]{1,0:T(8,128)S(1)}, u32[]{:S(2)}, u32[]{:S(2)}) collective-permute-start(f32[192,128]{1,0:T(8,128)S(1)} %slice.8), channel_id=1, source_target_pairs={{0,8},{8,0},{16,24},{24,16},{32,40},{40,32},{48,56},{56,48},{64,72... | collective-permute-start | bytes 294920 | tf_op jit(solution)/shard_map/ppermute | solution.py:429
  85.4 5.3 %collective-permute-start.4 = (f32[16,192,128]{2,1,0:T(8,128)S(1)}, f32[16,192,128]{2,1,0:T(8,128)S(1)}, u32[]{:S(2)}, u32[]{:S(2)}) collective-permute-start(f32[16,192,128]{2,1,0:T(8,128)S(1)} %all_to_all.22.mine_ref), channel_id=1, source_target_pairs={{0,1},{1,0},{2,3},{3,2},{4,5},{5,4},{6,7},{7,6},{8,9},{9,8},{10,11... | collective-permute-start | bytes 4718600 | tf_op jit(solution)/shard_map/ppermute | solution.py:425
  87.3 10.1 %collective-permute-start.3 = (f32[192,128]{1,0:T(8,128)S(1)}, f32[192,128]{1,0:T(8,128)S(1)}, u32[]{:S(2)}, u32[]{:S(2)}) collective-permute-start(f32[192,128]{1,0:T(8,128)S(1)} %get-tuple-element.35), channel_id=1, source_target_pairs={{0,24},{8,16},{16,8},{24,0},{32,56},{40,48},{48,40},{56,32},{64,88... | collective-permute-start | bytes 294920 | tf_op jit(solution)/shard_map/ppermute | solution.py:429
  114.3 4.2 %collective-permute-start.5 = (f32[8,192,128]{2,1,0:T(8,128)S(1)}, f32[8,192,128]{2,1,0:T(8,128)S(1)}, u32[]{:S(2)}, u32[]{:S(2)}) collective-permute-start(f32[8,192,128]{2,1,0:T(8,128)S(1)} %all_to_all.23.mine_ref), channel_id=1, source_target_pairs={{0,1},{1,0},{2,3},{3,2},{4,5},{5,4},{6,7},{7,6},{8,9},{9,8},{10,11... | collective-permute-start | bytes 2359304 | tf_op jit(solution)/shard_map/ppermute | solution.py:425
  121.2 15.7 %copy-start.2 = (f32[416,128]{1,0:T(8,128)}, f32[416,128]{1,0:T(8,128)S(1)}, u32[]{:S(2)}) copy-start(f32[416,128]{1,0:T(8,128)S(1)} %get-tuple-element.32.refs_2_) | copy-start | bytes 638980
  121.2 15.6 %collective-permute-start.6 = (f32[432,128]{1,0:T(8,128)S(1)}, f32[432,128]{1,0:T(8,128)S(1)}, u32[]{:S(2)}, u32[]{:S(2)}) collective-permute-start(f32[432,128]{1,0:T(8,128)S(1)} %constant_dynamic-slice_fusion.1), channel_id=1, source_target_pairs={{0,64},{8,72},{16,80},{24,88},{32,96},{40,104},{48,112},{56,120},{... | collective-permute-start | bytes 663560 | tf_op jit(solution)/shard_map/ppermute | solution.py:429
  136.8 3.4 %collective-permute-start.7 = (f32[432,128]{1,0:T(8,128)S(1)}, f32[432,128]{1,0:T(8,128)S(1)}, u32[]{:S(2)}, u32[]{:S(2)}) collective-permute-start(f32[432,128]{1,0:T(8,128)S(1)} %collective-permute-done.6.got_ref), channel_id=1, source_target_pairs={{0,1},{1,0},{2,3},{3,2},{4,5},{5,4},{6,7},{7,6},{8,9},{9,8},{10,11... | collective-permute-start | bytes 663560 | tf_op jit(solution)/shard_map/ppermute | solution.py:425
  138.7 37.9 %copy-start.3 = (f32[416,128]{1,0:T(8,128)S(1)}, f32[416,128]{1,0:T(8,128)}, u32[]{:S(2)}) copy-start(f32[416,128]{1,0:T(8,128)} %copy-done.2) | copy-start | bytes 638980
  142.2 18.9 %collective-permute-start.8 = (f32[224,128]{1,0:T(8,128)S(1)}, f32[224,128]{1,0:T(8,128)S(1)}, u32[]{:S(2)}, u32[]{:S(2)}) collective-permute-start(f32[224,128]{1,0:T(8,128)S(1)} %constant_dynamic-slice_fusion), channel_id=1, source_target_pairs={{0,128},{8,136},{16,144},{24,152},{32,160},{40,168},{48,176},{56,1... | collective-permute-start | bytes 344072 | tf_op jit(solution)/shard_map/ppermute | solution.py:429
  161.1 3.2 %collective-permute-start.9 = (f32[224,128]{1,0:T(8,128)S(1)}, f32[224,128]{1,0:T(8,128)S(1)}, u32[]{:S(2)}, u32[]{:S(2)}) collective-permute-start(f32[224,128]{1,0:T(8,128)S(1)} %collective-permute-done.8.got_ref), channel_id=1, source_target_pairs={{0,1},{1,0},{2,3},{3,2},{4,5},{5,4},{6,7},{7,6},{8,9},{9,8},{10,11... | collective-permute-start | bytes 344072 | tf_op jit(solution)/shard_map/ppermute | solution.py:425
  166.2 10.5 %collective-permute-start.10 = (f32[160,128]{1,0:T(8,128)S(1)}, f32[160,128]{1,0:T(8,128)S(1)}, u32[]{:S(2)}, u32[]{:S(2)}) collective-permute-start(f32[160,128]{1,0:T(8,128)S(1)} %get-tuple-element.27.own_ref), channel_id=1, source_target_pairs={{0,384},{8,392},{16,400},{24,408},{32,416},{40,424},{48,432},{56,4... | collective-permute-start | bytes 245768 | tf_op jit(solution)/shard_map/ppermute | solution.py:429

commit v4 on v3

--- a/solution.py
+++ b/solution.py
@@ -15,7 +15,7 @@
 MEMBERS = 8
 CORES = 2
 CHIPS = MEMBERS // CORES
-PAD = 64
+GRANULE = 8
 VMEM_BYTES = 16 * 1024 * 1024
 BOTH = ("leaf", "rows")
 NEAR = {2: 4, 3: 8, 4: 16, 5: 48}
@@ -29,8 +29,15 @@
     return lax.dot_general(a, b, (((1,), (1,)), ((), ())), precision=precision, preferred_element_type=F32)
 
 
-def share_rows(height, tiers, rank):
-    return PAD // MEMBERS + (rank // MEMBERS) * (tiers - height)
+def pair_rows(height, tiers, rank):
+    return GRANULE + (rank // MEMBERS) * (2 * (tiers - height) - 1)
+
+
+def places(height, first, tiers, rank):
+    even = height - height % 2
+    start = sum(pair_rows(h, tiers, rank) for h in range(first, even, 2))
+    skipped = (rank // MEMBERS) * (tiers - even) if height % 2 else 0
+    return start + (GRANULE // 2) * (height % 2), start + GRANULE + skipped
 
 
 def solve(pairs, targets):
@@ -105,19 +112,15 @@
     return jnp.concatenate([s[width + rank :], t[width + rank :]], axis=1)
 
 
-def gathered(halves, node, place, rank):
-    low, each = PAD // MEMBERS, rank // MEMBERS
-    chips = slice(CHIPS * node, CHIPS * (node + 1))
-
-    def joined(start, rows):
-        return jnp.concatenate([half[chips, start : start + rows, :].reshape(CHIPS * rows, rank) for half in halves], axis=0)
-
-    def section(width, blocks):
-        parts = [joined(place, low)[:width]]
-        parts += [joined(place + low + each * k, each) for k in range(blocks)]
-        return jnp.concatenate(parts, axis=0)
-
-    return section
+def gathered(halves, node, height, first, tiers, rank, width):
+    each, few = rank // MEMBERS, width // MEMBERS
+    chips = range(CHIPS * node, CHIPS * (node + 1))
+    top, place = places(height, first, tiers, rank)
+    parts = [half[chip, top : top + few, :] for half in halves for chip in chips]
+    for k in range(tiers - height):
+        rows = slice(place + each * k, place + each * (k + 1))
+        parts += [half[chips.start : chips.stop, rows, :].reshape(CHIPS * each, rank) for half in halves]
+    return jnp.concatenate(parts, axis=0)
 
 
 def by_core(core, mine_ref, theirs_ref, body):
@@ -138,64 +141,71 @@
     return pltpu.CompilerParams(vmem_limit_bytes=VMEM_BYTES)
 
 
-def own_rows(both, member, wide_ref, width, rank):
-    rest = (both.shape[0] - width) // rank
-    low, each = PAD // MEMBERS, rank // MEMBERS
-    wide_ref[0:width, :] = both[:width]
-    wide_ref[width:PAD, :] = jnp.zeros((PAD - width, 2 * rank), F32)
-    wide_ref[PAD : PAD + rank * rest, :] = both[width:]
-    slices = [wide_ref[pl.ds(pl.multiple_of(member * low, low), low), :]]
-    for k in range(rest):
-        slices.append(wide_ref[pl.ds(pl.multiple_of(PAD + rank * k + member * each, each), each), :])
+def own_rows(both, member, wide_ref, rank):
+    each = rank // MEMBERS
+    wide_ref[...] = both
+    slices = [
+        wide_ref[pl.ds(pl.multiple_of(rank * k + member * each, each), each), :] for k in range(both.shape[0] // rank)
+    ]
     return jnp.concatenate(slices, axis=0)
 
 
-def share_change(rows, images, skip, rank):
-    low, each = PAD // MEMBERS, rank // MEMBERS
-    parts = []
-    for g in range(skip, images.shape[0] // rank):
-        chosen = jnp.concatenate([rows[:low], rows[low + each * g :]], axis=0)
-        parts.append(mm_nt(chosen, images[rank * g : rank * (g + 1)]))
-    return jnp.concatenate(parts, axis=0)
-
-
-def four_leaves_kernel(tiers, rank, width, mine_ref, theirs_ref, low_ref, high_ref, change_ref, *wide_refs):
+def four_leaves_kernel(
+    tiers, rank, width, mine_ref, theirs_ref, low_ref, high_ref, change_ref, wide_a, wide_b, wide_c, top_ref
+):
     by_core(
         position(0)[0],
         mine_ref,
         theirs_ref,
-        functools.partial(join_four, tiers, rank, width, low_ref, high_ref, change_ref, wide_refs),
+        functools.partial(
+            join_four, tiers, rank, width, low_ref, high_ref, change_ref, (wide_a, wide_b, wide_c), top_ref
+        ),
     )
 
 
-def join_four(tiers, rank, width, low_ref, high_ref, change_ref, wide_refs, halves):
+def join_four(tiers, rank, width, low_ref, high_ref, change_ref, wide_refs, top_ref, halves):
     _, member, odd = position(0)
     upper = position(1)[2]
-    place = share_rows(0, tiers, rank)
-    nodes = [
-        (gathered(halves, k, 0, rank)(width, tiers), gathered(halves, k, place, rank)(width, tiers - 1))
-        for k in range(4)
-    ]
+    each, few = rank // MEMBERS, width // MEMBERS
+    nodes = [[gathered(halves, k, h, 0, tiers, rank, width) for h in range(2)] for k in range(4)]
+    tops, blocks = [None] * tiers, [None] * tiers
+
+    def note(both, images, first, wide_ref):
+        top = mm_nt(both[:width], images[rank * (2 - first) :])
+        rows = own_rows(both[width:], member, wide_ref, rank)
+        for h in range(2, tiers):
+            g = h - first
+            term = mm_nt(rows[each * g :], images[rank * g : rank * (g + 1)])
+            part = top[:, rank * (h - 2) : rank * (h - 1)]
+            blocks[h] = term if blocks[h] is None else blocks[h] + term
+            tops[h] = part if tops[h] is None else tops[h] + part
+
     pairs = [(nodes[0], nodes[1]), (nodes[2], nodes[3])]
     found = couple([(s[0], t[0]) for s, t in pairs], width, rank)
     picked = [jnp.where(odd == 0, s_c, t_c) for s_c, t_c in found]
     low_ref[...] = jnp.where(upper == 0, picked[0], picked[1])
-    change, joined = None, []
+    joined = []
     for (s_c, t_c), (s, t), wide_ref in zip(found, pairs, wide_refs):
         both = jnp.concatenate([s_c, t_c], axis=1)
         images = images_of(s[0], t[0], width, rank)
         joined.append(s[1] + t[1] - mm_nt(both, images[:rank]))
-        term = share_change(own_rows(both, member, wide_ref, width, rank), images, 1, rank)
-        change = term if change is None else change + term
+        note(both, images, 1, wide_ref)
     ((s_c, t_c),) = couple([tuple(joined)], width, rank)
     high_ref[...] = jnp.where(upper == 0, s_c, t_c)
-    both = jnp.concatenate([s_c, t_c], axis=1)
-    rows = own_rows(both, member, wide_refs[2], width, rank)
-    change_ref[...] = change + share_change(rows, images_of(*joined, width, rank), 0, rank)
+    note(jnp.concatenate([s_c, t_c], axis=1), images_of(*joined, width, rank), 2, wide_refs[2])
+    for h in range(2, tiers):
+        top, place = places(h, 2, tiers, rank)
+        change_ref[place : place + each * (tiers - h), :] = blocks[h]
+        for k in range(MEMBERS):
+            top_ref[k, few * (h - 2) : few * (h - 1), :] = tops[h][few * k : few * (k + 1)]
+    mine = top_ref[member]
+    for h in range(2, tiers, 2):
+        top, _ = places(h, 2, tiers, rank)
+        change_ref[top : top + GRANULE, :] = mine[few * (h - 2) : few * h]
 
 
 def four_leaves(tiers, rank, width, mine, theirs):
-    rows = sum(share_rows(h, tiers, rank) for h in range(2, tiers))
+    rows = sum(pair_rows(h, tiers, rank) for h in range(2, tiers, 2))
     return pl.pallas_call(
         functools.partial(four_leaves_kernel, tiers, rank, width),
         out_shape=[
@@ -205,7 +215,8 @@
         ],
         in_specs=vmem(2),
         out_specs=vmem(3),
-        scratch_shapes=[pltpu.VMEM((PAD + rank * (tiers - k), 2 * rank), F32) for k in (1, 1, 2)],
+        scratch_shapes=[pltpu.VMEM((rank * (tiers - k), 2 * rank), F32) for k in (1, 1, 2)]
+        + [pltpu.VMEM((MEMBERS, (width // MEMBERS) * (tiers - 2), rank), F32)],
         compiler_params=params(),
         name="level0",
     )(mine, theirs)
@@ -227,13 +238,9 @@
     core, _, bit = position(height)
 
     def body(halves):
-        nodes = []
-        for k in range(2):
-            place, sections = 0, []
-            for h in range(height, tiers):
-                sections.append(gathered(halves, k, place, rank)(width, tiers - h))
-                place += share_rows(h, tiers, rank)
-            nodes.append(sections)
+        nodes = [
+            [gathered(halves, k, h, height, tiers, rank, width) for h in range(height, tiers)] for k in range(2)
+        ]
         join_pair(bit, nodes[0], nodes[1], width, rank, coeff_ref, next_ref)
 
     by_core(core, mine_ref, theirs_ref, body)
@@ -281,26 +288,50 @@
     )(*sections)
 
 
-def finish_kernel(tiers, rank, width, own_ref, far_ref, solved_ref, images_ref, *refs):
-    coeff_refs, out_ref = refs[: tiers - 1], refs[tiers - 1]
+def prepare_kernel(tiers, rank, width, solved_ref, images_ref, *refs):
+    coeff_refs, out_ref = refs[:-1], refs[-1]
+    last = tiers - 1
+    found = [None] * last
+    for h in reversed(range(last)):
+        between = rank * (last - 1 - h)
+        value = jnp.concatenate([coeff_refs[h][0:width, :], coeff_refs[h][width + between :, :]], axis=0)
+        if between > 0:
+            value = value - mm(jnp.concatenate(found[h + 1 :], axis=1), coeff_refs[h][width : width + between, :])
+        found[h] = value
+    images = images_ref[...]
+    start = jnp.concatenate([solved_ref[...], images[:, rank * last :].T], axis=0)
+    out_ref[...] = start - mm_nt(jnp.concatenate(found, axis=1), images[:, : rank * last])
+
+
+def prepare(tiers, rank, width, solved, images, coeffs):
+    rows = images.shape[0]
+    return pl.pallas_call(
+        functools.partial(prepare_kernel, tiers, rank, width),
+        out_shape=jax.ShapeDtypeStruct((width + rank, rows), F32),
+        in_specs=vmem(2 + len(coeffs)),
+        out_specs=pl.BlockSpec(memory_space=pltpu.VMEM),
+        compiler_params=params(),
+        cost_estimate=pl.CostEstimate(
+            flops=6 * (width + rank) * images.size, bytes_accessed=4 * images.size, transcendentals=0
+        ),
+        name="prepare",
+    )(solved, images, *coeffs)
+
+
+def finish_kernel(rank, width, own_ref, far_ref, ready_ref, out_ref):
     ((value, _),) = couple([(own_ref[...], far_ref[...])], width, rank)
-    found = [None] * tiers
-    found[tiers - 1] = value
-    for h in reversed(range(tiers - 1)):
-        above = jnp.concatenate(found[h + 1 :], axis=1)
-        found[h] = coeff_refs[h][0:width, :] - mm(above, coeff_refs[h][width:, :])
-    out_ref[...] = solved_ref[...] - mm_nt(images_ref[...], jnp.concatenate(found, axis=1)).T
-
-
-def finish(tiers, rank, width, own, far, solved, images, coeffs):
-    return pl.pallas_call(
-        functools.partial(finish_kernel, tiers, rank, width),
-        out_shape=jax.ShapeDtypeStruct(solved.shape, F32),
-        in_specs=vmem(4 + len(coeffs)),
+    out_ref[...] = ready_ref[0:width, :] - mm(value, ready_ref[width:, :])
+
+
+def finish(rank, width, own, far, ready):
+    return pl.pallas_call(
+        functools.partial(finish_kernel, rank, width),
+        out_shape=jax.ShapeDtypeStruct((width, ready.shape[1]), F32),
+        in_specs=vmem(3),
         out_specs=pl.BlockSpec(memory_space=pltpu.VMEM),
         compiler_params=params(),
         name="finish",
-    )(own, far, solved, images, *coeffs)
+    )(own, far, ready)
 
 
 def pack_kernel(bases_ref, given_ref, out_ref):
@@ -381,30 +412,34 @@
     own = [own_ref[0, rows * h : rows * (h + 1)] for h in range(tiers)]
     flipped = jnp.concatenate(own, axis=1).T
     solved_high, solved_low = pieces(solved)
-    few, each = PAD // MEMBERS, rank // MEMBERS
+    few, each = width // MEMBERS, rank // MEMBERS
 
     def put(block, place, size):
-        block = block.reshape(MEMBERS, size, rank)
-        first, second = block[:CHIPS], block[CHIPS:]
-        keep_ref[:, place : place + size, :] = jnp.where(core == 0, first, second)
-        give_ref[:, place : place + size, :] = jnp.where(core == 0, second, first)
-
-    place = 0
+        half = CHIPS * size
+        first, second = block[:half], block[half:]
+        for ref, value in (
+            (keep_ref, jnp.where(core == 0, first, second)),
+            (give_ref, jnp.where(core == 0, second, first)),
+        ):
+            if size % GRANULE == 0:
+                ref[:, place : place + size, :] = value.reshape(CHIPS, size, rank)
+                continue
+            for chip in range(CHIPS):
+                ref[chip, place : place + size, :] = value[size * chip : size * (chip + 1)]
+
     for h in range(tiers):
-        top = mm(solved_high, own[h], None) + mm(solved_low, own[h], None)
-        put(jnp.concatenate([top, jnp.zeros((PAD - width, rank), F32)], axis=0), place, few)
-        place += few
+        top, place = places(h, 0, tiers, rank)
+        put(mm(solved_high, own[h], None) + mm(solved_low, own[h], None), top, few)
         high, low = pieces(images[:, rank * h : rank * (h + 1)])
         body = mm(flipped[rank * h :], high, None) + mm(flipped[rank * h :], low, None)
         for k in range(tiers - h):
-            put(body[rank * k : rank * (k + 1)], place, each)
-            place += each
+            put(body[rank * k : rank * (k + 1)], place + each * k, each)
     copy.wait()
 
 
 def leaf_step(tiers, rank, width, inverse, moved, mine, theirs, own):
     rows = inverse.shape[0]
-    share = sum(share_rows(h, tiers, rank) for h in range(tiers))
+    share = sum(pair_rows(h, tiers, rank) for h in range(0, tiers, 2))
     return pl.pallas_call(
         functools.partial(leaf_kernel, tiers, rank, width),
         out_shape=[
@@ -460,7 +495,7 @@
     parts = keep + swap_cores(give)
     share = lax.all_to_all(parts, "rows", 0, 0, axis_index_groups=groups).sum(axis=0)
 
-    cut = share_rows(0, tiers, rank) + share_rows(1, tiers, rank)
+    cut = pair_rows(0, tiers, rank)
     tail = share[cut:]
     mine = spread(share[:cut], [tuple(range(i, i + 4)) for i in leaves if i % 4 == 0])
     theirs = swap_cores(mine)
@@ -482,7 +517,8 @@
         coeff, own = pair_level(pair_kernel, height, tiers, rank, width, own, got, passed)
         coeffs.append(coeff)
     far = swap_leaves(own, NEAR[5])
-    return finish(tiers, rank, width, own, far, solved, images, coeffs).T
+    ready = prepare(tiers, rank, width, solved, images, coeffs)
+    return finish(rank, width, own, far, ready).T
 
 
 def solution(mesh):

time: 183 us -> 181 us (0.989)
  transfers between devices with their start and end apart: 11 -> 11, of which waited for: 10 -> 9; matrix products, arithmetic and copies ran while one was open for 0% -> 0% of each run, Pallas kernels for 5% -> 6%
where the time goes in v4:
time: 181 us; the launch traced here: 177 us
  blocking collectives  79.8 us (44%)
  starting transfers between devices  37.6 us (21%)
  waiting for transfers between devices  35.6 us (20%)
  Pallas kernels  21.9 us (12%)
  local copies, waits for them, and re-layouts  1.93 us (1%)
    all_to_all x2, blocking collectives, spread(): lax.all_to_all(jnp.broadcast_to(value[None], (count,) + value.shape), BOT...  41.1 us
    ppermute x5, waiting for transfers between devices, swap_leaves(): lax.ppermute(value, 'leaf', [(i, i ^ mask) for i in range(lax.axis_size('...  27.6 us
    ppermute x5, starting transfers between devices, swap_leaves(): lax.ppermute(value, 'leaf', [(i, i ^ mask) for i in range(lax.axis_size('...  26 us
    all_to_all x1, blocking collectives, local(): mine = lax.all_to_all(packed, 'rows', 0, 0, axis_index_groups=groups)  24 us
    all_to_all x1, blocking collectives, local(): lax.all_to_all(parts, 'rows', 0, 0, axis_index_groups=groups).sum(axis=0)  14.7 us
    ppermute x6, starting transfers between devices, swap_cores(): return lax.ppermute(value, 'rows', [(i, i ^ 1) for i in range(MEMBERS)])  11.6 us
    ppermute x6, waiting for transfers between devices, swap_cores(): return lax.ppermute(value, 'rows', [(i, i ^ 1) for i in range(MEMBERS)])  7.96 us
    pallas_call x1, Pallas kernels, four_leaves(): pl.pallas_call(functools.partial(four_leaves_kernel, tiers, rank, width),...  6.72 us
  transfers between devices with their start and end apart: 11, of which 9 were waited for; matrix products, arithmetic and copies ran while one was open for 0% of the time, Pallas kernels for 6%

profile of v4, /device:TPU:24, one launch (start us, length us, event | category | flops | bytes accessed | tf_op | source)
XLA Modules:
  0.0 177.2 jit_solution(3144993667331968300)
XLA Ops:
  2.0 24.0 %all_to_all.20.mine_ref = bf16[4,1600,128]{2,1,0:T(8,128)(2,1)S(1)} all-to-all(bf16[4,1600,128]{2,1,0:T(8,128)(2,1)S(1)} %pack.1.own_ref), channel_id=1, replica_groups={{0,2,4,6},{1,3,5,7},{8,10,12,14},{9,11,13,15},{16,18,20,22},{17,19,21,2..., dimensions={0} | all-to-all | bytes 3276800 | tf_op jit(solution)/shard_map/all_to_all | solution.py:489
  25.9 1.9 %collective-permute-start = (bf16[4,1600,128]{2,1,0:T(8,128)(2,1)S(1)}, bf16[4,1600,128]{2,1,0:T(8,128)(2,1)S(1)}, u32[]{:S(2)}, u32[]{:S(2)}) collective-permute-start(bf16[4,1600,128]{2,1,0:T(8,128)(2,1)S(1)} %all_to_all.20.mine_ref), channel_id=1, source_target_pairs={{0,1},{1,0},{2,3},{3,2},{4,5},{5,4},{6,7},{7,6},{8,9},{9,8},{10,11... | collective-permute-start | bytes 4915208 | tf_op jit(solution)/shard_map/ppermute | solution.py:460
  27.9 2.4 %reorder.1.moved_ref = bf16[256,2048]{1,0:T(8,128)(2,1)S(1)} custom-call(s32[1,2048]{1,0:T(1,128)S(1)} %copy-done.3, bf16[256,2048]{1,0:T(8,128)(2,1)S(1)} %copy-done), custom_call_target="tpu_custom_call" | custom-call | flops 2147483648 | bytes 2097152 | tf_op jit(solution)/shard_map/reorder/pallas_call | solution.py:374
  30.2 1.1 collective-permute-done.theirs_ref
  31.3 2.5 %leaf.1 = (f32[32,256]{1,0:T(8,128)S(1)}, f32[256,768]{1,0:T(8,128)S(1)}, f32[4,360,128]{2,1,0:T(8,128)S(1)}, f32[4,360,128]{2,1,0:T(8,128)S(1)}) custom-call(bf16[256,2048]{1,0:T(8,128)(2,1)S(1)} %copy-done, bf16[256,2048]{1,0:T(8,128)(2,1)S(1)} %reorder.1.moved_ref, bf16[4,1600,128]{2,1,0:T(8,128)(2,1)S(1)} %all_to_all.20.mine_ref, ...), custom_call_target="tpu_custom_call" | custom-call | tf_op jit(solution)/shard_map/leaf/pallas_call | solution.py:443
  33.8 2.0 %collective-permute-start.1 = (f32[4,360,128]{2,1,0:T(8,128)S(1)}, f32[4,360,128]{2,1,0:T(8,128)S(1)}, u32[]{:S(2)}, u32[]{:S(2)}) collective-permute-start(f32[4,360,128]{2,1,0:T(8,128)S(1)} %get-tuple-element.23), channel_id=1, source_target_pairs={{0,1},{1,0},{2,3},{3,2},{4,5},{5,4},{6,7},{7,6},{8,9},{9,8},{10,11... | collective-permute-start | bytes 2211848 | tf_op jit(solution)/shard_map/ppermute | solution.py:460
  35.9 2.1 %collective-permute-done.1 = f32[4,360,128]{2,1,0:T(8,128)S(1)} collective-permute-done((f32[4,360,128]{2,1,0:T(8,128)S(1)}, f32[4,360,128]{2,1,0:T(8,128)S(1)}, u32[]{:S(2)}, u32[]{:S(2)}) %collective-permute-start.1) | collective-permute-done | bytes 737312 | tf_op jit(solution)/shard_map/ppermute | solution.py:460
  38.0 14.7 %all_to_all.21 = f32[4,360,128]{2,1,0:T(8,128)S(1)} all-to-all(f32[4,360,128]{2,1,0:T(8,128)S(1)} %add.19), channel_id=1, replica_groups={{0,2,4,6},{1,3,5,7},{8,10,12,14},{9,11,13,15},{16,18,20,22},{17,19,21,2..., dimensions={0} | all-to-all | bytes 1474560 | tf_op jit(solution)/shard_map/all_to_all | solution.py:496
  52.9 25.4 %all_to_all.22.mine_ref = f32[16,184,128]{2,1,0:T(8,128)S(1)} all-to-all(f32[16,184,128]{2,1,0:T(8,128)S(1)} %broadcast_in_dim.4), channel_id=1, replica_groups={{0,2,4,6,8,10,12,14,16,18,20,22,24,26,28,30},{1,3,5,7,9,11,13,15,17,19,..., dimensions={0} | all-to-all | bytes 3014656 | tf_op jit(solution)/shard_map/all_to_all | solution.py:478
  78.3 1.9 %collective-permute-start.4 = (f32[16,184,128]{2,1,0:T(8,128)S(1)}, f32[16,184,128]{2,1,0:T(8,128)S(1)}, u32[]{:S(2)}, u32[]{:S(2)}) collective-permute-start(f32[16,184,128]{2,1,0:T(8,128)S(1)} %all_to_all.22.mine_ref), channel_id=1, source_target_pairs={{0,1},{1,0},{2,3},{3,2},{4,5},{5,4},{6,7},{7,6},{8,9},{9,8},{10,11... | collective-permute-start | bytes 4521992 | tf_op jit(solution)/shard_map/ppermute | solution.py:460
  80.3 2.2 %collective-permute-start.2 = (f32[176,128]{1,0:T(8,128)S(1)}, f32[176,128]{1,0:T(8,128)S(1)}, u32[]{:S(2)}, u32[]{:S(2)}) collective-permute-start(f32[176,128]{1,0:T(8,128)S(1)} %slice.8), channel_id=1, source_target_pairs={{0,8},{8,0},{16,24},{24,16},{32,40},{40,32},{48,56},{56,48},{64,72... | collective-permute-start | bytes 270344 | tf_op jit(solution)/shard_map/ppermute | solution.py:464
  82.4 4.7 %collective-permute-done.2 = f32[176,128]{1,0:T(8,128)S(1)} collective-permute-done((f32[176,128]{1,0:T(8,128)S(1)}, f32[176,128]{1,0:T(8,128)S(1)}, u32[]{:S(2)}, u32[]{:S(2)}) %collective-permute-start.2) | collective-permute-done | bytes 90144 | tf_op jit(solution)/shard_map/ppermute | solution.py:464
  87.2 3.1 %collective-permute-start.3 = (f32[176,128]{1,0:T(8,128)S(1)}, f32[176,128]{1,0:T(8,128)S(1)}, u32[]{:S(2)}, u32[]{:S(2)}) collective-permute-start(f32[176,128]{1,0:T(8,128)S(1)} %slice_add_fusion), channel_id=1, source_target_pairs={{0,24},{8,16},{16,8},{24,0},{32,56},{40,48},{48,40},{56,32},{64,88... | collective-permute-start | bytes 270344 | tf_op jit(solution)/shard_map/ppermute | solution.py:464
  90.3 6.7 %level0.1 = (f32[672,128]{1,0:T(8,128)S(1)}, f32[544,128]{1,0:T(8,128)S(1)}, f32[176,128]{1,0:T(8,128)S(1)}) custom-call(f32[16,184,128]{2,1,0:T(8,128)S(1)} %all_to_all.22.mine_ref, f32[16,184,128]{2,1,0:T(8,128)S(1)} %collective-permute-done.4.theirs_ref), custom_call_target="tpu_custom_call" | custom-call | tf_op jit(solution)/shard_map/level0/pallas_call | solution.py:209
  97.1 15.7 %all_to_all.23.mine_ref = f32[8,176,128]{2,1,0:T(8,128)S(1)} all-to-all(f32[8,176,128]{2,1,0:T(8,128)S(1)} %broadcast_in_dim.5), channel_id=1, replica_groups={{0,2,4,6,32,34,36,38},{1,3,5,7,33,35,37,39},{8,10,12,14,40,42,44,46},{9..., dimensions={0} | all-to-all | bytes 1441792 | tf_op jit(solution)/shard_map/all_to_all | solution.py:478
  112.9 1.9 %collective-permute-start.5 = (f32[8,176,128]{2,1,0:T(8,128)S(1)}, f32[8,176,128]{2,1,0:T(8,128)S(1)}, u32[]{:S(2)}, u32[]{:S(2)}) collective-permute-start(f32[8,176,128]{2,1,0:T(8,128)S(1)} %all_to_all.23.mine_ref), channel_id=1, source_target_pairs={{0,1},{1,0},{2,3},{3,2},{4,5},{5,4},{6,7},{7,6},{8,9},{9,8},{10,11... | collective-permute-start | bytes 2162696 | tf_op jit(solution)/shard_map/ppermute | solution.py:460
  114.8 2.1 %collective-permute-done.5.theirs_ref = f32[8,176,128]{2,1,0:T(8,128)S(1)} collective-permute-done((f32[8,176,128]{2,1,0:T(8,128)S(1)}, f32[8,176,128]{2,1,0:T(8,128)S(1)}, u32[]{:S(2)}, u32[]{:S(2)}) %collective-permute-start.5) | collective-permute-done | bytes 720928 | tf_op jit(solution)/shard_map/ppermute | solution.py:460
  116.9 2.6 %level2.1 = (f32[416,128]{1,0:T(8,128)S(1)}, f32[864,128]{1,0:T(8,128)S(1)}) custom-call(f32[8,176,128]{2,1,0:T(8,128)S(1)} %all_to_all.23.mine_ref, f32[8,176,128]{2,1,0:T(8,128)S(1)} %collective-permute-done.5.theirs_ref), custom_call_target="tpu_custom_call" | custom-call | tf_op jit(solution)/shard_map/level2/pallas_call | solution.py:278
  119.6 5.2 %collective-permute-start.6 = (f32[432,128]{1,0:T(8,128)S(1)}, f32[432,128]{1,0:T(8,128)S(1)}, u32[]{:S(2)}, u32[]{:S(2)}) collective-permute-start(f32[432,128]{1,0:T(8,128)S(1)} %constant_dynamic-slice_fusion.1), channel_id=1, source_target_pairs={{0,64},{8,72},{16,80},{24,88},{32,96},{40,104},{48,112},{56,120},{... | collective-permute-start | bytes 663560 | tf_op jit(solution)/shard_map/ppermute | solution.py:464
  124.8 10.5 %collective-permute-done.6.got_ref = f32[432,128]{1,0:T(8,128)S(1)} collective-permute-done((f32[432,128]{1,0:T(8,128)S(1)}, f32[432,128]{1,0:T(8,128)S(1)}, u32[]{:S(2)}, u32[]{:S(2)}) %collective-permute-start.6) | collective-permute-done | bytes 221216 | tf_op jit(solution)/shard_map/ppermute | solution.py:464
  135.3 1.9 %collective-permute-start.7 = (f32[432,128]{1,0:T(8,128)S(1)}, f32[432,128]{1,0:T(8,128)S(1)}, u32[]{:S(2)}, u32[]{:S(2)}) collective-permute-start(f32[432,128]{1,0:T(8,128)S(1)} %collective-permute-done.6.got_ref), channel_id=1, source_target_pairs={{0,1},{1,0},{2,3},{3,2},{4,5},{5,4},{6,7},{7,6},{8,9},{9,8},{10,11... | collective-permute-start | bytes 663560 | tf_op jit(solution)/shard_map/ppermute | solution.py:460
  137.2 1.4 collective-permute-done.7.passed_ref
  138.6 2.0 %level3.1 = (f32[288,128]{1,0:T(8,128)S(1)}, f32[448,128]{1,0:T(8,128)S(1)}) custom-call(f32[864,128]{1,0:T(8,128)S(1)} %get-tuple-element.25.own_ref, f32[432,128]{1,0:T(8,128)S(1)} %collective-permute-done.6.got_ref, f32[432,128]{1,0:T(8,128)S(1)} %collective-permute-done.7.passed_ref), custom_call_target="tpu_custom_call" | custom-call | tf_op jit(solution)/shard_map/level3/pallas_call | solution.py:278
  140.7 9.1 %collective-permute-start.8 = (f32[224,128]{1,0:T(8,128)S(1)}, f32[224,128]{1,0:T(8,128)S(1)}, u32[]{:S(2)}, u32[]{:S(2)}) collective-permute-start(f32[224,128]{1,0:T(8,128)S(1)} %constant_dynamic-slice_fusion), channel_id=1, source_target_pairs={{0,128},{8,136},{16,144},{24,152},{32,160},{40,168},{48,176},{56,1... | collective-permute-start | bytes 344072 | tf_op jit(solution)/shard_map/ppermute | solution.py:464
  149.8 9.8 %collective-permute-done.8.got_ref = f32[224,128]{1,0:T(8,128)S(1)} collective-permute-done((f32[224,128]{1,0:T(8,128)S(1)}, f32[224,128]{1,0:T(8,128)S(1)}, u32[]{:S(2)}, u32[]{:S(2)}) %collective-permute-start.8) | collective-permute-done | bytes 114720 | tf_op jit(solution)/shard_map/ppermute | solution.py:464
  159.6 2.0 %collective-permute-start.9 = (f32[224,128]{1,0:T(8,128)S(1)}, f32[224,128]{1,0:T(8,128)S(1)}, u32[]{:S(2)}, u32[]{:S(2)}) collective-permute-start(f32[224,128]{1,0:T(8,128)S(1)} %collective-permute-done.8.got_ref), channel_id=1, source_target_pairs={{0,1},{1,0},{2,3},{3,2},{4,5},{5,4},{6,7},{7,6},{8,9},{9,8},{10,11... | collective-permute-start | bytes 344072 | tf_op jit(solution)/shard_map/ppermute | solution.py:460
  161.5 1.2 collective-permute-done.9.passed_ref
  162.8 1.8 %level4.1 = (f32[160,128]{1,0:T(8,128)S(1)}, f32[160,128]{1,0:T(8,128)S(1)}) custom-call(f32[448,128]{1,0:T(8,128)S(1)} %get-tuple-element.26.own_ref, f32[224,128]{1,0:T(8,128)S(1)} %collective-permute-done.8.got_ref, f32[224,128]{1,0:T(8,128)S(1)} %collective-permute-done.9.passed_ref), custom_call_target="tpu_custom_call" | custom-call | tf_op jit(solution)/shard_map/level4/pallas_call | solution.py:278
  164.6 6.4 %collective-permute-start.10 = (f32[160,128]{1,0:T(8,128)S(1)}, f32[160,128]{1,0:T(8,128)S(1)}, u32[]{:S(2)}, u32[]{:S(2)}) collective-permute-start(f32[160,128]{1,0:T(8,128)S(1)} %get-tuple-element.27.own_ref), channel_id=1, source_target_pairs={{0,384},{8,392},{16,400},{24,408},{32,416},{40,424},{48,432},{56,4... | collective-permute-start | bytes 245768 | tf_op jit(solution)/shard_map/ppermute | solution.py:464
  171.1 1.4 prepare.1.ready_ref
  172.5 2.6 %collective-permute-done.10.far_ref = f32[160,128]{1,0:T(8,128)S(1)} collective-permute-done((f32[160,128]{1,0:T(8,128)S(1)}, f32[160,128]{1,0:T(8,128)S(1)}, u32[]{:S(2)}, u32[]{:S(2)}) %collective-permute-start.10) | collective-permute-done | bytes 81952 | tf_op jit(solution)/shard_map/ppermute | solution.py:464
  175.1 2.1 %finish.1 = f32[32,256]{1,0:T(8,128)} custom-call(f32[160,128]{1,0:T(8,128)S(1)} %get-tuple-element.27.own_ref, f32[160,128]{1,0:T(8,128)S(1)} %collective-permute-done.10.far_ref, f32[160,256]{1,0:T(8,128)S(1)} %prepare.1.ready_ref), custom_call_target="tpu_custom_call" | custom-call | tf_op jit(solution)/shard_map/finish/pallas_call | solution.py:327
  (21 shorter events, 2.3 us)
Async XLA Ops:
  0.0 1.0 copy-start.1
  1.0 0.7 copy-start.2
  1.9 25.9 %copy-start = (bf16[256,2048]{1,0:T(8,128)(2,1)S(1)}, bf16[256,2048]{1,0:T(8,128)(2,1)}, u32[]{:S(2)}) copy-start(bf16[256,2048]{1,0:T(8,128)(2,1)} %inverse_ref.2) | copy-start | bytes 3145732
  1.9 25.9 %copy-start.3 = (s32[1,2048]{1,0:T(1,128)S(1)}, s32[1,2048]{1,0:T(1,128)}, u32[]{:S(2)}) copy-start(s32[1,2048]{1,0:T(1,128)} %order_ref) | copy-start | bytes 24580
  25.9 5.4 %collective-permute-start = (bf16[4,1600,128]{2,1,0:T(8,128)(2,1)S(1)}, bf16[4,1600,128]{2,1,0:T(8,128)(2,1)S(1)}, u32[]{:S(2)}, u32[]{:S(2)}) collective-permute-start(bf16[4,1600,128]{2,1,0:T(8,128)(2,1)S(1)} %all_to_all.20.mine_ref), channel_id=1, source_target_pairs={{0,1},{1,0},{2,3},{3,2},{4,5},{5,4},{6,7},{7,6},{8,9},{9,8},{10,11... | collective-permute-start | bytes 4915208 | tf_op jit(solution)/shard_map/ppermute | solution.py:460
  33.8 4.1 %collective-permute-start.1 = (f32[4,360,128]{2,1,0:T(8,128)S(1)}, f32[4,360,128]{2,1,0:T(8,128)S(1)}, u32[]{:S(2)}, u32[]{:S(2)}) collective-permute-start(f32[4,360,128]{2,1,0:T(8,128)S(1)} %get-tuple-element.23), channel_id=1, source_target_pairs={{0,1},{1,0},{2,3},{3,2},{4,5},{5,4},{6,7},{7,6},{8,9},{9,8},{10,11... | collective-permute-start | bytes 2211848 | tf_op jit(solution)/shard_map/ppermute | solution.py:460
  78.3 12.0 %collective-permute-start.4 = (f32[16,184,128]{2,1,0:T(8,128)S(1)}, f32[16,184,128]{2,1,0:T(8,128)S(1)}, u32[]{:S(2)}, u32[]{:S(2)}) collective-permute-start(f32[16,184,128]{2,1,0:T(8,128)S(1)} %all_to_all.22.mine_ref), channel_id=1, source_target_pairs={{0,1},{1,0},{2,3},{3,2},{4,5},{5,4},{6,7},{7,6},{8,9},{9,8},{10,11... | collective-permute-start | bytes 4521992 | tf_op jit(solution)/shard_map/ppermute | solution.py:460
  80.3 6.9 %collective-permute-start.2 = (f32[176,128]{1,0:T(8,128)S(1)}, f32[176,128]{1,0:T(8,128)S(1)}, u32[]{:S(2)}, u32[]{:S(2)}) collective-permute-start(f32[176,128]{1,0:T(8,128)S(1)} %slice.8), channel_id=1, source_target_pairs={{0,8},{8,0},{16,24},{24,16},{32,40},{40,32},{48,56},{56,48},{64,72... | collective-permute-start | bytes 270344 | tf_op jit(solution)/shard_map/ppermute | solution.py:464
  87.2 9.8 %collective-permute-start.3 = (f32[176,128]{1,0:T(8,128)S(1)}, f32[176,128]{1,0:T(8,128)S(1)}, u32[]{:S(2)}, u32[]{:S(2)}) collective-permute-start(f32[176,128]{1,0:T(8,128)S(1)} %slice_add_fusion), channel_id=1, source_target_pairs={{0,24},{8,16},{16,8},{24,0},{32,56},{40,48},{48,40},{56,32},{64,88... | collective-permute-start | bytes 270344 | tf_op jit(solution)/shard_map/ppermute | solution.py:464
  112.9 4.1 %collective-permute-start.5 = (f32[8,176,128]{2,1,0:T(8,128)S(1)}, f32[8,176,128]{2,1,0:T(8,128)S(1)}, u32[]{:S(2)}, u32[]{:S(2)}) collective-permute-start(f32[8,176,128]{2,1,0:T(8,128)S(1)} %all_to_all.23.mine_ref), channel_id=1, source_target_pairs={{0,1},{1,0},{2,3},{3,2},{4,5},{5,4},{6,7},{7,6},{8,9},{9,8},{10,11... | collective-permute-start | bytes 2162696 | tf_op jit(solution)/shard_map/ppermute | solution.py:460
  119.6 15.7 %collective-permute-start.6 = (f32[432,128]{1,0:T(8,128)S(1)}, f32[432,128]{1,0:T(8,128)S(1)}, u32[]{:S(2)}, u32[]{:S(2)}) collective-permute-start(f32[432,128]{1,0:T(8,128)S(1)} %constant_dynamic-slice_fusion.1), channel_id=1, source_target_pairs={{0,64},{8,72},{16,80},{24,88},{32,96},{40,104},{48,112},{56,120},{... | collective-permute-start | bytes 663560 | tf_op jit(solution)/shard_map/ppermute | solution.py:464
  135.3 3.4 %collective-permute-start.7 = (f32[432,128]{1,0:T(8,128)S(1)}, f32[432,128]{1,0:T(8,128)S(1)}, u32[]{:S(2)}, u32[]{:S(2)}) collective-permute-start(f32[432,128]{1,0:T(8,128)S(1)} %collective-permute-done.6.got_ref), channel_id=1, source_target_pairs={{0,1},{1,0},{2,3},{3,2},{4,5},{5,4},{6,7},{7,6},{8,9},{9,8},{10,11... | collective-permute-start | bytes 663560 | tf_op jit(solution)/shard_map/ppermute | solution.py:460
  140.7 18.9 %collective-permute-start.8 = (f32[224,128]{1,0:T(8,128)S(1)}, f32[224,128]{1,0:T(8,128)S(1)}, u32[]{:S(2)}, u32[]{:S(2)}) collective-permute-start(f32[224,128]{1,0:T(8,128)S(1)} %constant_dynamic-slice_fusion), channel_id=1, source_target_pairs={{0,128},{8,136},{16,144},{24,152},{32,160},{40,168},{48,176},{56,1... | collective-permute-start | bytes 344072 | tf_op jit(solution)/shard_map/ppermute | solution.py:464
  159.6 3.2 %collective-permute-start.9 = (f32[224,128]{1,0:T(8,128)S(1)}, f32[224,128]{1,0:T(8,128)S(1)}, u32[]{:S(2)}, u32[]{:S(2)}) collective-permute-start(f32[224,128]{1,0:T(8,128)S(1)} %collective-permute-done.8.got_ref), channel_id=1, source_target_pairs={{0,1},{1,0},{2,3},{3,2},{4,5},{5,4},{6,7},{7,6},{8,9},{9,8},{10,11... | collective-permute-start | bytes 344072 | tf_op jit(solution)/shard_map/ppermute | solution.py:460
  164.6 10.5 %collective-permute-start.10 = (f32[160,128]{1,0:T(8,128)S(1)}, f32[160,128]{1,0:T(8,128)S(1)}, u32[]{:S(2)}, u32[]{:S(2)}) collective-permute-start(f32[160,128]{1,0:T(8,128)S(1)} %get-tuple-element.27.own_ref), channel_id=1, source_target_pairs={{0,384},{8,392},{16,400},{24,408},{32,416},{40,424},{48,432},{56,4... | collective-permute-start | bytes 245768 | tf_op jit(solution)/shard_map/ppermute | solution.py:464

commit v5 on v4

--- a/solution.py
+++ b/solution.py
@@ -246,13 +246,81 @@
     by_core(core, mine_ref, theirs_ref, body)
 
 
+def mask_of(rank, compare):
+    return compare(
+        lax.broadcasted_iota(jnp.int32, (rank, rank), 0), lax.broadcasted_iota(jnp.int32, (rank, rank), 1)
+    )
+
+
+def fold_two(a, b):
+    rank = a.shape[0]
+    diagonal = jnp.sum(jnp.where(mask_of(rank, jnp.equal), b, 0.0), axis=0, keepdims=True)
+    return jnp.concatenate(
+        [jnp.where(mask_of(rank, jnp.greater_equal), a, b), jnp.broadcast_to(diagonal, (2 * GRANULE, rank))], axis=0
+    )
+
+
+def unfold_two(folded):
+    rank = folded.shape[1]
+    block = folded[:rank]
+    flipped = block.T
+    a = jnp.where(mask_of(rank, jnp.greater_equal), block, flipped)
+    b = jnp.where(mask_of(rank, jnp.less), block, flipped)
+    diagonal = jnp.broadcast_to(folded[rank : rank + 1], (rank, rank))
+    return a, jnp.where(mask_of(rank, jnp.equal), diagonal, b)
+
+
+def fold_one(a):
+    half, part = a.shape[0] // 2, a.shape[0] // 4
+    corner = a[half:, half:]
+    return jnp.concatenate([a[:half], jnp.concatenate([corner[:part], corner[part:]], axis=1)], axis=0)
+
+
+def unfold_one(folded):
+    half = folded.shape[1] // 2
+    upper, corner = folded[:half], folded[half:]
+    corner = jnp.concatenate([corner[:, :half], corner[:, half:]], axis=0)
+    return jnp.concatenate([upper, jnp.concatenate([upper.T[half:], corner], axis=1)], axis=0)
+
+
+def folded_rows(height, tiers, rank, width):
+    count = tiers - height
+    pairs, single = count // 2, count % 2
+    plain = sum(width + rank * (k - 1) for k in range(1, count + 1))
+    return plain + pairs * (rank + 2 * GRANULE) + single * (3 * rank // 4)
+
+
+def fold(sections, width, rank):
+    parts = [without(section, width, rank) for section in sections]
+    blocks = [section[width : width + rank] for section in sections]
+    while len(blocks) > 1:
+        parts.append(fold_two(blocks[0], blocks[1]))
+        blocks = blocks[2:]
+    parts += [fold_one(block) for block in blocks]
+    return jnp.concatenate(parts, axis=0)
+
+
+def unfold(value, height, tiers, rank, width):
+    place, plain, blocks = 0, [], []
+    for h in range(height, tiers):
+        rows = width + rank * (tiers - h - 1)
+        plain.append(value[place : place + rows])
+        place += rows
+    while len(blocks) + 1 < tiers - height:
+        blocks += unfold_two(value[place : place + rank + 2 * GRANULE])
+        place += rank + 2 * GRANULE
+    if len(blocks) < tiers - height:
+        blocks.append(unfold_one(value[place : place + 3 * rank // 4]))
+    return [
+        jnp.concatenate([part[:width], block] + ([part[width:]] if part.shape[0] > width else []), axis=0)
+        for part, block in zip(plain, blocks)
+    ]
+
+
 def join_pair(bit, s, t, width, rank, coeff_ref, next_ref):
     (pair,) = couple([(s[0], t[0])], width, rank)
     coeff_ref[...] = jnp.where(bit == 0, pair[0], pair[1])
-    place = 0
-    for section in merged(pair, s, t, width, rank):
-        next_ref[place : place + section.shape[0], :] = section
-        place += section.shape[0]
+    next_ref[...] = fold(merged(pair, s, t, width, rank), width, rank)
 
 
 def pair_kernel(height, tiers, rank, width, own_ref, got_ref, passed_ref, coeff_ref, next_ref):
@@ -261,20 +329,12 @@
     far = jnp.concatenate([jnp.where(core == 0, got, passed), jnp.where(core == 0, passed, got)], axis=0)
     lower = jnp.where(bit == 0, own, far)
     upper = jnp.where(bit == 0, far, own)
-
-    def cut(value):
-        place, out = 0, []
-        for h in range(height, tiers):
-            rows = width + rank * (tiers - h)
-            out.append(value[place : place + rows])
-            place += rows
-        return out
-
-    join_pair(bit, cut(lower), cut(upper), width, rank, coeff_ref, next_ref)
+    s, t = [unfold(value, height, tiers, rank, width) for value in (lower, upper)]
+    join_pair(bit, s, t, width, rank, coeff_ref, next_ref)
 
 
 def pair_level(kernel, height, tiers, rank, width, *sections):
-    rows = sum(width + rank * (tiers - h) for h in range(height + 1, tiers))
+    rows = folded_rows(height + 1, tiers, rank, width)
     return pl.pallas_call(
         functools.partial(kernel, height, tiers, rank, width),
         out_shape=[
@@ -319,7 +379,8 @@
 
 
 def finish_kernel(rank, width, own_ref, far_ref, ready_ref, out_ref):
-    ((value, _),) = couple([(own_ref[...], far_ref[...])], width, rank)
+    (own,), (far,) = [unfold(ref[...], 0, 1, rank, width) for ref in (own_ref, far_ref)]
+    ((value, _),) = couple([(own, far)], width, rank)
     out_ref[...] = ready_ref[0:width, :] - mm(value, ready_ref[width:, :])
 
 

time: 181 us -> 176 us (0.972)
  waiting for transfers between devices: 35.6 us -> 31.1 us
    ppermute x5, waiting for transfers between devices: 27.6 us -> 23.2 us  [swap_leaves(): lax.ppermute(value, 'leaf', [(i, i ^ mask) for i in range(lax.axis_size('...]
where the time goes in v5:
time: 176 us; the launch traced here: 173 us
  blocking collectives  79.8 us (45%)
  starting transfers between devices  37.6 us (21%)
  waiting for transfers between devices  31.1 us (18%)
  Pallas kernels  22.3 us (13%)
  local copies, waits for them, and re-layouts  1.93 us (1%)
    all_to_all x2, blocking collectives, spread(): lax.all_to_all(jnp.broadcast_to(value[None], (count,) + value.shape), BOT...  41.1 us
    ppermute x5, starting transfers between devices, swap_leaves(): lax.ppermute(value, 'leaf', [(i, i ^ mask) for i in range(lax.axis_size('...  26 us
    all_to_all x1, blocking collectives, local(): mine = lax.all_to_all(packed, 'rows', 0, 0, axis_index_groups=groups)  24 us
    ppermute x5, waiting for transfers between devices, swap_leaves(): lax.ppermute(value, 'leaf', [(i, i ^ mask) for i in range(lax.axis_size('...  23.2 us
    all_to_all x1, blocking collectives, local(): lax.all_to_all(parts, 'rows', 0, 0, axis_index_groups=groups).sum(axis=0)  14.7 us
    ppermute x6, starting transfers between devices, swap_cores(): return lax.ppermute(value, 'rows', [(i, i ^ 1) for i in range(MEMBERS)])  11.6 us
    ppermute x6, waiting for transfers between devices, swap_cores(): return lax.ppermute(value, 'rows', [(i, i ^ 1) for i in range(MEMBERS)])  7.86 us
    pallas_call x3, Pallas kernels, pair_level(): pl.pallas_call(functools.partial(kernel, height, tiers, rank, width), out...  6.79 us
  transfers between devices with their start and end apart: 11, of which 9 were waited for; matrix products, arithmetic and copies ran while one was open for 0% of the time, Pallas kernels for 6%

profile of v5, /device:TPU:24, one launch (start us, length us, event | category | flops | bytes accessed | tf_op | source)
XLA Modules:
  0.0 173.2 jit_solution(7920463790236458573)
XLA Ops:
  2.0 24.0 %all_to_all.20.mine_ref = bf16[4,1600,128]{2,1,0:T(8,128)(2,1)S(1)} all-to-all(bf16[4,1600,128]{2,1,0:T(8,128)(2,1)S(1)} %pack.1.own_ref), channel_id=1, replica_groups={{0,2,4,6},{1,3,5,7},{8,10,12,14},{9,11,13,15},{16,18,20,22},{17,19,21,2..., dimensions={0} | all-to-all | bytes 3276800 | tf_op jit(solution)/shard_map/all_to_all | solution.py:550
  25.9 1.9 %collective-permute-start = (bf16[4,1600,128]{2,1,0:T(8,128)(2,1)S(1)}, bf16[4,1600,128]{2,1,0:T(8,128)(2,1)S(1)}, u32[]{:S(2)}, u32[]{:S(2)}) collective-permute-start(bf16[4,1600,128]{2,1,0:T(8,128)(2,1)S(1)} %all_to_all.20.mine_ref), channel_id=1, source_target_pairs={{0,1},{1,0},{2,3},{3,2},{4,5},{5,4},{6,7},{7,6},{8,9},{9,8},{10,11... | collective-permute-start | bytes 4915208 | tf_op jit(solution)/shard_map/ppermute | solution.py:521
  27.9 2.4 %reorder.1.moved_ref = bf16[256,2048]{1,0:T(8,128)(2,1)S(1)} custom-call(s32[1,2048]{1,0:T(1,128)S(1)} %copy-done.3, bf16[256,2048]{1,0:T(8,128)(2,1)S(1)} %copy-done), custom_call_target="tpu_custom_call" | custom-call | flops 2147483648 | bytes 2097152 | tf_op jit(solution)/shard_map/reorder/pallas_call | solution.py:435
  30.2 1.1 collective-permute-done.theirs_ref
  31.3 2.5 %leaf.1 = (f32[32,256]{1,0:T(8,128)S(1)}, f32[256,768]{1,0:T(8,128)S(1)}, f32[4,360,128]{2,1,0:T(8,128)S(1)}, f32[4,360,128]{2,1,0:T(8,128)S(1)}) custom-call(bf16[256,2048]{1,0:T(8,128)(2,1)S(1)} %copy-done, bf16[256,2048]{1,0:T(8,128)(2,1)S(1)} %reorder.1.moved_ref, bf16[4,1600,128]{2,1,0:T(8,128)(2,1)S(1)} %all_to_all.20.mine_ref, ...), custom_call_target="tpu_custom_call" | custom-call | tf_op jit(solution)/shard_map/leaf/pallas_call | solution.py:504
  33.8 2.0 %collective-permute-start.1 = (f32[4,360,128]{2,1,0:T(8,128)S(1)}, f32[4,360,128]{2,1,0:T(8,128)S(1)}, u32[]{:S(2)}, u32[]{:S(2)}) collective-permute-start(f32[4,360,128]{2,1,0:T(8,128)S(1)} %get-tuple-element.23), channel_id=1, source_target_pairs={{0,1},{1,0},{2,3},{3,2},{4,5},{5,4},{6,7},{7,6},{8,9},{9,8},{10,11... | collective-permute-start | bytes 2211848 | tf_op jit(solution)/shard_map/ppermute | solution.py:521
  35.9 2.1 %collective-permute-done.1 = f32[4,360,128]{2,1,0:T(8,128)S(1)} collective-permute-done((f32[4,360,128]{2,1,0:T(8,128)S(1)}, f32[4,360,128]{2,1,0:T(8,128)S(1)}, u32[]{:S(2)}, u32[]{:S(2)}) %collective-permute-start.1) | collective-permute-done | bytes 737312 | tf_op jit(solution)/shard_map/ppermute | solution.py:521
  38.0 14.7 %all_to_all.21 = f32[4,360,128]{2,1,0:T(8,128)S(1)} all-to-all(f32[4,360,128]{2,1,0:T(8,128)S(1)} %add.19), channel_id=1, replica_groups={{0,2,4,6},{1,3,5,7},{8,10,12,14},{9,11,13,15},{16,18,20,22},{17,19,21,2..., dimensions={0} | all-to-all | bytes 1474560 | tf_op jit(solution)/shard_map/all_to_all | solution.py:557
  52.9 25.4 %all_to_all.22.mine_ref = f32[16,184,128]{2,1,0:T(8,128)S(1)} all-to-all(f32[16,184,128]{2,1,0:T(8,128)S(1)} %broadcast_in_dim.4), channel_id=1, replica_groups={{0,2,4,6,8,10,12,14,16,18,20,22,24,26,28,30},{1,3,5,7,9,11,13,15,17,19,..., dimensions={0} | all-to-all | bytes 3014656 | tf_op jit(solution)/shard_map/all_to_all | solution.py:539
  78.3 1.9 %collective-permute-start.4 = (f32[16,184,128]{2,1,0:T(8,128)S(1)}, f32[16,184,128]{2,1,0:T(8,128)S(1)}, u32[]{:S(2)}, u32[]{:S(2)}) collective-permute-start(f32[16,184,128]{2,1,0:T(8,128)S(1)} %all_to_all.22.mine_ref), channel_id=1, source_target_pairs={{0,1},{1,0},{2,3},{3,2},{4,5},{5,4},{6,7},{7,6},{8,9},{9,8},{10,11... | collective-permute-start | bytes 4521992 | tf_op jit(solution)/shard_map/ppermute | solution.py:521
  80.2 2.2 %collective-permute-start.2 = (f32[176,128]{1,0:T(8,128)S(1)}, f32[176,128]{1,0:T(8,128)S(1)}, u32[]{:S(2)}, u32[]{:S(2)}) collective-permute-start(f32[176,128]{1,0:T(8,128)S(1)} %slice.8), channel_id=1, source_target_pairs={{0,8},{8,0},{16,24},{24,16},{32,40},{40,32},{48,56},{56,48},{64,72... | collective-permute-start | bytes 270344 | tf_op jit(solution)/shard_map/ppermute | solution.py:525
  82.4 4.7 %collective-permute-done.2 = f32[176,128]{1,0:T(8,128)S(1)} collective-permute-done((f32[176,128]{1,0:T(8,128)S(1)}, f32[176,128]{1,0:T(8,128)S(1)}, u32[]{:S(2)}, u32[]{:S(2)}) %collective-permute-start.2) | collective-permute-done | bytes 90144 | tf_op jit(solution)/shard_map/ppermute | solution.py:525
  87.2 3.1 %collective-permute-start.3 = (f32[176,128]{1,0:T(8,128)S(1)}, f32[176,128]{1,0:T(8,128)S(1)}, u32[]{:S(2)}, u32[]{:S(2)}) collective-permute-start(f32[176,128]{1,0:T(8,128)S(1)} %slice_add_fusion), channel_id=1, source_target_pairs={{0,24},{8,16},{16,8},{24,0},{32,56},{40,48},{48,40},{56,32},{64,88... | collective-permute-start | bytes 270344 | tf_op jit(solution)/shard_map/ppermute | solution.py:525
  90.3 6.7 %level0.1 = (f32[672,128]{1,0:T(8,128)S(1)}, f32[544,128]{1,0:T(8,128)S(1)}, f32[176,128]{1,0:T(8,128)S(1)}) custom-call(f32[16,184,128]{2,1,0:T(8,128)S(1)} %all_to_all.22.mine_ref, f32[16,184,128]{2,1,0:T(8,128)S(1)} %collective-permute-done.4.theirs_ref), custom_call_target="tpu_custom_call" | custom-call | tf_op jit(solution)/shard_map/level0/pallas_call | solution.py:209
  97.1 15.7 %all_to_all.23.mine_ref = f32[8,176,128]{2,1,0:T(8,128)S(1)} all-to-all(f32[8,176,128]{2,1,0:T(8,128)S(1)} %broadcast_in_dim.5), channel_id=1, replica_groups={{0,2,4,6,32,34,36,38},{1,3,5,7,33,35,37,39},{8,10,12,14,40,42,44,46},{9..., dimensions={0} | all-to-all | bytes 1441792 | tf_op jit(solution)/shard_map/all_to_all | solution.py:539
  112.8 1.9 %collective-permute-start.5 = (f32[8,176,128]{2,1,0:T(8,128)S(1)}, f32[8,176,128]{2,1,0:T(8,128)S(1)}, u32[]{:S(2)}, u32[]{:S(2)}) collective-permute-start(f32[8,176,128]{2,1,0:T(8,128)S(1)} %all_to_all.23.mine_ref), channel_id=1, source_target_pairs={{0,1},{1,0},{2,3},{3,2},{4,5},{5,4},{6,7},{7,6},{8,9},{9,8},{10,11... | collective-permute-start | bytes 2162696 | tf_op jit(solution)/shard_map/ppermute | solution.py:521
  114.8 2.1 %collective-permute-done.5.theirs_ref = f32[8,176,128]{2,1,0:T(8,128)S(1)} collective-permute-done((f32[8,176,128]{2,1,0:T(8,128)S(1)}, f32[8,176,128]{2,1,0:T(8,128)S(1)}, u32[]{:S(2)}, u32[]{:S(2)}) %collective-permute-start.5) | collective-permute-done | bytes 720928 | tf_op jit(solution)/shard_map/ppermute | solution.py:521
  116.9 2.6 %level2.1 = (f32[416,128]{1,0:T(8,128)S(1)}, f32[720,128]{1,0:T(8,128)S(1)}) custom-call(f32[8,176,128]{2,1,0:T(8,128)S(1)} %all_to_all.23.mine_ref, f32[8,176,128]{2,1,0:T(8,128)S(1)} %collective-permute-done.5.theirs_ref), custom_call_target="tpu_custom_call" | custom-call | tf_op jit(solution)/shard_map/level2/pallas_call | solution.py:338
  119.6 5.2 %collective-permute-start.6 = (f32[360,128]{1,0:T(8,128)S(1)}, f32[360,128]{1,0:T(8,128)S(1)}, u32[]{:S(2)}, u32[]{:S(2)}) collective-permute-start(f32[360,128]{1,0:T(8,128)S(1)} %constant_dynamic-slice_fusion.1), channel_id=1, source_target_pairs={{0,64},{8,72},{16,80},{24,88},{32,96},{40,104},{48,112},{56,120},{... | collective-permute-start | bytes 552968 | tf_op jit(solution)/shard_map/ppermute | solution.py:525
  124.8 8.9 %collective-permute-done.6.got_ref = f32[360,128]{1,0:T(8,128)S(1)} collective-permute-done((f32[360,128]{1,0:T(8,128)S(1)}, f32[360,128]{1,0:T(8,128)S(1)}, u32[]{:S(2)}, u32[]{:S(2)}) %collective-permute-start.6) | collective-permute-done | bytes 184352 | tf_op jit(solution)/shard_map/ppermute | solution.py:525
  133.7 1.9 %collective-permute-start.7 = (f32[360,128]{1,0:T(8,128)S(1)}, f32[360,128]{1,0:T(8,128)S(1)}, u32[]{:S(2)}, u32[]{:S(2)}) collective-permute-start(f32[360,128]{1,0:T(8,128)S(1)} %collective-permute-done.6.got_ref), channel_id=1, source_target_pairs={{0,1},{1,0},{2,3},{3,2},{4,5},{5,4},{6,7},{7,6},{8,9},{9,8},{10,11... | collective-permute-start | bytes 552968 | tf_op jit(solution)/shard_map/ppermute | solution.py:521
  135.6 1.4 collective-permute-done.7.passed_ref
  137.0 2.2 %level3.1 = (f32[288,128]{1,0:T(8,128)S(1)}, f32[336,128]{1,0:T(8,128)S(1)}) custom-call(f32[720,128]{1,0:T(8,128)S(1)} %get-tuple-element.25.own_ref, f32[360,128]{1,0:T(8,128)S(1)} %collective-permute-done.6.got_ref, f32[360,128]{1,0:T(8,128)S(1)} %collective-permute-done.7.passed_ref), custom_call_target="tpu_custom_call" | custom-call | tf_op jit(solution)/shard_map/level3/pallas_call | solution.py:338
  139.1 9.1 %collective-permute-start.8 = (f32[168,128]{1,0:T(8,128)S(1)}, f32[168,128]{1,0:T(8,128)S(1)}, u32[]{:S(2)}, u32[]{:S(2)}) collective-permute-start(f32[168,128]{1,0:T(8,128)S(1)} %constant_dynamic-slice_fusion), channel_id=1, source_target_pairs={{0,128},{8,136},{16,144},{24,152},{32,160},{40,168},{48,176},{56,1... | collective-permute-start | bytes 258056 | tf_op jit(solution)/shard_map/ppermute | solution.py:525
  148.3 7.3 %collective-permute-done.8.got_ref = f32[168,128]{1,0:T(8,128)S(1)} collective-permute-done((f32[168,128]{1,0:T(8,128)S(1)}, f32[168,128]{1,0:T(8,128)S(1)}, u32[]{:S(2)}, u32[]{:S(2)}) %collective-permute-start.8) | collective-permute-done | bytes 86048 | tf_op jit(solution)/shard_map/ppermute | solution.py:525
  155.6 2.0 %collective-permute-start.9 = (f32[168,128]{1,0:T(8,128)S(1)}, f32[168,128]{1,0:T(8,128)S(1)}, u32[]{:S(2)}, u32[]{:S(2)}) collective-permute-start(f32[168,128]{1,0:T(8,128)S(1)} %collective-permute-done.8.got_ref), channel_id=1, source_target_pairs={{0,1},{1,0},{2,3},{3,2},{4,5},{5,4},{6,7},{7,6},{8,9},{9,8},{10,11... | collective-permute-start | bytes 258056 | tf_op jit(solution)/shard_map/ppermute | solution.py:521
  157.6 1.2 collective-permute-done.9.passed_ref
  158.8 2.0 %level4.1 = (f32[160,128]{1,0:T(8,128)S(1)}, f32[128,128]{1,0:T(8,128)S(1)}) custom-call(f32[336,128]{1,0:T(8,128)S(1)} %get-tuple-element.26.own_ref, f32[168,128]{1,0:T(8,128)S(1)} %collective-permute-done.8.got_ref, f32[168,128]{1,0:T(8,128)S(1)} %collective-permute-done.9.passed_ref), custom_call_target="tpu_custom_call" | custom-call | tf_op jit(solution)/shard_map/level4/pallas_call | solution.py:338
  160.7 6.4 %collective-permute-start.10 = (f32[128,128]{1,0:T(8,128)S(1)}, f32[128,128]{1,0:T(8,128)S(1)}, u32[]{:S(2)}, u32[]{:S(2)}) collective-permute-start(f32[128,128]{1,0:T(8,128)S(1)} %get-tuple-element.27.own_ref), channel_id=1, source_target_pairs={{0,384},{8,392},{16,400},{24,408},{32,416},{40,424},{48,432},{56,4... | collective-permute-start | bytes 196616 | tf_op jit(solution)/shard_map/ppermute | solution.py:525
  167.2 1.4 prepare.1.ready_ref
  168.6 2.3 %collective-permute-done.10.far_ref = f32[128,128]{1,0:T(8,128)S(1)} collective-permute-done((f32[128,128]{1,0:T(8,128)S(1)}, f32[128,128]{1,0:T(8,128)S(1)}, u32[]{:S(2)}, u32[]{:S(2)}) %collective-permute-start.10) | collective-permute-done | bytes 65568 | tf_op jit(solution)/shard_map/ppermute | solution.py:525
  170.9 2.3 %finish.1 = f32[32,256]{1,0:T(8,128)} custom-call(f32[128,128]{1,0:T(8,128)S(1)} %get-tuple-element.27.own_ref, f32[128,128]{1,0:T(8,128)S(1)} %collective-permute-done.10.far_ref, f32[160,256]{1,0:T(8,128)S(1)} %prepare.1.ready_ref), custom_call_target="tpu_custom_call" | custom-call | tf_op jit(solution)/shard_map/finish/pallas_call | solution.py:388
  (21 shorter events, 2.3 us)
Async XLA Ops:
  0.0 1.0 copy-start.1
  1.0 0.7 copy-start.2
  1.9 25.9 %copy-start = (bf16[256,2048]{1,0:T(8,128)(2,1)S(1)}, bf16[256,2048]{1,0:T(8,128)(2,1)}, u32[]{:S(2)}) copy-start(bf16[256,2048]{1,0:T(8,128)(2,1)} %inverse_ref.2) | copy-start | bytes 3145732
  1.9 25.9 %copy-start.3 = (s32[1,2048]{1,0:T(1,128)S(1)}, s32[1,2048]{1,0:T(1,128)}, u32[]{:S(2)}) copy-start(s32[1,2048]{1,0:T(1,128)} %order_ref) | copy-start | bytes 24580
  25.9 5.4 %collective-permute-start = (bf16[4,1600,128]{2,1,0:T(8,128)(2,1)S(1)}, bf16[4,1600,128]{2,1,0:T(8,128)(2,1)S(1)}, u32[]{:S(2)}, u32[]{:S(2)}) collective-permute-start(bf16[4,1600,128]{2,1,0:T(8,128)(2,1)S(1)} %all_to_all.20.mine_ref), channel_id=1, source_target_pairs={{0,1},{1,0},{2,3},{3,2},{4,5},{5,4},{6,7},{7,6},{8,9},{9,8},{10,11... | collective-permute-start | bytes 4915208 | tf_op jit(solution)/shard_map/ppermute | solution.py:521
  33.8 4.1 %collective-permute-start.1 = (f32[4,360,128]{2,1,0:T(8,128)S(1)}, f32[4,360,128]{2,1,0:T(8,128)S(1)}, u32[]{:S(2)}, u32[]{:S(2)}) collective-permute-start(f32[4,360,128]{2,1,0:T(8,128)S(1)} %get-tuple-element.23), channel_id=1, source_target_pairs={{0,1},{1,0},{2,3},{3,2},{4,5},{5,4},{6,7},{7,6},{8,9},{9,8},{10,11... | collective-permute-start | bytes 2211848 | tf_op jit(solution)/shard_map/ppermute | solution.py:521
  78.3 12.0 %collective-permute-start.4 = (f32[16,184,128]{2,1,0:T(8,128)S(1)}, f32[16,184,128]{2,1,0:T(8,128)S(1)}, u32[]{:S(2)}, u32[]{:S(2)}) collective-permute-start(f32[16,184,128]{2,1,0:T(8,128)S(1)} %all_to_all.22.mine_ref), channel_id=1, source_target_pairs={{0,1},{1,0},{2,3},{3,2},{4,5},{5,4},{6,7},{7,6},{8,9},{9,8},{10,11... | collective-permute-start | bytes 4521992 | tf_op jit(solution)/shard_map/ppermute | solution.py:521
  80.2 6.9 %collective-permute-start.2 = (f32[176,128]{1,0:T(8,128)S(1)}, f32[176,128]{1,0:T(8,128)S(1)}, u32[]{:S(2)}, u32[]{:S(2)}) collective-permute-start(f32[176,128]{1,0:T(8,128)S(1)} %slice.8), channel_id=1, source_target_pairs={{0,8},{8,0},{16,24},{24,16},{32,40},{40,32},{48,56},{56,48},{64,72... | collective-permute-start | bytes 270344 | tf_op jit(solution)/shard_map/ppermute | solution.py:525
  87.2 9.8 %collective-permute-start.3 = (f32[176,128]{1,0:T(8,128)S(1)}, f32[176,128]{1,0:T(8,128)S(1)}, u32[]{:S(2)}, u32[]{:S(2)}) collective-permute-start(f32[176,128]{1,0:T(8,128)S(1)} %slice_add_fusion), channel_id=1, source_target_pairs={{0,24},{8,16},{16,8},{24,0},{32,56},{40,48},{48,40},{56,32},{64,88... | collective-permute-start | bytes 270344 | tf_op jit(solution)/shard_map/ppermute | solution.py:525
  112.8 4.1 %collective-permute-start.5 = (f32[8,176,128]{2,1,0:T(8,128)S(1)}, f32[8,176,128]{2,1,0:T(8,128)S(1)}, u32[]{:S(2)}, u32[]{:S(2)}) collective-permute-start(f32[8,176,128]{2,1,0:T(8,128)S(1)} %all_to_all.23.mine_ref), channel_id=1, source_target_pairs={{0,1},{1,0},{2,3},{3,2},{4,5},{5,4},{6,7},{7,6},{8,9},{9,8},{10,11... | collective-permute-start | bytes 2162696 | tf_op jit(solution)/shard_map/ppermute | solution.py:521
  119.6 14.0 %collective-permute-start.6 = (f32[360,128]{1,0:T(8,128)S(1)}, f32[360,128]{1,0:T(8,128)S(1)}, u32[]{:S(2)}, u32[]{:S(2)}) collective-permute-start(f32[360,128]{1,0:T(8,128)S(1)} %constant_dynamic-slice_fusion.1), channel_id=1, source_target_pairs={{0,64},{8,72},{16,80},{24,88},{32,96},{40,104},{48,112},{56,120},{... | collective-permute-start | bytes 552968 | tf_op jit(solution)/shard_map/ppermute | solution.py:525
  133.7 3.3 %collective-permute-start.7 = (f32[360,128]{1,0:T(8,128)S(1)}, f32[360,128]{1,0:T(8,128)S(1)}, u32[]{:S(2)}, u32[]{:S(2)}) collective-permute-start(f32[360,128]{1,0:T(8,128)S(1)} %collective-permute-done.6.got_ref), channel_id=1, source_target_pairs={{0,1},{1,0},{2,3},{3,2},{4,5},{5,4},{6,7},{7,6},{8,9},{9,8},{10,11... | collective-permute-start | bytes 552968 | tf_op jit(solution)/shard_map/ppermute | solution.py:521
  139.1 16.4 %collective-permute-start.8 = (f32[168,128]{1,0:T(8,128)S(1)}, f32[168,128]{1,0:T(8,128)S(1)}, u32[]{:S(2)}, u32[]{:S(2)}) collective-permute-start(f32[168,128]{1,0:T(8,128)S(1)} %constant_dynamic-slice_fusion), channel_id=1, source_target_pairs={{0,128},{8,136},{16,144},{24,152},{32,160},{40,168},{48,176},{56,1... | collective-permute-start | bytes 258056 | tf_op jit(solution)/shard_map/ppermute | solution.py:525
  155.6 3.2 %collective-permute-start.9 = (f32[168,128]{1,0:T(8,128)S(1)}, f32[168,128]{1,0:T(8,128)S(1)}, u32[]{:S(2)}, u32[]{:S(2)}) collective-permute-start(f32[168,128]{1,0:T(8,128)S(1)} %collective-permute-done.8.got_ref), channel_id=1, source_target_pairs={{0,1},{1,0},{2,3},{3,2},{4,5},{5,4},{6,7},{7,6},{8,9},{9,8},{10,11... | collective-permute-start | bytes 258056 | tf_op jit(solution)/shard_map/ppermute | solution.py:521
  160.7 10.2 %collective-permute-start.10 = (f32[128,128]{1,0:T(8,128)S(1)}, f32[128,128]{1,0:T(8,128)S(1)}, u32[]{:S(2)}, u32[]{:S(2)}) collective-permute-start(f32[128,128]{1,0:T(8,128)S(1)} %get-tuple-element.27.own_ref), channel_id=1, source_target_pairs={{0,384},{8,392},{16,400},{24,408},{32,416},{40,424},{48,432},{56,4... | collective-permute-start | bytes 196616 | tf_op jit(solution)/shard_map/ppermute | solution.py:525

commit v6 on v5

--- a/solution.py
+++ b/solution.py
@@ -30,14 +30,15 @@
 
 
 def pair_rows(height, tiers, rank):
-    return GRANULE + (rank // MEMBERS) * (2 * (tiers - height) - 1)
+    return 2 * GRANULE + (rank // MEMBERS) * (2 * (tiers - height) - 2)
 
 
 def places(height, first, tiers, rank):
     even = height - height % 2
     start = sum(pair_rows(h, tiers, rank) for h in range(first, even, 2))
-    skipped = (rank // MEMBERS) * (tiers - even) if height % 2 else 0
-    return start + (GRANULE // 2) * (height % 2), start + GRANULE + skipped
+    each = rank // MEMBERS
+    skipped = each * (tiers - even - 1) if height % 2 else 0
+    return start + (GRANULE // 2) * (height % 2), start + GRANULE, start + 2 * GRANULE + each + skipped
 
 
 def solve(pairs, targets):
@@ -115,12 +116,23 @@
 def gathered(halves, node, height, first, tiers, rank, width):
     each, few = rank // MEMBERS, width // MEMBERS
     chips = range(CHIPS * node, CHIPS * (node + 1))
-    top, place = places(height, first, tiers, rank)
-    parts = [half[chip, top : top + few, :] for half in halves for chip in chips]
-    for k in range(tiers - height):
-        rows = slice(place + each * k, place + each * (k + 1))
-        parts += [half[chips.start : chips.stop, rows, :].reshape(CHIPS * each, rank) for half in halves]
-    return jnp.concatenate(parts, axis=0)
+
+    def joined(start):
+        rows = slice(start, start + each)
+        return [half[chips.start : chips.stop, rows, :].reshape(CHIPS * each, rank) for half in halves]
+
+    _, middle, _ = places(height, first, tiers, rank)
+    block = jnp.concatenate(joined(middle + GRANULE), axis=0)
+    diagonal = sum(half[chip, middle : middle + 1, :] for half in halves for chip in chips)
+    blocks = unfold_two(jnp.concatenate([block, diagonal], axis=0))
+    sections = []
+    for h in (height, height + 1):
+        top, _, place = places(h, first, tiers, rank)
+        parts = [half[chip, top : top + few, :] for half in halves for chip in chips] + [blocks[h - height]]
+        for k in range(tiers - h - 1):
+            parts += joined(place + each * k)
+        sections.append(jnp.concatenate(parts, axis=0))
+    return sections
 
 
 def by_core(core, mine_ref, theirs_ref, body):
@@ -167,7 +179,7 @@
     _, member, odd = position(0)
     upper = position(1)[2]
     each, few = rank // MEMBERS, width // MEMBERS
-    nodes = [[gathered(halves, k, h, 0, tiers, rank, width) for h in range(2)] for k in range(4)]
+    nodes = [gathered(halves, k, 0, 0, tiers, rank, width) for k in range(4)]
     tops, blocks = [None] * tiers, [None] * tiers
 
     def note(both, images, first, wide_ref):
@@ -194,14 +206,21 @@
     high_ref[...] = jnp.where(upper == 0, s_c, t_c)
     note(jnp.concatenate([s_c, t_c], axis=1), images_of(*joined, width, rank), 2, wide_refs[2])
     for h in range(2, tiers):
-        top, place = places(h, 2, tiers, rank)
-        change_ref[place : place + each * (tiers - h), :] = blocks[h]
+        _, _, place = places(h, 2, tiers, rank)
+        if h + 1 < tiers:
+            change_ref[place : place + each * (tiers - h - 1), :] = blocks[h][each:]
         for k in range(MEMBERS):
             top_ref[k, few * (h - 2) : few * (h - 1), :] = tops[h][few * k : few * (k + 1)]
     mine = top_ref[member]
+    row = lax.broadcasted_iota(jnp.int32, (each, rank), 0) + member * each
+    column = lax.broadcasted_iota(jnp.int32, (each, rank), 1)
     for h in range(2, tiers, 2):
-        top, _ = places(h, 2, tiers, rank)
+        top, middle, _ = places(h, 2, tiers, rank)
         change_ref[top : top + GRANULE, :] = mine[few * (h - 2) : few * h]
+        a, b = blocks[h][:each], blocks[h + 1][:each]
+        diagonal = jnp.sum(jnp.where(row == column, b, 0.0), axis=0, keepdims=True)
+        change_ref[middle : middle + GRANULE, :] = jnp.broadcast_to(diagonal, (GRANULE, rank))
+        change_ref[middle + GRANULE : middle + GRANULE + each, :] = jnp.where(row >= column, a, b)
 
 
 def four_leaves(tiers, rank, width, mine, theirs):
@@ -239,7 +258,7 @@
 
     def body(halves):
         nodes = [
-            [gathered(halves, k, h, height, tiers, rank, width) for h in range(height, tiers)] for k in range(2)
+            sum([gathered(halves, k, h, height, tiers, rank, width) for h in range(height, tiers, 2)], []) for k in range(2)
         ]
         join_pair(bit, nodes[0], nodes[1], width, rank, coeff_ref, next_ref)
 
@@ -489,12 +508,20 @@
                 ref[chip, place : place + size, :] = value[size * chip : size * (chip + 1)]
 
     for h in range(tiers):
-        top, place = places(h, 0, tiers, rank)
+        top, middle, place = places(h, 0, tiers, rank)
         put(mm(solved_high, own[h], None) + mm(solved_low, own[h], None), top, few)
         high, low = pieces(images[:, rank * h : rank * (h + 1)])
         body = mm(flipped[rank * h :], high, None) + mm(flipped[rank * h :], low, None)
-        for k in range(tiers - h):
-            put(body[rank * k : rank * (k + 1)], place + each * k, each)
+        for k in range(tiers - h - 1):
+            put(body[rank * (k + 1) : rank * (k + 2)], place + each * k, each)
+        if h % 2 == 0:
+            even = body[:rank]
+            continue
+        odd = body[:rank]
+        diagonal = jnp.where(mask_of(rank, jnp.equal), odd, 0.0).reshape(MEMBERS, each, rank)
+        diagonal = jnp.broadcast_to(jnp.sum(diagonal, axis=1, keepdims=True), (MEMBERS, GRANULE, rank))
+        put(diagonal.reshape(MEMBERS * GRANULE, rank), middle, GRANULE)
+        put(jnp.where(mask_of(rank, jnp.greater_equal), even, odd), middle + GRANULE, each)
     copy.wait()
 
 

time: 176 us -> 174 us (0.989)
  no operation moved by 1% of the time
where the time goes in v6:
time: 174 us; the launch traced here: 171 us
  blocking collectives  78.4 us (45%)
  starting transfers between devices  37.2 us (21%)
  waiting for transfers between devices  30.9 us (18%)
  Pallas kernels  22.4 us (13%)
  local copies, waits for them, and re-layouts  1.92 us (1%)
    all_to_all x2, blocking collectives, spread(): lax.all_to_all(jnp.broadcast_to(value[None], (count,) + value.shape), BOT...  40.2 us
    ppermute x5, starting transfers between devices, swap_leaves(): lax.ppermute(value, 'leaf', [(i, i ^ mask) for i in range(lax.axis_size('...  25.6 us
    all_to_all x1, blocking collectives, local(): mine = lax.all_to_all(packed, 'rows', 0, 0, axis_index_groups=groups)  24 us
    ppermute x5, waiting for transfers between devices, swap_leaves(): lax.ppermute(value, 'leaf', [(i, i ^ mask) for i in range(lax.axis_size('...  23.2 us
    all_to_all x1, blocking collectives, local(): lax.all_to_all(parts, 'rows', 0, 0, axis_index_groups=groups).sum(axis=0)  14.2 us
    ppermute x6, starting transfers between devices, swap_cores(): return lax.ppermute(value, 'rows', [(i, i ^ 1) for i in range(MEMBERS)])  11.6 us
    ppermute x6, waiting for transfers between devices, swap_cores(): return lax.ppermute(value, 'rows', [(i, i ^ 1) for i in range(MEMBERS)])  7.7 us
    pallas_call x3, Pallas kernels, pair_level(): pl.pallas_call(functools.partial(kernel, height, tiers, rank, width), out...  6.86 us
  transfers between devices with their start and end apart: 11, of which 9 were waited for; matrix products, arithmetic and copies ran while one was open for 0% of the time, Pallas kernels for 6%

profile of v6, /device:TPU:24, one launch (start us, length us, event | category | flops | bytes accessed | tf_op | source)
XLA Modules:
  0.0 171.3 jit_solution(4709894540135361496)
XLA Ops:
  2.0 24.0 %all_to_all.20.mine_ref = bf16[4,1600,128]{2,1,0:T(8,128)(2,1)S(1)} all-to-all(bf16[4,1600,128]{2,1,0:T(8,128)(2,1)S(1)} %pack.1.own_ref), channel_id=1, replica_groups={{0,2,4,6},{1,3,5,7},{8,10,12,14},{9,11,13,15},{16,18,20,22},{17,19,21,2..., dimensions={0} | all-to-all | bytes 3276800 | tf_op jit(solution)/shard_map/all_to_all | solution.py:577
  25.9 1.9 %collective-permute-start = (bf16[4,1600,128]{2,1,0:T(8,128)(2,1)S(1)}, bf16[4,1600,128]{2,1,0:T(8,128)(2,1)S(1)}, u32[]{:S(2)}, u32[]{:S(2)}) collective-permute-start(bf16[4,1600,128]{2,1,0:T(8,128)(2,1)S(1)} %all_to_all.20.mine_ref), channel_id=1, source_target_pairs={{0,1},{1,0},{2,3},{3,2},{4,5},{5,4},{6,7},{7,6},{8,9},{9,8},{10,11... | collective-permute-start | bytes 4915208 | tf_op jit(solution)/shard_map/ppermute | solution.py:548
  27.9 2.4 %reorder.1.moved_ref = bf16[256,2048]{1,0:T(8,128)(2,1)S(1)} custom-call(s32[1,2048]{1,0:T(1,128)S(1)} %copy-done.3, bf16[256,2048]{1,0:T(8,128)(2,1)S(1)} %copy-done), custom_call_target="tpu_custom_call" | custom-call | flops 2147483648 | bytes 2097152 | tf_op jit(solution)/shard_map/reorder/pallas_call | solution.py:454
  30.2 1.1 collective-permute-done.theirs_ref
  31.3 2.5 %leaf.1 = (f32[32,256]{1,0:T(8,128)S(1)}, f32[256,768]{1,0:T(8,128)S(1)}, f32[4,336,128]{2,1,0:T(8,128)S(1)}, f32[4,336,128]{2,1,0:T(8,128)S(1)}) custom-call(bf16[256,2048]{1,0:T(8,128)(2,1)S(1)} %copy-done, bf16[256,2048]{1,0:T(8,128)(2,1)S(1)} %reorder.1.moved_ref, bf16[4,1600,128]{2,1,0:T(8,128)(2,1)S(1)} %all_to_all.20.mine_ref, ...), custom_call_target="tpu_custom_call" | custom-call | tf_op jit(solution)/shard_map/leaf/pallas_call | solution.py:531
  33.8 2.0 %collective-permute-start.1 = (f32[4,336,128]{2,1,0:T(8,128)S(1)}, f32[4,336,128]{2,1,0:T(8,128)S(1)}, u32[]{:S(2)}, u32[]{:S(2)}) collective-permute-start(f32[4,336,128]{2,1,0:T(8,128)S(1)} %get-tuple-element.23), channel_id=1, source_target_pairs={{0,1},{1,0},{2,3},{3,2},{4,5},{5,4},{6,7},{7,6},{8,9},{9,8},{10,11... | collective-permute-start | bytes 2064392 | tf_op jit(solution)/shard_map/ppermute | solution.py:548
  35.9 2.0 %collective-permute-done.1 = f32[4,336,128]{2,1,0:T(8,128)S(1)} collective-permute-done((f32[4,336,128]{2,1,0:T(8,128)S(1)}, f32[4,336,128]{2,1,0:T(8,128)S(1)}, u32[]{:S(2)}, u32[]{:S(2)}) %collective-permute-start.1) | collective-permute-done | bytes 688160 | tf_op jit(solution)/shard_map/ppermute | solution.py:548
  38.0 14.2 %all_to_all.21 = f32[4,336,128]{2,1,0:T(8,128)S(1)} all-to-all(f32[4,336,128]{2,1,0:T(8,128)S(1)} %add.19), channel_id=1, replica_groups={{0,2,4,6},{1,3,5,7},{8,10,12,14},{9,11,13,15},{16,18,20,22},{17,19,21,2..., dimensions={0} | all-to-all | bytes 1376256 | tf_op jit(solution)/shard_map/all_to_all | solution.py:584
  52.3 25.0 %all_to_all.22.mine_ref = f32[16,176,128]{2,1,0:T(8,128)S(1)} all-to-all(f32[16,176,128]{2,1,0:T(8,128)S(1)} %broadcast_in_dim.4), channel_id=1, replica_groups={{0,2,4,6,8,10,12,14,16,18,20,22,24,26,28,30},{1,3,5,7,9,11,13,15,17,19,..., dimensions={0} | all-to-all | bytes 2883584 | tf_op jit(solution)/shard_map/all_to_all | solution.py:566
  77.3 1.9 %collective-permute-start.4 = (f32[16,176,128]{2,1,0:T(8,128)S(1)}, f32[16,176,128]{2,1,0:T(8,128)S(1)}, u32[]{:S(2)}, u32[]{:S(2)}) collective-permute-start(f32[16,176,128]{2,1,0:T(8,128)S(1)} %all_to_all.22.mine_ref), channel_id=1, source_target_pairs={{0,1},{1,0},{2,3},{3,2},{4,5},{5,4},{6,7},{7,6},{8,9},{9,8},{10,11... | collective-permute-start | bytes 4325384 | tf_op jit(solution)/shard_map/ppermute | solution.py:548
  79.2 2.1 %collective-permute-start.2 = (f32[160,128]{1,0:T(8,128)S(1)}, f32[160,128]{1,0:T(8,128)S(1)}, u32[]{:S(2)}, u32[]{:S(2)}) collective-permute-start(f32[160,128]{1,0:T(8,128)S(1)} %slice.8), channel_id=1, source_target_pairs={{0,8},{8,0},{16,24},{24,16},{32,40},{40,32},{48,56},{56,48},{64,72... | collective-permute-start | bytes 245768 | tf_op jit(solution)/shard_map/ppermute | solution.py:552
  81.3 4.6 %collective-permute-done.2 = f32[160,128]{1,0:T(8,128)S(1)} collective-permute-done((f32[160,128]{1,0:T(8,128)S(1)}, f32[160,128]{1,0:T(8,128)S(1)}, u32[]{:S(2)}, u32[]{:S(2)}) %collective-permute-start.2) | collective-permute-done | bytes 81952 | tf_op jit(solution)/shard_map/ppermute | solution.py:552
  85.9 2.9 %collective-permute-start.3 = (f32[160,128]{1,0:T(8,128)S(1)}, f32[160,128]{1,0:T(8,128)S(1)}, u32[]{:S(2)}, u32[]{:S(2)}) collective-permute-start(f32[160,128]{1,0:T(8,128)S(1)} %slice_add_fusion), channel_id=1, source_target_pairs={{0,24},{8,16},{16,8},{24,0},{32,56},{40,48},{48,40},{56,32},{64,88... | collective-permute-start | bytes 245768 | tf_op jit(solution)/shard_map/ppermute | solution.py:552
  88.9 6.7 %level0.1 = (f32[672,128]{1,0:T(8,128)S(1)}, f32[544,128]{1,0:T(8,128)S(1)}, f32[160,128]{1,0:T(8,128)S(1)}) custom-call(f32[16,176,128]{2,1,0:T(8,128)S(1)} %all_to_all.22.mine_ref, f32[16,176,128]{2,1,0:T(8,128)S(1)} %collective-permute-done.4.theirs_ref), custom_call_target="tpu_custom_call" | custom-call | tf_op jit(solution)/shard_map/level0/pallas_call | solution.py:228
  95.7 15.2 %all_to_all.23.mine_ref = f32[8,160,128]{2,1,0:T(8,128)S(1)} all-to-all(f32[8,160,128]{2,1,0:T(8,128)S(1)} %broadcast_in_dim.5), channel_id=1, replica_groups={{0,2,4,6,32,34,36,38},{1,3,5,7,33,35,37,39},{8,10,12,14,40,42,44,46},{9..., dimensions={0} | all-to-all | bytes 1310720 | tf_op jit(solution)/shard_map/all_to_all | solution.py:566
  111.0 1.9 %collective-permute-start.5 = (f32[8,160,128]{2,1,0:T(8,128)S(1)}, f32[8,160,128]{2,1,0:T(8,128)S(1)}, u32[]{:S(2)}, u32[]{:S(2)}) collective-permute-start(f32[8,160,128]{2,1,0:T(8,128)S(1)} %all_to_all.23.mine_ref), channel_id=1, source_target_pairs={{0,1},{1,0},{2,3},{3,2},{4,5},{5,4},{6,7},{7,6},{8,9},{9,8},{10,11... | collective-permute-start | bytes 1966088 | tf_op jit(solution)/shard_map/ppermute | solution.py:548
  112.9 2.0 %collective-permute-done.5.theirs_ref = f32[8,160,128]{2,1,0:T(8,128)S(1)} collective-permute-done((f32[8,160,128]{2,1,0:T(8,128)S(1)}, f32[8,160,128]{2,1,0:T(8,128)S(1)}, u32[]{:S(2)}, u32[]{:S(2)}) %collective-permute-start.5) | collective-permute-done | bytes 655392 | tf_op jit(solution)/shard_map/ppermute | solution.py:548
  114.9 2.7 %level2.1 = (f32[416,128]{1,0:T(8,128)S(1)}, f32[720,128]{1,0:T(8,128)S(1)}) custom-call(f32[8,160,128]{2,1,0:T(8,128)S(1)} %all_to_all.23.mine_ref, f32[8,160,128]{2,1,0:T(8,128)S(1)} %collective-permute-done.5.theirs_ref), custom_call_target="tpu_custom_call" | custom-call | tf_op jit(solution)/shard_map/level2/pallas_call | solution.py:357
  117.7 5.2 %collective-permute-start.6 = (f32[360,128]{1,0:T(8,128)S(1)}, f32[360,128]{1,0:T(8,128)S(1)}, u32[]{:S(2)}, u32[]{:S(2)}) collective-permute-start(f32[360,128]{1,0:T(8,128)S(1)} %constant_dynamic-slice_fusion.1), channel_id=1, source_target_pairs={{0,64},{8,72},{16,80},{24,88},{32,96},{40,104},{48,112},{56,120},{... | collective-permute-start | bytes 552968 | tf_op jit(solution)/shard_map/ppermute | solution.py:552
  122.9 8.9 %collective-permute-done.6.got_ref = f32[360,128]{1,0:T(8,128)S(1)} collective-permute-done((f32[360,128]{1,0:T(8,128)S(1)}, f32[360,128]{1,0:T(8,128)S(1)}, u32[]{:S(2)}, u32[]{:S(2)}) %collective-permute-start.6) | collective-permute-done | bytes 184352 | tf_op jit(solution)/shard_map/ppermute | solution.py:552
  131.8 1.9 %collective-permute-start.7 = (f32[360,128]{1,0:T(8,128)S(1)}, f32[360,128]{1,0:T(8,128)S(1)}, u32[]{:S(2)}, u32[]{:S(2)}) collective-permute-start(f32[360,128]{1,0:T(8,128)S(1)} %collective-permute-done.6.got_ref), channel_id=1, source_target_pairs={{0,1},{1,0},{2,3},{3,2},{4,5},{5,4},{6,7},{7,6},{8,9},{9,8},{10,11... | collective-permute-start | bytes 552968 | tf_op jit(solution)/shard_map/ppermute | solution.py:548
  133.7 1.4 collective-permute-done.7.passed_ref
  135.1 2.2 %level3.1 = (f32[288,128]{1,0:T(8,128)S(1)}, f32[336,128]{1,0:T(8,128)S(1)}) custom-call(f32[720,128]{1,0:T(8,128)S(1)} %get-tuple-element.25.own_ref, f32[360,128]{1,0:T(8,128)S(1)} %collective-permute-done.6.got_ref, f32[360,128]{1,0:T(8,128)S(1)} %collective-permute-done.7.passed_ref), custom_call_target="tpu_custom_call" | custom-call | tf_op jit(solution)/shard_map/level3/pallas_call | solution.py:357
  137.3 9.1 %collective-permute-start.8 = (f32[168,128]{1,0:T(8,128)S(1)}, f32[168,128]{1,0:T(8,128)S(1)}, u32[]{:S(2)}, u32[]{:S(2)}) collective-permute-start(f32[168,128]{1,0:T(8,128)S(1)} %constant_dynamic-slice_fusion), channel_id=1, source_target_pairs={{0,128},{8,136},{16,144},{24,152},{32,160},{40,168},{48,176},{56,1... | collective-permute-start | bytes 258056 | tf_op jit(solution)/shard_map/ppermute | solution.py:552
  146.4 7.3 %collective-permute-done.8.got_ref = f32[168,128]{1,0:T(8,128)S(1)} collective-permute-done((f32[168,128]{1,0:T(8,128)S(1)}, f32[168,128]{1,0:T(8,128)S(1)}, u32[]{:S(2)}, u32[]{:S(2)}) %collective-permute-start.8) | collective-permute-done | bytes 86048 | tf_op jit(solution)/shard_map/ppermute | solution.py:552
  153.7 2.0 %collective-permute-start.9 = (f32[168,128]{1,0:T(8,128)S(1)}, f32[168,128]{1,0:T(8,128)S(1)}, u32[]{:S(2)}, u32[]{:S(2)}) collective-permute-start(f32[168,128]{1,0:T(8,128)S(1)} %collective-permute-done.8.got_ref), channel_id=1, source_target_pairs={{0,1},{1,0},{2,3},{3,2},{4,5},{5,4},{6,7},{7,6},{8,9},{9,8},{10,11... | collective-permute-start | bytes 258056 | tf_op jit(solution)/shard_map/ppermute | solution.py:548
  155.7 1.2 collective-permute-done.9.passed_ref
  156.9 2.0 %level4.1 = (f32[160,128]{1,0:T(8,128)S(1)}, f32[128,128]{1,0:T(8,128)S(1)}) custom-call(f32[336,128]{1,0:T(8,128)S(1)} %get-tuple-element.26.own_ref, f32[168,128]{1,0:T(8,128)S(1)} %collective-permute-done.8.got_ref, f32[168,128]{1,0:T(8,128)S(1)} %collective-permute-done.9.passed_ref), custom_call_target="tpu_custom_call" | custom-call | tf_op jit(solution)/shard_map/level4/pallas_call | solution.py:357
  158.8 6.2 %collective-permute-start.10 = (f32[128,128]{1,0:T(8,128)S(1)}, f32[128,128]{1,0:T(8,128)S(1)}, u32[]{:S(2)}, u32[]{:S(2)}) collective-permute-start(f32[128,128]{1,0:T(8,128)S(1)} %get-tuple-element.27.own_ref), channel_id=1, source_target_pairs={{0,384},{8,392},{16,400},{24,408},{32,416},{40,424},{48,432},{56,4... | collective-permute-start | bytes 196616 | tf_op jit(solution)/shard_map/ppermute | solution.py:552
  165.1 1.5 prepare.1.ready_ref
  166.6 2.4 %collective-permute-done.10.far_ref = f32[128,128]{1,0:T(8,128)S(1)} collective-permute-done((f32[128,128]{1,0:T(8,128)S(1)}, f32[128,128]{1,0:T(8,128)S(1)}, u32[]{:S(2)}, u32[]{:S(2)}) %collective-permute-start.10) | collective-permute-done | bytes 65568 | tf_op jit(solution)/shard_map/ppermute | solution.py:552
  169.0 2.3 %finish.1 = f32[32,256]{1,0:T(8,128)} custom-call(f32[128,128]{1,0:T(8,128)S(1)} %get-tuple-element.27.own_ref, f32[128,128]{1,0:T(8,128)S(1)} %collective-permute-done.10.far_ref, f32[160,256]{1,0:T(8,128)S(1)} %prepare.1.ready_ref), custom_call_target="tpu_custom_call" | custom-call | tf_op jit(solution)/shard_map/finish/pallas_call | solution.py:407
  (21 shorter events, 2.3 us)
Async XLA Ops:
  0.0 1.0 copy-start.1
  1.0 0.7 copy-start.2
  1.9 25.9 %copy-start = (bf16[256,2048]{1,0:T(8,128)(2,1)S(1)}, bf16[256,2048]{1,0:T(8,128)(2,1)}, u32[]{:S(2)}) copy-start(bf16[256,2048]{1,0:T(8,128)(2,1)} %inverse_ref.2) | copy-start | bytes 3145732
  1.9 25.9 %copy-start.3 = (s32[1,2048]{1,0:T(1,128)S(1)}, s32[1,2048]{1,0:T(1,128)}, u32[]{:S(2)}) copy-start(s32[1,2048]{1,0:T(1,128)} %order_ref) | copy-start | bytes 24580
  25.9 5.4 %collective-permute-start = (bf16[4,1600,128]{2,1,0:T(8,128)(2,1)S(1)}, bf16[4,1600,128]{2,1,0:T(8,128)(2,1)S(1)}, u32[]{:S(2)}, u32[]{:S(2)}) collective-permute-start(bf16[4,1600,128]{2,1,0:T(8,128)(2,1)S(1)} %all_to_all.20.mine_ref), channel_id=1, source_target_pairs={{0,1},{1,0},{2,3},{3,2},{4,5},{5,4},{6,7},{7,6},{8,9},{9,8},{10,11... | collective-permute-start | bytes 4915208 | tf_op jit(solution)/shard_map/ppermute | solution.py:548
  33.8 4.0 %collective-permute-start.1 = (f32[4,336,128]{2,1,0:T(8,128)S(1)}, f32[4,336,128]{2,1,0:T(8,128)S(1)}, u32[]{:S(2)}, u32[]{:S(2)}) collective-permute-start(f32[4,336,128]{2,1,0:T(8,128)S(1)} %get-tuple-element.23), channel_id=1, source_target_pairs={{0,1},{1,0},{2,3},{3,2},{4,5},{5,4},{6,7},{7,6},{8,9},{9,8},{10,11... | collective-permute-start | bytes 2064392 | tf_op jit(solution)/shard_map/ppermute | solution.py:548
  77.3 11.6 %collective-permute-start.4 = (f32[16,176,128]{2,1,0:T(8,128)S(1)}, f32[16,176,128]{2,1,0:T(8,128)S(1)}, u32[]{:S(2)}, u32[]{:S(2)}) collective-permute-start(f32[16,176,128]{2,1,0:T(8,128)S(1)} %all_to_all.22.mine_ref), channel_id=1, source_target_pairs={{0,1},{1,0},{2,3},{3,2},{4,5},{5,4},{6,7},{7,6},{8,9},{9,8},{10,11... | collective-permute-start | bytes 4325384 | tf_op jit(solution)/shard_map/ppermute | solution.py:548
  79.2 6.7 %collective-permute-start.2 = (f32[160,128]{1,0:T(8,128)S(1)}, f32[160,128]{1,0:T(8,128)S(1)}, u32[]{:S(2)}, u32[]{:S(2)}) collective-permute-start(f32[160,128]{1,0:T(8,128)S(1)} %slice.8), channel_id=1, source_target_pairs={{0,8},{8,0},{16,24},{24,16},{32,40},{40,32},{48,56},{56,48},{64,72... | collective-permute-start | bytes 245768 | tf_op jit(solution)/shard_map/ppermute | solution.py:552
  85.9 9.7 %collective-permute-start.3 = (f32[160,128]{1,0:T(8,128)S(1)}, f32[160,128]{1,0:T(8,128)S(1)}, u32[]{:S(2)}, u32[]{:S(2)}) collective-permute-start(f32[160,128]{1,0:T(8,128)S(1)} %slice_add_fusion), channel_id=1, source_target_pairs={{0,24},{8,16},{16,8},{24,0},{32,56},{40,48},{48,40},{56,32},{64,88... | collective-permute-start | bytes 245768 | tf_op jit(solution)/shard_map/ppermute | solution.py:552
  111.0 4.0 %collective-permute-start.5 = (f32[8,160,128]{2,1,0:T(8,128)S(1)}, f32[8,160,128]{2,1,0:T(8,128)S(1)}, u32[]{:S(2)}, u32[]{:S(2)}) collective-permute-start(f32[8,160,128]{2,1,0:T(8,128)S(1)} %all_to_all.23.mine_ref), channel_id=1, source_target_pairs={{0,1},{1,0},{2,3},{3,2},{4,5},{5,4},{6,7},{7,6},{8,9},{9,8},{10,11... | collective-permute-start | bytes 1966088 | tf_op jit(solution)/shard_map/ppermute | solution.py:548
  117.7 14.1 %collective-permute-start.6 = (f32[360,128]{1,0:T(8,128)S(1)}, f32[360,128]{1,0:T(8,128)S(1)}, u32[]{:S(2)}, u32[]{:S(2)}) collective-permute-start(f32[360,128]{1,0:T(8,128)S(1)} %constant_dynamic-slice_fusion.1), channel_id=1, source_target_pairs={{0,64},{8,72},{16,80},{24,88},{32,96},{40,104},{48,112},{56,120},{... | collective-permute-start | bytes 552968 | tf_op jit(solution)/shard_map/ppermute | solution.py:552
  131.8 3.3 %collective-permute-start.7 = (f32[360,128]{1,0:T(8,128)S(1)}, f32[360,128]{1,0:T(8,128)S(1)}, u32[]{:S(2)}, u32[]{:S(2)}) collective-permute-start(f32[360,128]{1,0:T(8,128)S(1)} %collective-permute-done.6.got_ref), channel_id=1, source_target_pairs={{0,1},{1,0},{2,3},{3,2},{4,5},{5,4},{6,7},{7,6},{8,9},{9,8},{10,11... | collective-permute-start | bytes 552968 | tf_op jit(solution)/shard_map/ppermute | solution.py:548
  137.3 16.4 %collective-permute-start.8 = (f32[168,128]{1,0:T(8,128)S(1)}, f32[168,128]{1,0:T(8,128)S(1)}, u32[]{:S(2)}, u32[]{:S(2)}) collective-permute-start(f32[168,128]{1,0:T(8,128)S(1)} %constant_dynamic-slice_fusion), channel_id=1, source_target_pairs={{0,128},{8,136},{16,144},{24,152},{32,160},{40,168},{48,176},{56,1... | collective-permute-start | bytes 258056 | tf_op jit(solution)/shard_map/ppermute | solution.py:552
  153.7 3.2 %collective-permute-start.9 = (f32[168,128]{1,0:T(8,128)S(1)}, f32[168,128]{1,0:T(8,128)S(1)}, u32[]{:S(2)}, u32[]{:S(2)}) collective-permute-start(f32[168,128]{1,0:T(8,128)S(1)} %collective-permute-done.8.got_ref), channel_id=1, source_target_pairs={{0,1},{1,0},{2,3},{3,2},{4,5},{5,4},{6,7},{7,6},{8,9},{9,8},{10,11... | collective-permute-start | bytes 258056 | tf_op jit(solution)/shard_map/ppermute | solution.py:548
  158.8 10.2 %collective-permute-start.10 = (f32[128,128]{1,0:T(8,128)S(1)}, f32[128,128]{1,0:T(8,128)S(1)}, u32[]{:S(2)}, u32[]{:S(2)}) collective-permute-start(f32[128,128]{1,0:T(8,128)S(1)} %get-tuple-element.27.own_ref), channel_id=1, source_target_pairs={{0,384},{8,392},{16,400},{24,408},{32,416},{40,424},{48,432},{56,4... | collective-permute-start | bytes 196616 | tf_op jit(solution)/shard_map/ppermute | solution.py:552

commit v7 on v6

--- a/solution.py
+++ b/solution.py
@@ -41,7 +41,7 @@
     return start + (GRANULE // 2) * (height % 2), start + GRANULE, start + 2 * GRANULE + each + skipped
 
 
-def solve(pairs, targets):
+def solve(pairs, targets=None):
     rank = pairs[0][0].shape[0]
     eye = (
         lax.broadcasted_iota(jnp.int32, (rank, rank), 0) == lax.broadcasted_iota(jnp.int32, (rank, rank), 1)
@@ -55,7 +55,7 @@
     gaps = [eye - mm(system, guess) for system, guess in zip(systems, guesses)]
     size = functools.reduce(jnp.maximum, [jnp.sum(gap * gap) for gap in gaps])
 
-    firsts = [mm(target, guess) for target, guess in zip(targets, guesses)]
+    firsts = guesses if targets is None else [mm(target, guess) for target, guess in zip(targets, guesses)]
 
     def close():
         return [first + mm(first, gap) for first, gap in zip(firsts, gaps)]
@@ -84,6 +84,8 @@
 
     def far_off():
         found = [refine(left, right, guess) for (left, right), guess in zip(pairs, guesses)]
+        if targets is None:
+            return found
         return [mm(target, inverse, FULL) for target, inverse in zip(targets, found)]
 
     return lax.cond(size < 1e-6, close, far_off)
@@ -107,6 +109,19 @@
     targets = [t_r - mm(s_r, t_a) for (s_r, t_r), (_, t_a) in zip(rests, blocks)]
     found = solve(blocks, targets)
     return [(s_c, s_r - mm(s_c, s_a)) for s_c, (s_r, _), (s_a, _) in zip(found, rests, blocks)]
+
+
+def couple_wide(children, width, rank):
+    blocks = [(s[width : width + rank], t[width : width + rank]) for s, t in children]
+    found = []
+    for (s, t), (s_a, t_a), inverse in zip(children, blocks, solve(blocks)):
+        flipped = inverse.T
+        upper = jnp.concatenate([-mm(t_a, inverse), flipped], axis=1)
+        lower = jnp.concatenate([inverse, -mm(s_a, flipped)], axis=1)
+        rests = jnp.concatenate([without(s, width, rank), without(t, width, rank)], axis=1)
+        both = mm(rests, jnp.concatenate([upper, lower], axis=0))
+        found.append((both[:, :rank], both[:, rank:]))
+    return found
 
 
 def images_of(s, t, width, rank):
@@ -193,7 +208,7 @@
             tops[h] = part if tops[h] is None else tops[h] + part
 
     pairs = [(nodes[0], nodes[1]), (nodes[2], nodes[3])]
-    found = couple([(s[0], t[0]) for s, t in pairs], width, rank)
+    found = couple_wide([(s[0], t[0]) for s, t in pairs], width, rank)
     picked = [jnp.where(odd == 0, s_c, t_c) for s_c, t_c in found]
     low_ref[...] = jnp.where(upper == 0, picked[0], picked[1])
     joined = []
@@ -202,7 +217,7 @@
         images = images_of(s[0], t[0], width, rank)
         joined.append(s[1] + t[1] - mm_nt(both, images[:rank]))
         note(both, images, 1, wide_ref)
-    ((s_c, t_c),) = couple([tuple(joined)], width, rank)
+    ((s_c, t_c),) = couple_wide([tuple(joined)], width, rank)
     high_ref[...] = jnp.where(upper == 0, s_c, t_c)
     note(jnp.concatenate([s_c, t_c], axis=1), images_of(*joined, width, rank), 2, wide_refs[2])
     for h in range(2, tiers):

time: 174 us -> 174 us (level)
  no operation moved by 1% of the time
where the time goes in v7:
time: 174 us; the launch traced here: 171 us
  blocking collectives  78.6 us (45%)
  starting transfers between devices  37.2 us (21%)
  waiting for transfers between devices  31 us (18%)
  Pallas kernels  22.4 us (13%)
  local copies, waits for them, and re-layouts  1.92 us (1%)
    all_to_all x2, blocking collectives, spread(): lax.all_to_all(jnp.broadcast_to(value[None], (count,) + value.shape), BOT...  40.4 us
    ppermute x5, starting transfers between devices, swap_leaves(): lax.ppermute(value, 'leaf', [(i, i ^ mask) for i in range(lax.axis_size('...  25.5 us
    all_to_all x1, blocking collectives, local(): mine = lax.all_to_all(packed, 'rows', 0, 0, axis_index_groups=groups)  24 us
    ppermute x5, waiting for transfers between devices, swap_leaves(): lax.ppermute(value, 'leaf', [(i, i ^ mask) for i in range(lax.axis_size('...  23.3 us
    all_to_all x1, blocking collectives, local(): lax.all_to_all(parts, 'rows', 0, 0, axis_index_groups=groups).sum(axis=0)  14.2 us
    ppermute x6, starting transfers between devices, swap_cores(): return lax.ppermute(value, 'rows', [(i, i ^ 1) for i in range(MEMBERS)])  11.6 us
    ppermute x6, waiting for transfers between devices, swap_cores(): return lax.ppermute(value, 'rows', [(i, i ^ 1) for i in range(MEMBERS)])  7.71 us
    pallas_call x1, Pallas kernels, four_leaves(): pl.pallas_call(functools.partial(four_leaves_kernel, tiers, rank, width),...  6.88 us
  transfers between devices with their start and end apart: 11, of which 9 were waited for; matrix products, arithmetic and copies ran while one was open for 0% of the time, Pallas kernels for 6%

profile of v7, /device:TPU:24, one launch (start us, length us, event | category | flops | bytes accessed | tf_op | source)
XLA Modules:
  0.0 171.4 jit_solution(11942291981651837202)
XLA Ops:
  2.0 24.0 %all_to_all.20.mine_ref = bf16[4,1600,128]{2,1,0:T(8,128)(2,1)S(1)} all-to-all(bf16[4,1600,128]{2,1,0:T(8,128)(2,1)S(1)} %pack.1.own_ref), channel_id=1, replica_groups={{0,2,4,6},{1,3,5,7},{8,10,12,14},{9,11,13,15},{16,18,20,22},{17,19,21,2..., dimensions={0} | all-to-all | bytes 3276800 | tf_op jit(solution)/shard_map/all_to_all | solution.py:592
  25.9 1.9 %collective-permute-start = (bf16[4,1600,128]{2,1,0:T(8,128)(2,1)S(1)}, bf16[4,1600,128]{2,1,0:T(8,128)(2,1)S(1)}, u32[]{:S(2)}, u32[]{:S(2)}) collective-permute-start(bf16[4,1600,128]{2,1,0:T(8,128)(2,1)S(1)} %all_to_all.20.mine_ref), channel_id=1, source_target_pairs={{0,1},{1,0},{2,3},{3,2},{4,5},{5,4},{6,7},{7,6},{8,9},{9,8},{10,11... | collective-permute-start | bytes 4915208 | tf_op jit(solution)/shard_map/ppermute | solution.py:563
  27.9 2.4 %reorder.1.moved_ref = bf16[256,2048]{1,0:T(8,128)(2,1)S(1)} custom-call(s32[1,2048]{1,0:T(1,128)S(1)} %copy-done.3, bf16[256,2048]{1,0:T(8,128)(2,1)S(1)} %copy-done), custom_call_target="tpu_custom_call" | custom-call | flops 2147483648 | bytes 2097152 | tf_op jit(solution)/shard_map/reorder/pallas_call | solution.py:469
  30.2 1.1 collective-permute-done.theirs_ref
  31.3 2.5 %leaf.1 = (f32[32,256]{1,0:T(8,128)S(1)}, f32[256,768]{1,0:T(8,128)S(1)}, f32[4,336,128]{2,1,0:T(8,128)S(1)}, f32[4,336,128]{2,1,0:T(8,128)S(1)}) custom-call(bf16[256,2048]{1,0:T(8,128)(2,1)S(1)} %copy-done, bf16[256,2048]{1,0:T(8,128)(2,1)S(1)} %reorder.1.moved_ref, bf16[4,1600,128]{2,1,0:T(8,128)(2,1)S(1)} %all_to_all.20.mine_ref, ...), custom_call_target="tpu_custom_call" | custom-call | tf_op jit(solution)/shard_map/leaf/pallas_call | solution.py:546
  33.8 2.0 %collective-permute-start.1 = (f32[4,336,128]{2,1,0:T(8,128)S(1)}, f32[4,336,128]{2,1,0:T(8,128)S(1)}, u32[]{:S(2)}, u32[]{:S(2)}) collective-permute-start(f32[4,336,128]{2,1,0:T(8,128)S(1)} %get-tuple-element.23), channel_id=1, source_target_pairs={{0,1},{1,0},{2,3},{3,2},{4,5},{5,4},{6,7},{7,6},{8,9},{9,8},{10,11... | collective-permute-start | bytes 2064392 | tf_op jit(solution)/shard_map/ppermute | solution.py:563
  35.9 2.0 %collective-permute-done.1 = f32[4,336,128]{2,1,0:T(8,128)S(1)} collective-permute-done((f32[4,336,128]{2,1,0:T(8,128)S(1)}, f32[4,336,128]{2,1,0:T(8,128)S(1)}, u32[]{:S(2)}, u32[]{:S(2)}) %collective-permute-start.1) | collective-permute-done | bytes 688160 | tf_op jit(solution)/shard_map/ppermute | solution.py:563
  38.0 14.2 %all_to_all.21 = f32[4,336,128]{2,1,0:T(8,128)S(1)} all-to-all(f32[4,336,128]{2,1,0:T(8,128)S(1)} %add.19), channel_id=1, replica_groups={{0,2,4,6},{1,3,5,7},{8,10,12,14},{9,11,13,15},{16,18,20,22},{17,19,21,2..., dimensions={0} | all-to-all | bytes 1376256 | tf_op jit(solution)/shard_map/all_to_all | solution.py:599
  52.3 25.0 %all_to_all.22.mine_ref = f32[16,176,128]{2,1,0:T(8,128)S(1)} all-to-all(f32[16,176,128]{2,1,0:T(8,128)S(1)} %broadcast_in_dim.4), channel_id=1, replica_groups={{0,2,4,6,8,10,12,14,16,18,20,22,24,26,28,30},{1,3,5,7,9,11,13,15,17,19,..., dimensions={0} | all-to-all | bytes 2883584 | tf_op jit(solution)/shard_map/all_to_all | solution.py:581
  77.3 1.9 %collective-permute-start.4 = (f32[16,176,128]{2,1,0:T(8,128)S(1)}, f32[16,176,128]{2,1,0:T(8,128)S(1)}, u32[]{:S(2)}, u32[]{:S(2)}) collective-permute-start(f32[16,176,128]{2,1,0:T(8,128)S(1)} %all_to_all.22.mine_ref), channel_id=1, source_target_pairs={{0,1},{1,0},{2,3},{3,2},{4,5},{5,4},{6,7},{7,6},{8,9},{9,8},{10,11... | collective-permute-start | bytes 4325384 | tf_op jit(solution)/shard_map/ppermute | solution.py:563
  79.2 2.1 %collective-permute-start.2 = (f32[160,128]{1,0:T(8,128)S(1)}, f32[160,128]{1,0:T(8,128)S(1)}, u32[]{:S(2)}, u32[]{:S(2)}) collective-permute-start(f32[160,128]{1,0:T(8,128)S(1)} %slice.8), channel_id=1, source_target_pairs={{0,8},{8,0},{16,24},{24,16},{32,40},{40,32},{48,56},{56,48},{64,72... | collective-permute-start | bytes 245768 | tf_op jit(solution)/shard_map/ppermute | solution.py:567
  81.3 4.6 %collective-permute-done.2 = f32[160,128]{1,0:T(8,128)S(1)} collective-permute-done((f32[160,128]{1,0:T(8,128)S(1)}, f32[160,128]{1,0:T(8,128)S(1)}, u32[]{:S(2)}, u32[]{:S(2)}) %collective-permute-start.2) | collective-permute-done | bytes 81952 | tf_op jit(solution)/shard_map/ppermute | solution.py:567
  85.9 2.9 %collective-permute-start.3 = (f32[160,128]{1,0:T(8,128)S(1)}, f32[160,128]{1,0:T(8,128)S(1)}, u32[]{:S(2)}, u32[]{:S(2)}) collective-permute-start(f32[160,128]{1,0:T(8,128)S(1)} %slice_add_fusion), channel_id=1, source_target_pairs={{0,24},{8,16},{16,8},{24,0},{32,56},{40,48},{48,40},{56,32},{64,88... | collective-permute-start | bytes 245768 | tf_op jit(solution)/shard_map/ppermute | solution.py:567
  88.9 6.9 %level0.1 = (f32[672,128]{1,0:T(8,128)S(1)}, f32[544,128]{1,0:T(8,128)S(1)}, f32[160,128]{1,0:T(8,128)S(1)}) custom-call(f32[16,176,128]{2,1,0:T(8,128)S(1)} %all_to_all.22.mine_ref, f32[16,176,128]{2,1,0:T(8,128)S(1)} %collective-permute-done.4.theirs_ref), custom_call_target="tpu_custom_call" | custom-call | tf_op jit(solution)/shard_map/level0/pallas_call | solution.py:243
  95.9 15.5 %all_to_all.23.mine_ref = f32[8,160,128]{2,1,0:T(8,128)S(1)} all-to-all(f32[8,160,128]{2,1,0:T(8,128)S(1)} %broadcast_in_dim.5), channel_id=1, replica_groups={{0,2,4,6,32,34,36,38},{1,3,5,7,33,35,37,39},{8,10,12,14,40,42,44,46},{9..., dimensions={0} | all-to-all | bytes 1310720 | tf_op jit(solution)/shard_map/all_to_all | solution.py:581
  111.3 1.9 %collective-permute-start.5 = (f32[8,160,128]{2,1,0:T(8,128)S(1)}, f32[8,160,128]{2,1,0:T(8,128)S(1)}, u32[]{:S(2)}, u32[]{:S(2)}) collective-permute-start(f32[8,160,128]{2,1,0:T(8,128)S(1)} %all_to_all.23.mine_ref), channel_id=1, source_target_pairs={{0,1},{1,0},{2,3},{3,2},{4,5},{5,4},{6,7},{7,6},{8,9},{9,8},{10,11... | collective-permute-start | bytes 1966088 | tf_op jit(solution)/shard_map/ppermute | solution.py:563
  113.2 2.0 %collective-permute-done.5.theirs_ref = f32[8,160,128]{2,1,0:T(8,128)S(1)} collective-permute-done((f32[8,160,128]{2,1,0:T(8,128)S(1)}, f32[8,160,128]{2,1,0:T(8,128)S(1)}, u32[]{:S(2)}, u32[]{:S(2)}) %collective-permute-start.5) | collective-permute-done | bytes 655392 | tf_op jit(solution)/shard_map/ppermute | solution.py:563
  115.3 2.5 %level2.1 = (f32[416,128]{1,0:T(8,128)S(1)}, f32[720,128]{1,0:T(8,128)S(1)}) custom-call(f32[8,160,128]{2,1,0:T(8,128)S(1)} %all_to_all.23.mine_ref, f32[8,160,128]{2,1,0:T(8,128)S(1)} %collective-permute-done.5.theirs_ref), custom_call_target="tpu_custom_call" | custom-call | tf_op jit(solution)/shard_map/level2/pallas_call | solution.py:372
  117.8 5.2 %collective-permute-start.6 = (f32[360,128]{1,0:T(8,128)S(1)}, f32[360,128]{1,0:T(8,128)S(1)}, u32[]{:S(2)}, u32[]{:S(2)}) collective-permute-start(f32[360,128]{1,0:T(8,128)S(1)} %constant_dynamic-slice_fusion.1), channel_id=1, source_target_pairs={{0,64},{8,72},{16,80},{24,88},{32,96},{40,104},{48,112},{56,120},{... | collective-permute-start | bytes 552968 | tf_op jit(solution)/shard_map/ppermute | solution.py:567
  123.0 8.9 %collective-permute-done.6.got_ref = f32[360,128]{1,0:T(8,128)S(1)} collective-permute-done((f32[360,128]{1,0:T(8,128)S(1)}, f32[360,128]{1,0:T(8,128)S(1)}, u32[]{:S(2)}, u32[]{:S(2)}) %collective-permute-start.6) | collective-permute-done | bytes 184352 | tf_op jit(solution)/shard_map/ppermute | solution.py:567
  131.9 1.9 %collective-permute-start.7 = (f32[360,128]{1,0:T(8,128)S(1)}, f32[360,128]{1,0:T(8,128)S(1)}, u32[]{:S(2)}, u32[]{:S(2)}) collective-permute-start(f32[360,128]{1,0:T(8,128)S(1)} %collective-permute-done.6.got_ref), channel_id=1, source_target_pairs={{0,1},{1,0},{2,3},{3,2},{4,5},{5,4},{6,7},{7,6},{8,9},{9,8},{10,11... | collective-permute-start | bytes 552968 | tf_op jit(solution)/shard_map/ppermute | solution.py:563
  133.8 1.4 collective-permute-done.7.passed_ref
  135.2 2.2 %level3.1 = (f32[288,128]{1,0:T(8,128)S(1)}, f32[336,128]{1,0:T(8,128)S(1)}) custom-call(f32[720,128]{1,0:T(8,128)S(1)} %get-tuple-element.25.own_ref, f32[360,128]{1,0:T(8,128)S(1)} %collective-permute-done.6.got_ref, f32[360,128]{1,0:T(8,128)S(1)} %collective-permute-done.7.passed_ref), custom_call_target="tpu_custom_call" | custom-call | tf_op jit(solution)/shard_map/level3/pallas_call | solution.py:372
  137.4 9.1 %collective-permute-start.8 = (f32[168,128]{1,0:T(8,128)S(1)}, f32[168,128]{1,0:T(8,128)S(1)}, u32[]{:S(2)}, u32[]{:S(2)}) collective-permute-start(f32[168,128]{1,0:T(8,128)S(1)} %constant_dynamic-slice_fusion), channel_id=1, source_target_pairs={{0,128},{8,136},{16,144},{24,152},{32,160},{40,168},{48,176},{56,1... | collective-permute-start | bytes 258056 | tf_op jit(solution)/shard_map/ppermute | solution.py:567
  146.5 7.3 %collective-permute-done.8.got_ref = f32[168,128]{1,0:T(8,128)S(1)} collective-permute-done((f32[168,128]{1,0:T(8,128)S(1)}, f32[168,128]{1,0:T(8,128)S(1)}, u32[]{:S(2)}, u32[]{:S(2)}) %collective-permute-start.8) | collective-permute-done | bytes 86048 | tf_op jit(solution)/shard_map/ppermute | solution.py:567
  153.8 2.0 %collective-permute-start.9 = (f32[168,128]{1,0:T(8,128)S(1)}, f32[168,128]{1,0:T(8,128)S(1)}, u32[]{:S(2)}, u32[]{:S(2)}) collective-permute-start(f32[168,128]{1,0:T(8,128)S(1)} %collective-permute-done.8.got_ref), channel_id=1, source_target_pairs={{0,1},{1,0},{2,3},{3,2},{4,5},{5,4},{6,7},{7,6},{8,9},{9,8},{10,11... | collective-permute-start | bytes 258056 | tf_op jit(solution)/shard_map/ppermute | solution.py:563
  155.8 1.2 collective-permute-done.9.passed_ref
  157.0 2.0 %level4.1 = (f32[160,128]{1,0:T(8,128)S(1)}, f32[128,128]{1,0:T(8,128)S(1)}) custom-call(f32[336,128]{1,0:T(8,128)S(1)} %get-tuple-element.26.own_ref, f32[168,128]{1,0:T(8,128)S(1)} %collective-permute-done.8.got_ref, f32[168,128]{1,0:T(8,128)S(1)} %collective-permute-done.9.passed_ref), custom_call_target="tpu_custom_call" | custom-call | tf_op jit(solution)/shard_map/level4/pallas_call | solution.py:372
  159.0 6.2 %collective-permute-start.10 = (f32[128,128]{1,0:T(8,128)S(1)}, f32[128,128]{1,0:T(8,128)S(1)}, u32[]{:S(2)}, u32[]{:S(2)}) collective-permute-start(f32[128,128]{1,0:T(8,128)S(1)} %get-tuple-element.27.own_ref), channel_id=1, source_target_pairs={{0,384},{8,392},{16,400},{24,408},{32,416},{40,424},{48,432},{56,4... | collective-permute-start | bytes 196616 | tf_op jit(solution)/shard_map/ppermute | solution.py:567
  165.2 1.5 prepare.1.ready_ref
  166.6 2.5 %collective-permute-done.10.far_ref = f32[128,128]{1,0:T(8,128)S(1)} collective-permute-done((f32[128,128]{1,0:T(8,128)S(1)}, f32[128,128]{1,0:T(8,128)S(1)}, u32[]{:S(2)}, u32[]{:S(2)}) %collective-permute-start.10) | collective-permute-done | bytes 65568 | tf_op jit(solution)/shard_map/ppermute | solution.py:567
  169.1 2.3 %finish.1 = f32[32,256]{1,0:T(8,128)} custom-call(f32[128,128]{1,0:T(8,128)S(1)} %get-tuple-element.27.own_ref, f32[128,128]{1,0:T(8,128)S(1)} %collective-permute-done.10.far_ref, f32[160,256]{1,0:T(8,128)S(1)} %prepare.1.ready_ref), custom_call_target="tpu_custom_call" | custom-call | tf_op jit(solution)/shard_map/finish/pallas_call | solution.py:422
  (21 shorter events, 2.3 us)
Async XLA Ops:
  0.0 1.0 copy-start.1
  1.0 0.7 copy-start.2
  1.9 25.9 %copy-start = (bf16[256,2048]{1,0:T(8,128)(2,1)S(1)}, bf16[256,2048]{1,0:T(8,128)(2,1)}, u32[]{:S(2)}) copy-start(bf16[256,2048]{1,0:T(8,128)(2,1)} %inverse_ref.2) | copy-start | bytes 3145732
  1.9 25.9 %copy-start.3 = (s32[1,2048]{1,0:T(1,128)S(1)}, s32[1,2048]{1,0:T(1,128)}, u32[]{:S(2)}) copy-start(s32[1,2048]{1,0:T(1,128)} %order_ref) | copy-start | bytes 24580
  25.9 5.4 %collective-permute-start = (bf16[4,1600,128]{2,1,0:T(8,128)(2,1)S(1)}, bf16[4,1600,128]{2,1,0:T(8,128)(2,1)S(1)}, u32[]{:S(2)}, u32[]{:S(2)}) collective-permute-start(bf16[4,1600,128]{2,1,0:T(8,128)(2,1)S(1)} %all_to_all.20.mine_ref), channel_id=1, source_target_pairs={{0,1},{1,0},{2,3},{3,2},{4,5},{5,4},{6,7},{7,6},{8,9},{9,8},{10,11... | collective-permute-start | bytes 4915208 | tf_op jit(solution)/shard_map/ppermute | solution.py:563
  33.8 4.0 %collective-permute-start.1 = (f32[4,336,128]{2,1,0:T(8,128)S(1)}, f32[4,336,128]{2,1,0:T(8,128)S(1)}, u32[]{:S(2)}, u32[]{:S(2)}) collective-permute-start(f32[4,336,128]{2,1,0:T(8,128)S(1)} %get-tuple-element.23), channel_id=1, source_target_pairs={{0,1},{1,0},{2,3},{3,2},{4,5},{5,4},{6,7},{7,6},{8,9},{9,8},{10,11... | collective-permute-start | bytes 2064392 | tf_op jit(solution)/shard_map/ppermute | solution.py:563
  77.3 11.6 %collective-permute-start.4 = (f32[16,176,128]{2,1,0:T(8,128)S(1)}, f32[16,176,128]{2,1,0:T(8,128)S(1)}, u32[]{:S(2)}, u32[]{:S(2)}) collective-permute-start(f32[16,176,128]{2,1,0:T(8,128)S(1)} %all_to_all.22.mine_ref), channel_id=1, source_target_pairs={{0,1},{1,0},{2,3},{3,2},{4,5},{5,4},{6,7},{7,6},{8,9},{9,8},{10,11... | collective-permute-start | bytes 4325384 | tf_op jit(solution)/shard_map/ppermute | solution.py:563
  79.2 6.7 %collective-permute-start.2 = (f32[160,128]{1,0:T(8,128)S(1)}, f32[160,128]{1,0:T(8,128)S(1)}, u32[]{:S(2)}, u32[]{:S(2)}) collective-permute-start(f32[160,128]{1,0:T(8,128)S(1)} %slice.8), channel_id=1, source_target_pairs={{0,8},{8,0},{16,24},{24,16},{32,40},{40,32},{48,56},{56,48},{64,72... | collective-permute-start | bytes 245768 | tf_op jit(solution)/shard_map/ppermute | solution.py:567
  85.9 9.8 %collective-permute-start.3 = (f32[160,128]{1,0:T(8,128)S(1)}, f32[160,128]{1,0:T(8,128)S(1)}, u32[]{:S(2)}, u32[]{:S(2)}) collective-permute-start(f32[160,128]{1,0:T(8,128)S(1)} %slice_add_fusion), channel_id=1, source_target_pairs={{0,24},{8,16},{16,8},{24,0},{32,56},{40,48},{48,40},{56,32},{64,88... | collective-permute-start | bytes 245768 | tf_op jit(solution)/shard_map/ppermute | solution.py:567
  111.3 4.0 %collective-permute-start.5 = (f32[8,160,128]{2,1,0:T(8,128)S(1)}, f32[8,160,128]{2,1,0:T(8,128)S(1)}, u32[]{:S(2)}, u32[]{:S(2)}) collective-permute-start(f32[8,160,128]{2,1,0:T(8,128)S(1)} %all_to_all.23.mine_ref), channel_id=1, source_target_pairs={{0,1},{1,0},{2,3},{3,2},{4,5},{5,4},{6,7},{7,6},{8,9},{9,8},{10,11... | collective-permute-start | bytes 1966088 | tf_op jit(solution)/shard_map/ppermute | solution.py:563
  117.8 14.1 %collective-permute-start.6 = (f32[360,128]{1,0:T(8,128)S(1)}, f32[360,128]{1,0:T(8,128)S(1)}, u32[]{:S(2)}, u32[]{:S(2)}) collective-permute-start(f32[360,128]{1,0:T(8,128)S(1)} %constant_dynamic-slice_fusion.1), channel_id=1, source_target_pairs={{0,64},{8,72},{16,80},{24,88},{32,96},{40,104},{48,112},{56,120},{... | collective-permute-start | bytes 552968 | tf_op jit(solution)/shard_map/ppermute | solution.py:567
  131.9 3.3 %collective-permute-start.7 = (f32[360,128]{1,0:T(8,128)S(1)}, f32[360,128]{1,0:T(8,128)S(1)}, u32[]{:S(2)}, u32[]{:S(2)}) collective-permute-start(f32[360,128]{1,0:T(8,128)S(1)} %collective-permute-done.6.got_ref), channel_id=1, source_target_pairs={{0,1},{1,0},{2,3},{3,2},{4,5},{5,4},{6,7},{7,6},{8,9},{9,8},{10,11... | collective-permute-start | bytes 552968 | tf_op jit(solution)/shard_map/ppermute | solution.py:563
  137.4 16.4 %collective-permute-start.8 = (f32[168,128]{1,0:T(8,128)S(1)}, f32[168,128]{1,0:T(8,128)S(1)}, u32[]{:S(2)}, u32[]{:S(2)}) collective-permute-start(f32[168,128]{1,0:T(8,128)S(1)} %constant_dynamic-slice_fusion), channel_id=1, source_target_pairs={{0,128},{8,136},{16,144},{24,152},{32,160},{40,168},{48,176},{56,1... | collective-permute-start | bytes 258056 | tf_op jit(solution)/shard_map/ppermute | solution.py:567
  153.8 3.2 %collective-permute-start.9 = (f32[168,128]{1,0:T(8,128)S(1)}, f32[168,128]{1,0:T(8,128)S(1)}, u32[]{:S(2)}, u32[]{:S(2)}) collective-permute-start(f32[168,128]{1,0:T(8,128)S(1)} %collective-permute-done.8.got_ref), channel_id=1, source_target_pairs={{0,1},{1,0},{2,3},{3,2},{4,5},{5,4},{6,7},{7,6},{8,9},{9,8},{10,11... | collective-permute-start | bytes 258056 | tf_op jit(solution)/shard_map/ppermute | solution.py:563
  159.0 10.2 %collective-permute-start.10 = (f32[128,128]{1,0:T(8,128)S(1)}, f32[128,128]{1,0:T(8,128)S(1)}, u32[]{:S(2)}, u32[]{:S(2)}) collective-permute-start(f32[128,128]{1,0:T(8,128)S(1)} %get-tuple-element.27.own_ref), channel_id=1, source_target_pairs={{0,384},{8,392},{16,400},{24,408},{32,416},{40,424},{48,432},{56,4... | collective-permute-start | bytes 196616 | tf_op jit(solution)/shard_map/ppermute | solution.py:567
